TPU v7x, 32 devices: a whole 2x2x4 slice. The times are simulated.
32 devices in a mesh: seq: 8 (over z, x), book: 4 (over y, core).
Axes of the slice: x: 2, y: 2, z: 4, core: 2. Of those that a mesh axis runs over, the one named last changes fastest.
Arguments:
- features: bfloat16 [4, 1024, 512], P('book', 'seq'), may hold values from -6 to 6
- lengths: int32 [4, 8], P('book'), may hold values from 1 to 256, 1024 in all within a row
- owner: int32 [4, 1024, 1], P('book', 'seq'), may hold values from 0 to 7; in each aligned block of 128 rows (0 to 127, 128 to 255, ..., all dimensions but the last counted through in order) at most 17 rows name the same one
- w_enc: bfloat16 [3, 512, 256], replicated, may hold values from -0.15625 to 0.15625
- w_in: bfloat16 [256, 2048], P(None, ('seq', 'book')), may hold values from -0.375 to 0.375
- gain: float32 [2048], replicated, may hold values from 0.1 to 1.9
- cotangent: bfloat16 [4, 1088, 2048], P('book', 'seq'), may hold values from -6 to 6
Outputs:
- grad_features: bfloat16 [4, 1024, 512], P('book', 'seq')
- grad_w_enc: float32 [3, 512, 256], P(None, 'book')
- grad_w_in: float32 [256, 2048], P(None, ('seq', 'book'))
- grad_gain: float32 [2048], replicated
Inputs may be any that keep to these rules, and one draw needn't show every extreme that they name: Of the 128 frames of one device's block no more than 17 have the same owner, and in some block exactly 17 do. The 8 lengths of a stream sum to 1024; the largest is 256.
All inputs are finite; a program needn't handle non-finite values.
Results may differ from a plain program's by a relative error of at most 0.0095.
Values may be sent and summed in bfloat16 or wider, within the bound.
No kernel may reach another device: no remote copies, remote signals or barrier semaphores. Data moves between devices by JAX's collectives and lax.ppermute only.
A program may use at most 64 MiB of HBM per device.

v0:
```python
import jax
import jax.numpy as jnp
from jax import lax
from jax.sharding import PartitionSpec as P


def shifted(block, axis, distance):
    devices = range(lax.axis_size(axis))
    route = [(i - distance, i) for i in devices if i - distance in devices]
    return lax.ppermute(block, axis, route)


def book_mask(position, book_lengths, offset):
    starts = jnp.cumsum(book_lengths) - book_lengths
    start_of = jnp.max(jnp.where(starts[None, :] <= position[:, None], starts[None, :], 0), axis=1)
    return position - offset >= start_of


def per_device(features, lengths, owner, w_enc, w_in, gain, cotangent):
    feature_rows = features[0]
    frames, channels = feature_rows.shape
    tap_count, _, latent_width = w_enc.shape
    seq_count = lax.axis_size("seq")
    book_count = lax.axis_size("book")
    capacity = max(2, frames // seq_count + 1)
    first_frame = lax.axis_index("seq") * frames
    position = first_frame + jnp.arange(frames + tap_count - 1, dtype=jnp.int32)
    tap_masks = [book_mask(position, lengths[0], offset) for offset in range(tap_count)]
    feats_wide = feature_rows.astype(jnp.float32)
    activated = jax.nn.elu(feats_wide).astype(jnp.bfloat16)
    left_edge = shifted(activated[frames - (tap_count - 1) :], "seq", 1)
    padded = jnp.concatenate([left_edge, activated], axis=0)
    tap_inputs = []
    for offset in range(tap_count):
        begin = tap_count - 1 - offset
        window = padded[begin : begin + frames]
        tap_inputs.append(
            jnp.where(tap_masks[offset][:frames, None], window, jnp.zeros_like(window))
        )
    stacked = jnp.concatenate(tap_inputs, axis=1)
    latent = jnp.dot(
        stacked,
        w_enc.reshape(tap_count * channels, latent_width),
        preferred_element_type=jnp.float32,
    ).astype(jnp.bfloat16)
    owner_rank = owner[0, :, 0]
    one_hot = (owner_rank[:, None] == jnp.arange(seq_count, dtype=jnp.int32)[None, :]).astype(
        jnp.int32
    )
    slot_rank = jnp.sum((jnp.cumsum(one_hot, axis=0) - one_hot) * one_hot, axis=1)
    slot_index = owner_rank * capacity + slot_rank
    placement = (
        slot_index[:, None] == jnp.arange(seq_count * capacity, dtype=jnp.int32)[None, :]
    ).astype(jnp.bfloat16)
    outgoing = lax.dot_general(
        placement, latent, (((0,), (0,)), ((), ())), preferred_element_type=jnp.float32
    ).astype(jnp.bfloat16)
    arrived = lax.all_to_all(
        outgoing.reshape(seq_count, capacity, latent_width),
        "seq",
        split_axis=0,
        concat_axis=0,
        tiled=True,
    )
    arrived = arrived.reshape(seq_count * capacity, latent_width)
    w_full = lax.all_gather(w_in, ("seq", "book"), axis=1, tiled=True)
    grad_out = cotangent[0].astype(jnp.float32)
    hidden = jnp.dot(arrived, w_full, preferred_element_type=jnp.float32)
    inv_rms = lax.rsqrt(jnp.mean(hidden * hidden, axis=1, keepdims=True) + 1e-05)
    normed = hidden * inv_rms
    gain_term = grad_out * gain[None, :]
    hidden_grad = (
        inv_rms * (gain_term - normed * jnp.mean(gain_term * normed, axis=1, keepdims=True))
    ).astype(jnp.bfloat16)
    latent_back = lax.dot_general(
        hidden_grad, w_full, (((1,), (1,)), ((), ())), preferred_element_type=jnp.float32
    ).astype(jnp.bfloat16)
    w_part = lax.dot_general(
        arrived, hidden_grad, (((0,), (0,)), ((), ())), preferred_element_type=jnp.float32
    )
    gain_part = jnp.sum(grad_out * normed, axis=0)
    returned = lax.all_to_all(
        latent_back.reshape(seq_count, capacity, latent_width),
        "seq",
        split_axis=0,
        concat_axis=0,
        tiled=True,
    )
    returned = returned.reshape(seq_count * capacity, latent_width)
    latent_grad = jnp.dot(placement, returned, preferred_element_type=jnp.float32).astype(
        jnp.bfloat16
    )
    right_edge = shifted(latent_grad[: tap_count - 1], "seq", -1)
    extended = jnp.concatenate([latent_grad, right_edge], axis=0)
    tap_grads = []
    for offset in range(tap_count):
        window = extended[offset : offset + frames]
        tap_grads.append(
            jnp.where(
                tap_masks[offset][offset : offset + frames, None], window, jnp.zeros_like(window)
            )
        )
    kernel_back = jnp.transpose(w_enc, (0, 2, 1)).reshape(tap_count * latent_width, channels)
    activ_grad = jnp.dot(
        jnp.concatenate(tap_grads, axis=1), kernel_back, preferred_element_type=jnp.float32
    )
    slope = jnp.where(feats_wide > 0, 1.0, jnp.exp(feats_wide))
    feature_grad = (slope * activ_grad).astype(jnp.bfloat16)
    kernel_part = lax.dot_general(
        stacked, latent_grad, (((0,), (0,)), ((), ())), preferred_element_type=jnp.float32
    )
    kernel_part = kernel_part.reshape(tap_count, channels, latent_width)
    kernel_total, gain_total = lax.psum((kernel_part, gain_part), ("seq", "book"))
    share_width = channels // book_count
    kernel_mine = lax.dynamic_slice_in_dim(
        kernel_total, lax.axis_index("book") * share_width, share_width, 1
    )
    columns = w_in.shape[1]
    split_grad = w_part.reshape(latent_width, seq_count, book_count * columns)
    split_grad = lax.psum_scatter(
        split_grad.astype(jnp.bfloat16), "book", scatter_dimension=2, tiled=True
    ).astype(jnp.float32)
    w_grad = lax.psum_scatter(split_grad, "seq", scatter_dimension=1, tiled=True).reshape(
        latent_width, columns
    )
    return (feature_grad[None], kernel_mine, w_grad, gain_total)


def solution(mesh):
    placed = (
        P("book", "seq", None),
        P("book", None),
        P("book", "seq", None),
        P(),
        P(None, ("seq", "book")),
        P(),
        P("book", "seq", None),
    )
    return jax.shard_map(
        per_device,
        mesh=mesh,
        in_specs=placed,
        out_specs=(P("book", "seq", None), P(None, "book", None), P(None, ("seq", "book")), P()),
        check_vma=False,
    )
```

profile of v0, /device:TPU:0, one launch (start us, length us, event | category | flops | bytes accessed | tf_op | source)
XLA Modules:
  0.0 305.6 jit_solution(13702209326619964794)
XLA Ops:
  7.2 0.0 copy-start.2
  7.2 0.0 all-gather.2.cloned.1.call-start
  7.2 1.1 fusion.12
  8.3 4.8 %collective-permute-start = (bf16[2,512]{1,0:T(2,128)(2,1)S(1)}, bf16[2,512]{1,0:T(2,128)(2,1)S(1)}, u32[]{:S(2)}, u32[]{:S(2)}) collective-permute-start(bf16[2,512]{1,0:T(2,128)(2,1)S(1)} %slice.45), channel_id=1, source_target_pairs={{0,4},{4,8},{8,12},{12,16},{16,20},{20,24},{24,28},{1,5},{5,9},{9,... | collective-permute-start | bytes 6152 | tf_op jit(solution)/shard_map/ppermute | solution.py:10
  13.2 0.0 all-gather.2.cloned.1.call-update
  13.2 0.0 reduce-scatter.3.cloned.1.call-start
  13.2 0.7 fusion.27
  14.0 0.8 reduce-window_clone.1
  14.8 0.2 reduce_window_sum.20
  15.0 0.7 subtract_bitcast_fusion
  15.7 0.1 select_reduce_fusion.1
  15.7 0.8 select_reduce_fusion
  16.6 0.1 fusion.33
  16.7 1.0 broadcast_select_fusion
  17.7 0.7 multiply_add_fusion
  18.4 0.0 collective-permute-done
  18.4 0.1 fusion.20
  18.5 0.0 copy-done.2
  18.5 0.4 convolution_convert_fusion.2
  19.0 11.9 %all_to_all.10 = bf16[8,17,256]{2,1,0:T(8,128)(2,1)S(1)} all-to-all(bf16[8,17,256]{2,1,0:T(8,128)(2,1)S(1)} %reshape.76), channel_id=1, replica_groups=mesh['seq'=8,'book'=4] {'seq'}, dimensions={0} | all-to-all | bytes 139264 | tf_op jit(solution)/shard_map/all_to_all | solution.py:58
  31.0 0.0 copy-start.1
  31.0 0.0 copy-start.4
  31.0 36.4 %all-gather.2.cloned.1.call-done = bf16[256,2048]{0,1:T(8,128)(2,1)} async-done(((bf16[256,64]{0,1:T(8,128)(2,1)}), bf16[256,2048]{0,1:T(8,128)(2,1)}) %all-gather.2.cloned.1.call-update) | async-done | bytes 1048592 | tf_op jit(solution)/shard_map/all_gather | solution.py:66
  67.4 1.8 multiply_reduce_fusion
  69.2 0.0 copy-done.1
  69.2 0.0 copy-done.4
  69.2 0.5 fusion.7
  69.7 0.3 fusion.6
  70.0 0.0 copy-start
  70.0 1.5 convolution_convert_fusion
  71.5 0.0 reduce-scatter.3.cloned.1.call-update
  71.6 0.0 all-reduce.2.cloned.1.call-start
  71.6 0.0 copy-done
  71.6 0.3 convolution_convert_fusion.1
  72.0 11.2 %all_to_all.11 = bf16[8,17,256]{2,1,0:T(8,128)(2,1)S(1)} all-to-all(bf16[8,17,256]{2,1,0:T(8,128)(2,1)S(1)} %reshape.78), channel_id=1, replica_groups=mesh['seq'=8,'book'=4] {'seq'}, dimensions={0} | all-to-all | bytes 139264 | tf_op jit(solution)/shard_map/all_to_all | solution.py:82
  83.2 0.2 convolution_convert_fusion.4
  83.5 1.5 fusion.18
  85.0 0.0 all-reduce.2.cloned.1.call-update
  85.0 0.0 reduce-scatter.5.cloned.1.call-start
  85.1 10.5 %reduce-scatter.3.cloned.1.call-done = bf16[256,8,64]{0,2,1:T(8,128)(2,1)} async-done(((bf16[256,8,256]{0,2,1:T(8,128)(2,1)}), bf16[256,8,64]{0,2,1:T(8,128)(2,1)}) %reduce-scatter.3.cloned.1.call-update) | async-done | bytes 262160 | tf_op jit(solution)/shard_map/reduce_scatter | solution.py:120
  95.6 1.8 convert_element_type.56
  97.4 0.0 copy-start.3
  97.4 0.0 reduce-scatter.5.cloned.1.call-update
  97.4 0.3 copy.14
  97.7 1.3 collective-permute-start.1
  99.0 41.9 %psum.15 = f32[2048]{0:T(1024)} all-reduce(f32[2048]{0:T(1024)S(1)} %get-tuple-element.4), channel_id=1, replica_groups=mesh['seq'=8,'book'=4] {'seq','book'}, use_global_device_ids=true, to_apply=%region_10.11 | all-reduce | flops 2048 | bytes 16384 | tf_op jit(solution)/shard_map/psum | solution.py:113
  140.9 0.0 collective-permute-done.1
  140.9 0.1 fusion.23
  141.0 0.0 copy-done.3
  141.0 0.9 fusion.3
  142.0 92.2 %all-reduce.2.cloned.1.call-done = f32[3,512,256]{2,1,0:T(8,128)} async-done(((f32[3,512,256]{2,1,0:T(8,128)}), f32[3,512,256]{2,1,0:T(8,128)}) %all-reduce.2.cloned.1.call-update) | async-done | bytes 1572880 | tf_op jit(solution)/shard_map/psum | solution.py:113
  234.1 1.8 constant_dynamic-slice_fusion
  235.9 63.1 %reduce-scatter.5.cloned.1.call-done = f32[256,1,64]{0,2,1:T(8,128)} async-done(((f32[256,8,64]{0,2,1:T(8,128)}), f32[256,1,64]{0,2,1:T(8,128)}) %reduce-scatter.5.cloned.1.call-update) | async-done | bytes 65552 | tf_op jit(solution)/shard_map/reduce_scatter | solution.py:123
  (11 shorter events, 0.2 us)
Async XLA Ops:
  7.2 11.3 %copy-start.2 = (bf16[3,512,256]{2,1,0:T(8,128)(2,1)S(1)}, bf16[3,512,256]{2,1,0:T(8,128)(2,1)}, u32[]{:S(2)}) copy-start(bf16[3,512,256]{2,1,0:T(8,128)(2,1)} %param.10) | copy-start | bytes 2359300
  7.2 60.2 %all-gather.2.cloned.1.call-start = ((), (), s32[]{:S(2)}) async-start(), calls=%async_computation.4 | async-start | bytes 1081344 | tf_op jit(solution)/shard_map/all_gather | solution.py:66
  8.3 10.1 %collective-permute-start = (bf16[2,512]{1,0:T(2,128)(2,1)S(1)}, bf16[2,512]{1,0:T(2,128)(2,1)S(1)}, u32[]{:S(2)}, u32[]{:S(2)}) collective-permute-start(bf16[2,512]{1,0:T(2,128)(2,1)S(1)} %slice.45), channel_id=1, source_target_pairs={{0,4},{4,8},{8,12},{12,16},{16,20},{20,24},{24,28},{1,5},{5,9},{9,... | collective-permute-start | bytes 6152 | tf_op jit(solution)/shard_map/ppermute | solution.py:10
  13.2 82.4 %reduce-scatter.3.cloned.1.call-start = ((), (), s32[]{:S(2)}) async-start(), calls=%async_computation.6 | async-start | bytes 1310720 | tf_op jit(solution)/shard_map/reduce_scatter | solution.py:120
  31.0 38.3 %copy-start.1 = (bf16[1,136,2048]{2,1,0:T(8,128)(2,1)S(1)}, bf16[1,136,2048]{2,1,0:T(8,128)(2,1)}, u32[]{:S(2)}) copy-start(bf16[1,136,2048]{2,1,0:T(8,128)(2,1)} %param.13) | copy-start | bytes 1671172
  31.0 38.3 %copy-start.4 = (f32[2048]{0:T(1024)S(1)}, f32[2048]{0:T(1024)}, u32[]{:S(2)}) copy-start(f32[2048]{0:T(1024)} %param.12) | copy-start | bytes 24580
  70.0 1.6 copy-start
  71.6 162.6 %all-reduce.2.cloned.1.call-start = ((), (), s32[]{:S(2)}) async-start(), calls=%async_computation.5 | async-start | bytes 3145728 | tf_op jit(solution)/shard_map/psum | solution.py:113
  85.0 214.0 %reduce-scatter.5.cloned.1.call-start = ((), (), s32[]{:S(2)}) async-start(), calls=%async_computation.7 | async-start | bytes 589824 | tf_op jit(solution)/shard_map/reduce_scatter | solution.py:123
  97.4 43.6 %copy-start.3 = (bf16[1,128,512]{2,1,0:T(8,128)(2,1)S(1)}, bf16[1,128,512]{2,1,0:T(8,128)(2,1)}, u32[]{:S(2)}) copy-start(bf16[1,128,512]{2,1,0:T(8,128)(2,1)} %param.7) | copy-start | bytes 393220
  97.7 43.2 %collective-permute-start.1 = (bf16[2,256]{1,0:T(2,128)(2,1)S(1)}, bf16[2,256]{1,0:T(2,128)(2,1)S(1)}, u32[]{:S(2)}, u32[]{:S(2)}) collective-permute-start(bf16[2,256]{1,0:T(2,128)(2,1)S(1)} %slice.48), channel_id=1, source_target_pairs={{4,0},{8,4},{12,8},{16,12},{20,16},{24,20},{28,24},{5,1},{9,5},{13... | collective-permute-start | bytes 3080 | tf_op jit(solution)/shard_map/ppermute | solution.py:10
Sparse Core Ops, SparseCore 0:
  13.3 54.0 all-gather.1
  71.7 23.8 reduce-scatter.2
  101.7 132.3 all-reduce.1
  238.3 60.7 reduce-scatter.4
where the time goes:
time: 306 us
  waiting for transfers between devices  202 us (66%)
  blocking collectives  65 us (21%)
  between operations  14 us (5%)
  other arithmetic  8.87 us (3%)
  matrix products  6.8 us (2%)
  starting transfers between devices  6.3 us (2%)
    psum x1, waiting for transfers between devices, per_device(): lax.psum((kernel_part, gain_part), ('seq', 'book'))  92.2 us
    reduce_scatter x1, waiting for transfers between devices, per_device(): lax.psum_scatter(split_grad, 'seq', scatter_dimension=1, tiled=True)  63.1 us
    psum x1, blocking collectives, per_device(): lax.psum((kernel_part, gain_part), ('seq', 'book'))  41.9 us
    all_gather x1, waiting for transfers between devices, per_device(): w_full = lax.all_gather(w_in, ('seq', 'book'), axis=1, tiled=True)  36.4 us
    all_to_all x1, blocking collectives, per_device(): lax.all_to_all(outgoing.reshape(seq_count, capacity, latent_width), 'seq'...  11.9 us
    all_to_all x1, blocking collectives, per_device(): lax.all_to_all(latent_back.reshape(seq_count, capacity, latent_width), 's...  11.2 us
    reduce_scatter x1, waiting for transfers between devices, per_device(): lax.psum_scatter(split_grad.astype(jnp.bfloat16), 'book', scatter_dimensi...  10.5 us
    ppermute x2, starting transfers between devices, shifted(): return lax.ppermute(block, axis, route)  6.13 us
  transfers between devices with their start and end apart: 6, of which 4 were waited for; matrix products, arithmetic and copies ran while one was open for 4% of the time, Pallas kernels for 0%

commit v1 on v0

--- a/solution.py
+++ b/solution.py
@@ -1,7 +1,16 @@
+import functools
+
 import jax
 import jax.numpy as jnp
 from jax import lax
+from jax.experimental import pallas as pl
+from jax.experimental.pallas import tpu as pltpu
 from jax.sharding import PartitionSpec as P
+
+F32 = jnp.float32
+BF16 = jnp.bfloat16
+VMEM = pl.BlockSpec(memory_space=pltpu.VMEM)
+SMEM = pl.BlockSpec(memory_space=pltpu.SMEM)
 
 
 def shifted(block, axis, distance):
@@ -16,7 +25,7 @@
     return position - offset >= start_of
 
 
-def per_device(features, lengths, owner, w_enc, w_in, gain, cotangent):
+def per_device_gather(features, lengths, owner, w_enc, w_in, gain, cotangent):
     feature_rows = features[0]
     frames, channels = feature_rows.shape
     tap_count, _, latent_width = w_enc.shape
@@ -126,6 +135,442 @@
     return (feature_grad[None], kernel_mine, w_grad, gain_total)
 
 
+def round_up(value, unit):
+    return -(-value // unit) * unit
+
+
+def swap(block, axis, mask):
+    return lax.ppermute(block, axis, [(i, i ^ mask) for i in range(lax.axis_size(axis))])
+
+
+def iota(shape, dim):
+    return lax.broadcasted_iota(jnp.int32, shape, dim)
+
+
+def elu_wide(x):
+    low = jnp.minimum(x, 0.0)
+    series = 1.0 + low / 6.0
+    for order in (5.0, 4.0, 3.0, 2.0):
+        series = 1.0 + (low / order) * series
+    below = jnp.where(low > -0.25, low * series, jnp.exp(low) - 1.0)
+    return jnp.where(x > 0, x, below)
+
+
+def start_below(position, lengths_ref):
+    best = jnp.zeros_like(position)
+    start = jnp.int32(0)
+    for book in range(lengths_ref.shape[0]):
+        best = jnp.where(start <= position, jnp.maximum(best, start), best)
+        start = start + lengths_ref[book]
+    return best
+
+
+def ranks_of(owner_rows, seq_count):
+    blocks, frames = owner_rows.shape
+    parts = [
+        (iota((seq_count, frames), 0) == owner_rows[b : b + 1].astype(jnp.int32)).astype(F32)
+        for b in range(blocks)
+    ]
+    named = jnp.concatenate(parts, axis=0)
+    before = (iota((frames, frames), 0) < iota((frames, frames), 1)).astype(BF16)
+    counted = jnp.dot(named.astype(BF16), before, preferred_element_type=F32) * named
+    return jnp.concatenate(
+        [
+            jnp.sum(counted[b * seq_count : (b + 1) * seq_count], axis=0, keepdims=True)
+            for b in range(blocks)
+        ],
+        axis=0,
+    )
+
+
+def encode_kernel(piece, capacity, lengths_ref, feat_ref, edge_ref, owner_ref, w_ref, *rest):
+    out_refs, padded = rest[:-1], rest[-1]
+    frames, channels = feat_ref.shape
+    taps = w_ref.shape[0]
+    seq_count = 2 * len(out_refs)
+    me = lax.axis_index("seq")
+    edge = elu_wide(edge_ref[...].astype(F32)).astype(BF16).astype(F32)
+    padded[0:8, :] = edge[edge.shape[0] - 8 :, :]
+    padded[8:, :] = elu_wide(feat_ref[...].astype(F32)).astype(BF16).astype(F32)
+    position = me * frames + iota((frames, 1), 0)
+    start_of = start_below(position, lengths_ref)
+    total = jnp.zeros((frames, w_ref.shape[2]), F32)
+    for tap in range(taps):
+        window = padded[8 - tap : 8 - tap + frames, :]
+        window = jnp.where(position - tap >= start_of, window, 0.0).astype(BF16)
+        total = total + jnp.dot(window, w_ref[tap], preferred_element_type=F32)
+    latent = total.astype(BF16)
+    owner = owner_ref[...]
+    rank = ranks_of(owner, seq_count).astype(jnp.int32)
+    row = jnp.bitwise_xor(owner, me) * piece + rank
+    placed = (iota((seq_count * piece, frames), 0) == row).astype(F32).astype(BF16)
+    outgoing = jnp.dot(placed, latent, preferred_element_type=F32)
+    named = owner.astype(F32)
+    if outgoing.shape[1] > frames:
+        named = jnp.concatenate([named, jnp.zeros((1, outgoing.shape[1] - frames), F32)], axis=1)
+    last = iota((seq_count * piece, 1), 0) % piece == piece - 1
+    outgoing = jnp.where(last, named, outgoing).astype(BF16)
+    for far, out_ref in enumerate(out_refs):
+        out_ref[...] = outgoing[2 * far * piece : 2 * (far + 1) * piece]
+
+
+def middle_kernel(piece, capacity, frames, count, *refs):
+    far_count = count // 2
+    latents = refs[:far_count]
+    near = refs[far_count]
+    w_refs = refs[far_count + 1 : far_count + 9]
+    gain_ref, cot_ref, back_ref, hg_ref, arrived_ref, owners_ref = refs[far_count + 9 : far_count + 15]
+    gathered, w_full, hidden, back = refs[far_count + 15 :]
+    slots, width = cot_ref.shape
+    rows = back_ref.shape[0]
+    latent_width = back_ref.shape[1]
+    seq, book = lax.axis_index("seq"), lax.axis_index("book")
+    for far in range(far_count):
+        gathered[2 * far * piece : (2 * far + 1) * piece, :] = latents[far][0:piece, :]
+        gathered[(2 * far + 1) * piece : (2 * far + 2) * piece, :] = near[
+            far * piece : (far + 1) * piece, :
+        ]
+    for rel in range(count):
+        line = gathered[rel * piece : (rel + 1) * piece, 0:frames].astype(F32)
+        owners_ref[pl.ds(jnp.bitwise_xor(seq, rel), 1), :] = line[piece - 1 : piece, :]
+    columns = w_refs[0].shape[1]
+    for index, w_ref in enumerate(w_refs):
+        near_seq, near_y, near_core = index & 1, (index >> 1) & 1, index >> 2
+        for far in range(far_count):
+            at = jnp.bitwise_xor(seq, 2 * far + near_seq) * 4 + jnp.bitwise_xor(
+                book, near_y * 2 + near_core
+            )
+            w_full[pl.ds(pl.multiple_of(at * columns, columns), columns), :] = w_ref[far]
+    slot = iota((rows, 1), 0)
+    source = jnp.zeros_like(slot)
+    for block in range(1, count):
+        source = source + (slot >= block * capacity).astype(jnp.int32)
+    wanted = jnp.bitwise_xor(source, seq) * piece + slot - source * capacity
+    wanted = jnp.where(slot < slots, wanted, -1)
+    picked = (iota((rows, count * piece), 1) == wanted).astype(F32).astype(BF16)
+    arrived = jnp.dot(picked, gathered[...], preferred_element_type=F32).astype(BF16)
+    arrived_ref[...] = arrived
+    step = latent_width
+    squares = jnp.zeros((slots, step), F32)
+    crossed = jnp.zeros((slots, step), F32)
+    for at in range(0, width, step):
+        part = lax.dot_general(
+            arrived, w_full[at : at + step, :], (((1,), (1,)), ((), ())), preferred_element_type=F32
+        )[:slots]
+        hidden[:, at : at + step] = part
+        squares = squares + part * part
+        scaled = cot_ref[:, at : at + step].astype(F32) * gain_ref[:, at : at + step]
+        crossed = crossed + part * scaled
+    inv = lax.rsqrt(jnp.sum(squares, axis=1, keepdims=True) / width + 1e-05)
+    pull = inv * inv * (jnp.sum(crossed, axis=1, keepdims=True) / width)
+    total = jnp.zeros((rows, latent_width), F32)
+    for at in range(0, width, step):
+        part = hidden[:, at : at + step]
+        grad_out = cot_ref[:, at : at + step].astype(F32)
+        scaled = grad_out * gain_ref[:, at : at + step]
+        grad = inv * (scaled - part * pull)
+        grad = jnp.concatenate([grad, jnp.zeros((rows - slots, step), F32)], axis=0).astype(BF16)
+        hg_ref[:, at : at + step] = grad
+        total = total + jnp.dot(grad, w_full[at : at + step, :], preferred_element_type=F32)
+        line = slots + at // step
+        back[line : line + 1, :] = jnp.sum(grad_out * (part * inv), axis=0, keepdims=True)
+    back[0:slots, :] = total[:slots]
+    for line in range(slots + width // step, rows):
+        back[line : line + 1, :] = jnp.zeros((1, latent_width), F32)
+    back_ref[...] = back[...].astype(BF16)
+
+
+def chip_order(count):
+    return [(y, near, far) for y in (0, 1) for near in (0, 1) for far in range(count // 2)]
+
+
+def projection_kernel(count, hg_ref, arrived_ref, send_ref, keep_ref):
+    seq, book = lax.axis_index("seq"), lax.axis_index("book")
+    core = jnp.bitwise_and(book, 1)
+    chip = seq * 2 + (book >> 1)
+    half = send_ref.shape[1]
+    arrived = arrived_ref[...]
+    for place, (y, near, far) in enumerate(chip_order(count)):
+        at = jnp.bitwise_xor(chip, (2 * far + near) * 2 + y)
+        grad = hg_ref[:, pl.ds(pl.multiple_of(at * 2 * half, 2 * half), 2 * half)]
+        part = lax.dot_general(
+            grad, arrived, (((0,), (0,)), ((), ())), preferred_element_type=F32
+        )
+        low, high = part[:half], part[half:]
+        send_ref[place] = jnp.where(core == 0, high, low).astype(BF16)
+        keep_ref[place] = jnp.where(core == 0, low, high).astype(BF16)
+
+
+def prepare_kernel(capacity, rows, orders, lengths_ref, owners_ref, *refs):
+    f_refs = refs[: len(orders)]
+    turned_ref, facts_ref = refs[len(orders) :]
+    count, frames = owners_ref.shape
+    me = lax.axis_index("seq")
+    for f_ref, order in zip(f_refs, orders):
+        for index, rel in enumerate(order):
+            act = elu_wide(f_ref[index * frames : (index + 1) * frames, :].astype(F32))
+            at = jnp.bitwise_xor(me, rel) * frames
+            turned_ref[:, pl.ds(pl.multiple_of(at, frames), frames)] = act.T.astype(BF16)
+    owners = owners_ref[...]
+    ranks = ranks_of(owners, count)
+    eye = (iota((frames, frames), 0) == iota((frames, frames), 1)).astype(BF16)
+    dims = (((1,), (1,)), ((), ()))
+    owner_cols = lax.dot_general(eye, owners.astype(BF16), dims, preferred_element_type=F32)
+    rank_cols = lax.dot_general(eye, ranks.astype(BF16), dims, preferred_element_type=F32)
+    lane = iota((frames, facts_ref.shape[1]), 1)
+    for block in range(count):
+        owner = owner_cols[:, block : block + 1].astype(jnp.int32)
+        rank = rank_cols[:, block : block + 1].astype(jnp.int32)
+        slot = jnp.bitwise_xor(owner, me) * rows + block * capacity + rank
+        position = block * frames + iota((frames, 1), 0)
+        facts = slot
+        for tap in range(1, facts_ref.shape[1]):
+            later = position + tap
+            valid = (later < count * frames) & (position >= start_below(later, lengths_ref))
+            facts = jnp.where(lane == tap, valid.astype(jnp.int32), facts)
+        facts_ref[block * frames : (block + 1) * frames, :] = facts
+
+
+def spread_kernel(count, frames, taps, *refs):
+    backs = refs[:count]
+    facts_ref, turned_ref, send_ref, windows_ref, gain_ref, gathered, wide = refs[count:]
+    rows, latent_width = backs[0].shape
+    share = turned_ref.shape[0] // 4
+    gain_rows = gain_ref.shape[0]
+    book = lax.axis_index("book")
+    gain = jnp.zeros((gain_rows, latent_width), F32)
+    for rel, back_ref in enumerate(backs):
+        gathered[rel * rows : (rel + 1) * rows, :] = back_ref[...]
+        gain = gain + back_ref[...].astype(F32)[rows - gain_rows :]
+    gain_ref[...] = gain
+    for block in range(count):
+        here = slice(block * frames, (block + 1) * frames)
+        placed = iota((frames, count * rows), 1) == facts_ref[here, 0:1]
+        wide[here, :] = jnp.dot(
+            placed.astype(F32).astype(BF16), gathered[...], preferred_element_type=F32
+        )
+    wide[count * frames :, :] = jnp.zeros((8, latent_width), F32)
+    for block in range(count):
+        here = slice(block * frames, (block + 1) * frames)
+        windows_ref[here, 0:latent_width] = wide[here, :].astype(BF16)
+        for tap in range(1, taps):
+            later = wide[block * frames + tap : (block + 1) * frames + tap, :]
+            later = jnp.where(facts_ref[here, tap : tap + 1] > 0, later, 0.0)
+            windows_ref[here, tap * latent_width : (tap + 1) * latent_width] = later.astype(BF16)
+    part = kernel_part(turned_ref, windows_ref, book, share, 1)
+    for y in (0, 1):
+        for tap in range(taps):
+            at = (y * taps + tap) * share
+            send_ref[at : at + share, :] = part[
+                y * share : (y + 1) * share, tap * latent_width : (tap + 1) * latent_width
+            ].astype(BF16)
+    high = gain.astype(BF16)
+    at = 2 * taps * share
+    send_ref[at : at + 2 * gain_rows, :] = jnp.concatenate(
+        [high.astype(F32), gain - high.astype(F32)], axis=0
+    ).astype(BF16)
+
+
+def kernel_part(turned_ref, windows_ref, book, share, core):
+    blocks = []
+    for y in (0, 1):
+        at = jnp.bitwise_xor(book, 2 * y + core) * share
+        blocks.append(turned_ref[pl.ds(pl.multiple_of(at, share), share), :])
+    return jnp.dot(
+        jnp.concatenate(blocks, axis=0), windows_ref[...], preferred_element_type=F32
+    )
+
+
+def own_part_kernel(taps, turned_ref, windows_ref, out_ref):
+    share, latent_width = turned_ref.shape[0] // 4, out_ref.shape[1]
+    part = kernel_part(turned_ref, windows_ref, lax.axis_index("book"), share, 0)
+    for y in (0, 1):
+        for tap in range(taps):
+            at = (y * taps + tap) * share
+            out_ref[at : at + share, :] = part[
+                y * share : (y + 1) * share, tap * latent_width : (tap + 1) * latent_width
+            ]
+
+
+def fold_kernel(kept_ref, got_ref, gain_ref, send_ref, mine_ref, gain_out_ref):
+    half, gain_rows = mine_ref.shape[0], gain_ref.shape[0]
+    mine_ref[...] = kept_ref[0:half, :] + got_ref[0:half, :].astype(F32)
+    send_ref[0:half, :] = (
+        kept_ref[half : 2 * half, :] + got_ref[half : 2 * half, :].astype(F32)
+    ).astype(BF16)
+    pair = got_ref[2 * half : 2 * half + 2 * gain_rows, :].astype(F32)
+    gain = gain_ref[...] + (pair[:gain_rows] + pair[gain_rows:])
+    gain_out_ref[...] = gain
+    high = gain.astype(BF16).astype(F32)
+    send_ref[half : half + 2 * gain_rows, :] = jnp.concatenate(
+        [high, gain - high], axis=0
+    ).astype(BF16)
+
+
+def feature_kernel(feat_ref, windows_ref, w_ref, out_ref):
+    frames = feat_ref.shape[0]
+    taps, _, latent_width = w_ref.shape
+    at = pl.multiple_of(lax.axis_index("seq") * frames, frames)
+    total = jnp.zeros(feat_ref.shape, F32)
+    for tap in range(taps):
+        window = windows_ref[
+            pl.ds(at, frames), tap * latent_width : (tap + 1) * latent_width
+        ]
+        total = total + lax.dot_general(
+            window, w_ref[tap], (((1,), (1,)), ((), ())), preferred_element_type=F32
+        )
+    feats = feat_ref[...].astype(F32)
+    slope = jnp.where(feats > 0, 1.0, jnp.exp(jnp.minimum(feats, 0.0)))
+    out_ref[...] = (slope * total).astype(BF16)
+
+
+def call(kernel, outs, operands, scratch=(), smem=0, flops=0):
+    moved = sum(x.size * x.dtype.itemsize for x in (*outs, *operands))
+    return pl.pallas_call(
+        kernel,
+        out_shape=outs,
+        in_specs=[SMEM] * smem + [VMEM] * (len(operands) - smem),
+        out_specs=jax.tree.map(lambda _: VMEM, outs),
+        scratch_shapes=list(scratch),
+        compiler_params=pltpu.CompilerParams(vmem_limit_bytes=24 * 2**20),
+        cost_estimate=pl.CostEstimate(flops=flops, bytes_accessed=moved, transcendentals=0),
+    )(*operands)
+
+
+def shape(dims, dtype=BF16):
+    return jax.ShapeDtypeStruct(dims, dtype)
+
+
+def per_device(features, lengths, owner, w_enc, w_in, gain, cotangent):
+    feats = features[0]
+    cot = cotangent[0]
+    book_lengths = lengths[0]
+    frames, channels = feats.shape
+    taps, _, latent_width = w_enc.shape
+    slots, width = cot.shape
+    count = lax.axis_size("seq")
+    far_count = count // 2
+    fars = range(1, far_count)
+    capacity = max(2, frames // count + 1)
+    piece = round_up(capacity + 1, 16)
+    gain_rows = width // latent_width
+    rows = round_up(slots + gain_rows, 16)
+    share = channels // 4
+
+    edge = shifted(feats[frames - 16 :], "seq", 1)
+    w_own = w_in.T
+    w_far = [w_own] + [swap(w_own, "seq", 2 * far) for far in fars]
+    w_line = jnp.stack(w_far)
+    w_near = swap(w_line, "seq", 1)
+    w_side = swap(w_line, "book", 2)
+    w_diag = swap(w_line, ("seq", "book"), 4 + 2)
+    w_chips = [w_line, w_near, w_side, w_diag]
+    w_pieces = w_chips + [swap(block, "book", 1) for block in w_chips]
+
+    sent = call(
+        functools.partial(encode_kernel, piece, capacity),
+        [shape((2 * piece, latent_width))] * far_count,
+        (book_lengths, feats, edge, owner[0].T, w_enc),
+        scratch=[pltpu.VMEM((8 + frames, channels), F32)],
+        smem=1,
+    )
+    landed = [sent[0]] + [swap(sent[far], "seq", 2 * far) for far in fars]
+    near = swap(jnp.concatenate([block[piece:] for block in landed]), "seq", 1)
+
+    back, hidden_grad, arrived, owners = call(
+        functools.partial(middle_kernel, piece, capacity, frames, count),
+        [
+            shape((rows, latent_width)),
+            shape((rows, width)),
+            shape((rows, latent_width)),
+            shape((count, frames), F32),
+        ],
+        (*landed, near, *w_pieces, gain[None], cot),
+        scratch=[
+            pltpu.VMEM((count * piece, latent_width), BF16),
+            pltpu.VMEM((width, latent_width), BF16),
+            pltpu.VMEM((slots, width), F32),
+            pltpu.VMEM((rows, latent_width), F32),
+        ],
+    )
+    backs = [back] + [swap(back, "seq", rel) for rel in range(1, count)]
+
+    gathered, orders, mask, held, order = [feats], [[0]], far_count, feats, [0]
+    while mask:
+        got = swap(held, "seq", mask)
+        gathered.append(got)
+        orders.append([rel ^ mask for rel in order])
+        order = order + orders[-1]
+        mask //= 2
+        if mask:
+            held = jnp.concatenate([held, got])
+
+    w_send, w_keep = call(
+        functools.partial(projection_kernel, count),
+        [shape((2 * count, w_in.shape[1], latent_width))] * 2,
+        (hidden_grad, arrived),
+    )
+    w_sum = w_keep.astype(F32) + swap(w_send, "book", 1).astype(F32)
+    w_sum = w_sum[:count] + swap(w_sum[count:].astype(BF16), "book", 2).astype(F32)
+    w_sum = w_sum[:far_count] + swap(w_sum[far_count:].astype(BF16), "seq", 1).astype(F32)
+    w_total = w_sum[0]
+    for far in fars:
+        w_total = w_total + swap(w_sum[far].astype(BF16), "seq", 2 * far).astype(F32)
+
+    turned, facts = call(
+        functools.partial(prepare_kernel, capacity, rows, orders),
+        [shape((channels, count * frames)), shape((count * frames, taps), jnp.int32)],
+        (book_lengths, owners, *gathered),
+        smem=1,
+    )
+    message = 2 * taps * share + 2 * gain_rows
+    k_send, windows, gain_seq = call(
+        functools.partial(spread_kernel, count, frames, taps),
+        [
+            shape((message, latent_width)),
+            shape((count * frames, taps * latent_width)),
+            shape((gain_rows, latent_width), F32),
+        ],
+        (*backs, facts, turned),
+        scratch=[
+            pltpu.VMEM((count * rows, latent_width), BF16),
+            pltpu.VMEM((count * frames + 8, latent_width), F32),
+        ],
+    )
+    k_got = swap(k_send, "book", 1)
+    (k_kept,) = call(
+        functools.partial(own_part_kernel, taps),
+        [shape((2 * taps * share, latent_width), F32)],
+        (turned, windows),
+    )
+    y_send, k_mine, gain_pair = call(
+        fold_kernel,
+        [
+            shape((taps * share + 2 * gain_rows, latent_width)),
+            shape((taps * share, latent_width), F32),
+            shape((gain_rows, latent_width), F32),
+        ],
+        (k_kept, k_got, gain_seq),
+    )
+    y_got = swap(y_send, "book", 2)
+    (feature_grad,) = call(feature_kernel, [shape(feats.shape)], (feats, windows, w_enc))
+    y_wide = y_got.astype(F32)
+    kernel_mine = k_mine + y_wide[: taps * share]
+    tail = y_wide[taps * share :]
+    gain_total = (gain_pair + (tail[:gain_rows] + tail[gain_rows:])).reshape(width)
+    return (
+        feature_grad[None],
+        kernel_mine.reshape(taps, share, latent_width),
+        w_total.T,
+        gain_total,
+    )
+
+
+def fits(mesh):
+    count = mesh.shape["seq"]
+    return mesh.shape["book"] == 4 and count in (2, 4, 8)
+
+
 def solution(mesh):
     placed = (
         P("book", "seq", None),
@@ -137,7 +582,7 @@
         P("book", "seq", None),
     )
     return jax.shard_map(
-        per_device,
+        per_device if fits(mesh) else per_device_gather,
         mesh=mesh,
         in_specs=placed,
         out_specs=(P("book", "seq", None), P(None, "book", None), P(None, ("seq", "book")), P()),

time: 306 us -> 102 us (0.33)
  waiting for transfers between devices: 202 us -> 42.9 us
  blocking collectives: 65 us -> 0 us
  starting transfers between devices: 6.3 us -> 39.1 us
  between operations: 14 us -> 0.93 us
  Pallas kernels: 0 us -> 9.9 us
  matrix products: 6.8 us -> 0 us
  other arithmetic: 8.87 us -> 2.56 us
  local copies, waits for them, and re-layouts: 2.35 us -> 5.99 us
    psum x1 -> x0, waiting for transfers between devices: 92.2 us -> none  [per_device(): lax.psum((kernel_part, gain_part), ('seq', 'book'))]
    reduce_scatter x2 -> x0, waiting for transfers between devices: 73.7 us -> none  [the longest x1 63.1 us: per_device(): lax.psum_scatter(split_grad, 'seq', scatter_dimension=1, tiled=True)]
    psum x1 -> x0, blocking collectives: 41.9 us -> none  [per_device(): lax.psum((kernel_part, gain_part), ('seq', 'book'))]
    ppermute x0 -> x32, waiting for transfers between devices: none -> 41.4 us  [swap(): lax.ppermute(block, axis, [(i, i ^ mask) for i in range(lax.axis_size(axi...]
    all_gather x1 -> x0, waiting for transfers between devices: 36.4 us -> none  [per_device(): w_full = lax.all_gather(w_in, ('seq', 'book'), axis=1, tiled=True)]
    ppermute x0 -> x32, starting transfers between devices: none -> 35.7 us  [swap(): lax.ppermute(block, axis, [(i, i ^ mask) for i in range(lax.axis_size(axi...]
    all_to_all x2 -> x0, blocking collectives: 23.1 us -> none  [the longest x1 11.9 us: per_device(): lax.all_to_all(outgoing.reshape(seq_count, capacity, latent_width), 'seq'...]
    pallas_call x0 -> x8, Pallas kernels: none -> 9.9 us  [call(): pl.pallas_call(kernel, out_shape=outs, in_specs=[SMEM] * smem + [VMEM] *...]
  transfers between devices with their start and end apart: 6 -> 33, of which waited for: 4 -> 16; matrix products, arithmetic and copies ran while one was open for 4% -> 2% of each run, Pallas kernels for 0% -> 8%
where the time goes in v1:
time: 102 us; the launch traced here: 101 us
  waiting for transfers between devices  42.9 us (42%)
  starting transfers between devices  39.1 us (38%)
  Pallas kernels  9.9 us (10%)
  local copies, waits for them, and re-layouts  5.99 us (6%)
  other arithmetic  2.56 us (3%)
    ppermute x32, waiting for transfers between devices, swap(): lax.ppermute(block, axis, [(i, i ^ mask) for i in range(lax.axis_size(axi...  41.4 us
    ppermute x32, starting transfers between devices, swap(): lax.ppermute(block, axis, [(i, i ^ mask) for i in range(lax.axis_size(axi...  35.7 us
    pallas_call x8, Pallas kernels, call(): pl.pallas_call(kernel, out_shape=outs, in_specs=[SMEM] * smem + [VMEM] *...  9.9 us
    unnamed x19, local copies, waits for them, and re-layouts  5.21 us
    ppermute x1, starting transfers between devices, shifted(): return lax.ppermute(block, axis, route)  3.38 us
  transfers between devices with their start and end apart: 33, of which 16 were waited for; matrix products, arithmetic and copies ran while one was open for 2% of the time, Pallas kernels for 8%

profile of v1, /device:TPU:0, one launch (start us, length us, event | category | flops | bytes accessed | tf_op | source)
XLA Modules:
  0.0 101.3 jit_solution(11363116763231143651)
XLA Ops:
  0.6 4.1 %collective-permute-start.6 = (bf16[64,256]{1,0:T(8,128)(2,1)}, bf16[64,256]{1,0:T(8,128)(2,1)S(1)}, u32[]{:S(2)}, u32[]{:S(2)}) collective-permute-start(bf16[64,256]{1,0:T(8,128)(2,1)} %bitcast.49), channel_id=1, source_target_pairs={{0,16},{4,20},{8,24},{12,28},{16,0},{20,4},{24,8},{28,12},{1,17},{... | collective-permute-start | bytes 98312 | tf_op jit(solution)/shard_map/ppermute | solution.py:143
  4.7 1.6 %collective-permute-start.5 = (bf16[64,256]{1,0:T(8,128)(2,1)}, bf16[64,256]{1,0:T(8,128)(2,1)S(1)}, u32[]{:S(2)}, u32[]{:S(2)}) collective-permute-start(bf16[64,256]{1,0:T(8,128)(2,1)} %bitcast.50), channel_id=1, source_target_pairs={{0,8},{4,12},{8,0},{12,4},{16,24},{20,28},{24,16},{28,20},{1,9},{5... | collective-permute-start | bytes 98312 | tf_op jit(solution)/shard_map/ppermute | solution.py:143
  6.3 1.0 collective-permute-done.6
  7.3 1.6 %collective-permute-done.5 = bf16[64,256]{1,0:T(8,128)(2,1)S(1)} collective-permute-done((bf16[64,256]{1,0:T(8,128)(2,1)}, bf16[64,256]{1,0:T(8,128)(2,1)S(1)}, u32[]{:S(2)}, u32[]{:S(2)}) %collective-permute-start.5) | collective-permute-done | bytes 32800 | tf_op jit(solution)/shard_map/ppermute | solution.py:143
  8.9 3.4 %collective-permute-done.7 = bf16[64,256]{1,0:T(8,128)(2,1)S(1)} collective-permute-done((bf16[64,256]{1,0:T(8,128)(2,1)}, bf16[64,256]{1,0:T(8,128)(2,1)S(1)}, u32[]{:S(2)}, u32[]{:S(2)}) %collective-permute-start.7) | collective-permute-done | bytes 32800 | tf_op jit(solution)/shard_map/ppermute | solution.py:143
  12.2 0.8 pad_maximum_fusion.2.refs_5_
  13.0 2.5 %collective-permute-start.10 = (bf16[4,64,256]{2,1,0:T(8,128)(2,1)S(1)}, bf16[4,64,256]{2,1,0:T(8,128)(2,1)S(1)}, u32[]{:S(2)}, u32[]{:S(2)}) collective-permute-start(bf16[4,64,256]{2,1,0:T(8,128)(2,1)S(1)} %pad_maximum_fusion.2.refs_5_), channel_id=1, source_target_pairs={{0,6},{1,7},{2,4},{3,5},{4,2},{5,3},{6,0},{7,1},{8,14},{9,15},{10,... | collective-permute-start | bytes 393224 | tf_op jit(solution)/shard_map/ppermute | solution.py:143
  15.5 0.5 collective-permute-start.9
  16.0 0.5 collective-permute-start.8
  16.6 0.7 slice_bitcast_fusion.4
  17.3 3.4 %collective-permute-start = (bf16[16,512]{1,0:T(8,128)(2,1)S(1)}, bf16[16,512]{1,0:T(8,128)(2,1)S(1)}, u32[]{:S(2)}, u32[]{:S(2)}) collective-permute-start(bf16[16,512]{1,0:T(8,128)(2,1)S(1)} %slice_bitcast_fusion.4), channel_id=1, source_target_pairs={{0,4},{4,8},{8,12},{12,16},{16,20},{20,24},{24,28},{1,5},{5,9},{9,... | collective-permute-start | bytes 49160 | tf_op jit(solution)/shard_map/ppermute | solution.py:19
  20.7 1.4 %collective-permute-done.edge_ref = bf16[16,512]{1,0:T(8,128)(2,1)S(1)} collective-permute-done((bf16[16,512]{1,0:T(8,128)(2,1)S(1)}, bf16[16,512]{1,0:T(8,128)(2,1)S(1)}, u32[]{:S(2)}, u32[]{:S(2)}) %collective-permute-start) | collective-permute-done | bytes 16416 | tf_op jit(solution)/shard_map/ppermute | solution.py:19
  22.1 0.9 copy-done
  23.0 1.1 %copy-done.2 = bf16[3,512,256]{2,1,0:T(8,128)(2,1)S(1)} copy-done((bf16[3,512,256]{2,1,0:T(8,128)(2,1)S(1)}, bf16[3,512,256]{2,1,0:T(8,128)(2,1)}, u32[]{:S(2)}) %copy-start.2) | copy-done | bytes 786456
  24.1 0.7 copy-done.6
  24.8 0.7 copy-done.8
  25.5 1.3 %shard_map.102 = (bf16[64,256]{1,0:T(8,128)(2,1)S(1)}, bf16[64,256]{1,0:T(8,128)(2,1)S(1)}, bf16[64,256]{1,0:T(8,128)(2,1)S(1)}, bf16[64,256]{1,0:T(8,128)(2,1)S(1)}) custom-call(s32[8]{0:T(128)S(1)} %bitcast.44, bf16[128,512]{1,0:T(8,128)(2,1)S(1)} %bitcast.36, bf16[16,512]{1,0:T(8,128)(2,1)S(1)} %collective-permute-done.edge_ref, s32[1,128]{1,0:T(1,128)S(1)} %bitcast.46, ...), custom_call_target="tpu_custom_call" | custom-call | bytes 1065504 | tf_op jit(solution)/shard_map/pallas_call | solution.py:429
  26.8 1.8 %collective-permute-start.1 = (bf16[64,256]{1,0:T(8,128)(2,1)S(1)}, bf16[64,256]{1,0:T(8,128)(2,1)S(1)}, u32[]{:S(2)}, u32[]{:S(2)}) collective-permute-start(bf16[64,256]{1,0:T(8,128)(2,1)S(1)} %get-tuple-element.23), channel_id=1, source_target_pairs={{0,8},{4,12},{8,0},{12,4},{16,24},{20,28},{24,16},{28,20},{1,9},{5... | collective-permute-start | bytes 98312 | tf_op jit(solution)/shard_map/ppermute | solution.py:143
  28.6 0.9 collective-permute-start.2
  29.4 1.5 %collective-permute-done.1.refs_1_ = bf16[64,256]{1,0:T(8,128)(2,1)S(1)} collective-permute-done((bf16[64,256]{1,0:T(8,128)(2,1)S(1)}, bf16[64,256]{1,0:T(8,128)(2,1)S(1)}, u32[]{:S(2)}, u32[]{:S(2)}) %collective-permute-start.1) | collective-permute-done | bytes 32800 | tf_op jit(solution)/shard_map/ppermute | solution.py:143
  30.9 1.9 %collective-permute-start.3 = (bf16[64,256]{1,0:T(8,128)(2,1)S(1)}, bf16[64,256]{1,0:T(8,128)(2,1)S(1)}, u32[]{:S(2)}, u32[]{:S(2)}) collective-permute-start(bf16[64,256]{1,0:T(8,128)(2,1)S(1)} %get-tuple-element.25), channel_id=1, source_target_pairs={{0,24},{4,28},{8,16},{12,20},{16,8},{20,12},{24,0},{28,4},{1,25},{... | collective-permute-start | bytes 98312 | tf_op jit(solution)/shard_map/ppermute | solution.py:143
  32.8 0.6 collective-permute-done.2.refs_2_
  33.5 3.2 %collective-permute-done.3.refs_3_ = bf16[64,256]{1,0:T(8,128)(2,1)S(1)} collective-permute-done((bf16[64,256]{1,0:T(8,128)(2,1)S(1)}, bf16[64,256]{1,0:T(8,128)(2,1)S(1)}, u32[]{:S(2)}, u32[]{:S(2)}) %collective-permute-start.3) | collective-permute-done | bytes 32800 | tf_op jit(solution)/shard_map/ppermute | solution.py:143
  36.6 0.5 collective-permute-start.13
  37.1 0.1 collective-permute-start.12
  37.2 2.1 %collective-permute-start.4 = (bf16[128,256]{1,0:T(8,128)(2,1)S(1)}, bf16[128,256]{1,0:T(8,128)(2,1)S(1)}, u32[]{:S(2)}, u32[]{:S(2)}) collective-permute-start(bf16[128,256]{1,0:T(8,128)(2,1)S(1)} %pad_maximum_fusion.3), channel_id=1, source_target_pairs={{0,4},{4,0},{8,12},{12,8},{16,20},{20,16},{24,28},{28,24},{1,5},{5... | collective-permute-start | bytes 196616 | tf_op jit(solution)/shard_map/ppermute | solution.py:143
  39.4 2.7 %collective-permute-done.4.refs_4_ = bf16[128,256]{1,0:T(8,128)(2,1)S(1)} collective-permute-done((bf16[128,256]{1,0:T(8,128)(2,1)S(1)}, bf16[128,256]{1,0:T(8,128)(2,1)S(1)}, u32[]{:S(2)}, u32[]{:S(2)}) %collective-permute-start.4) | collective-permute-done | bytes 65568 | tf_op jit(solution)/shard_map/ppermute | solution.py:143
  42.1 0.7 copy-done.5
  42.8 1.2 %shard_map.103 = (bf16[144,256]{1,0:T(8,128)(2,1)S(1)}, bf16[144,2048]{1,0:T(8,128)(2,1)S(1)}, bf16[144,256]{1,0:T(8,128)(2,1)S(1)}, f32[8,128]{1,0:T(8,128)S(1)}) custom-call(bf16[64,256]{1,0:T(8,128)(2,1)S(1)} %get-tuple-element.22.refs_0_, bf16[64,256]{1,0:T(8,128)(2,1)S(1)} %collective-permute-done.1.refs_1_, ...), custom_call_target="tpu_custom_call" | custom-call | bytes 2551808 | tf_op jit(solution)/shard_map/pallas_call | solution.py:429
  44.0 0.5 shard_map.109
  44.5 0.1 collective-permute-start.27
  44.6 0.1 collective-permute-start.22
  44.7 8.4 %collective-permute-done.22.refs_1_ = bf16[128,512]{1,0:T(8,128)(2,1)S(1)} collective-permute-done((bf16[128,512]{1,0:T(8,128)(2,1)S(1)}, bf16[128,512]{1,0:T(8,128)(2,1)S(1)}, u32[]{:S(2)}, u32[]{:S(2)}) %collective-permute-start.22) | collective-permute-done | bytes 131104 | tf_op jit(solution)/shard_map/ppermute | solution.py:143
  53.1 0.1 collective-permute-start.23
  53.2 0.1 convert_add_fusion
  53.4 1.6 %collective-permute-start.28 = (bf16[8,64,256]{2,1,0:T(8,128)(2,1)S(1)}, bf16[8,64,256]{2,1,0:T(8,128)(2,1)S(1)}, u32[]{:S(2)}, u32[]{:S(2)}) collective-permute-start(bf16[8,64,256]{2,1,0:T(8,128)(2,1)S(1)} %slice.114), channel_id=1, source_target_pairs={{0,2},{1,3},{2,0},{3,1},{4,6},{5,7},{6,4},{7,5},{8,10},{9,11},{10,... | collective-permute-start | bytes 786440 | tf_op jit(solution)/shard_map/ppermute | solution.py:143
  55.0 6.5 %collective-permute-done.23.refs_2_ = bf16[256,512]{1,0:T(8,128)(2,1)S(1)} collective-permute-done((bf16[256,512]{1,0:T(8,128)(2,1)S(1)}, bf16[256,512]{1,0:T(8,128)(2,1)S(1)}, u32[]{:S(2)}, u32[]{:S(2)}) %collective-permute-start.23) | collective-permute-done | bytes 262176 | tf_op jit(solution)/shard_map/ppermute | solution.py:143
  61.5 0.8 collective-permute-start.24
  62.3 3.1 %collective-permute-start.21 = (bf16[144,256]{1,0:T(8,128)(2,1)S(1)}, bf16[144,256]{1,0:T(8,128)(2,1)S(1)}, u32[]{:S(2)}, u32[]{:S(2)}) collective-permute-start(bf16[144,256]{1,0:T(8,128)(2,1)S(1)} %get-tuple-element.26.refs_0_), channel_id=1, source_target_pairs={{0,28},{4,24},{8,20},{12,16},{16,12},{20,8},{24,4},{28,0},{1,29},{... | collective-permute-start | bytes 221192 | tf_op jit(solution)/shard_map/ppermute | solution.py:143
  65.3 1.5 %collective-permute-start.20 = (bf16[144,256]{1,0:T(8,128)(2,1)S(1)}, bf16[144,256]{1,0:T(8,128)(2,1)S(1)}, u32[]{:S(2)}, u32[]{:S(2)}) collective-permute-start(bf16[144,256]{1,0:T(8,128)(2,1)S(1)} %get-tuple-element.26.refs_0_), channel_id=1, source_target_pairs={{0,24},{4,28},{8,16},{12,20},{16,8},{20,12},{24,0},{28,4},{1,25},{... | collective-permute-start | bytes 221192 | tf_op jit(solution)/shard_map/ppermute | solution.py:143
  67.0 0.9 collective-permute-start.29
  67.8 2.3 %collective-permute-done.21.refs_7_ = bf16[144,256]{1,0:T(8,128)(2,1)S(1)} collective-permute-done((bf16[144,256]{1,0:T(8,128)(2,1)S(1)}, bf16[144,256]{1,0:T(8,128)(2,1)S(1)}, u32[]{:S(2)}, u32[]{:S(2)}) %collective-permute-start.21) | collective-permute-done | bytes 73760 | tf_op jit(solution)/shard_map/ppermute | solution.py:143
  70.1 1.3 %collective-permute-start.18 = (bf16[144,256]{1,0:T(8,128)(2,1)S(1)}, bf16[144,256]{1,0:T(8,128)(2,1)S(1)}, u32[]{:S(2)}, u32[]{:S(2)}) collective-permute-start(bf16[144,256]{1,0:T(8,128)(2,1)S(1)} %get-tuple-element.26.refs_0_), channel_id=1, source_target_pairs={{0,16},{4,20},{8,24},{12,28},{16,0},{20,4},{24,8},{28,12},{1,17},{... | collective-permute-start | bytes 221192 | tf_op jit(solution)/shard_map/ppermute | solution.py:143
  71.4 0.2 collective-permute-done.20.refs_6_
  71.7 3.0 %collective-permute-start.17 = (bf16[144,256]{1,0:T(8,128)(2,1)S(1)}, bf16[144,256]{1,0:T(8,128)(2,1)S(1)}, u32[]{:S(2)}, u32[]{:S(2)}) collective-permute-start(bf16[144,256]{1,0:T(8,128)(2,1)S(1)} %get-tuple-element.26.refs_0_), channel_id=1, source_target_pairs={{0,12},{4,8},{8,4},{12,0},{16,28},{20,24},{24,20},{28,16},{1,13},{... | collective-permute-start | bytes 221192 | tf_op jit(solution)/shard_map/ppermute | solution.py:143
  74.6 2.0 %collective-permute-done.19.refs_5_ = bf16[144,256]{1,0:T(8,128)(2,1)S(1)} collective-permute-done((bf16[144,256]{1,0:T(8,128)(2,1)S(1)}, bf16[144,256]{1,0:T(8,128)(2,1)S(1)}, u32[]{:S(2)}, u32[]{:S(2)}) %collective-permute-start.19) | collective-permute-done | bytes 73760 | tf_op jit(solution)/shard_map/ppermute | solution.py:143
  76.6 1.0 collective-permute-start.16
  77.6 3.6 %collective-permute-done.24.refs_3_ = bf16[512,512]{1,0:T(8,128)(2,1)S(1)} collective-permute-done((bf16[512,512]{1,0:T(8,128)(2,1)S(1)}, bf16[512,512]{1,0:T(8,128)(2,1)S(1)}, u32[]{:S(2)}, u32[]{:S(2)}) %collective-permute-start.24) | collective-permute-done | bytes 524320 | tf_op jit(solution)/shard_map/ppermute | solution.py:143
  81.2 0.7 collective-permute-start.15
  81.9 3.5 %shard_map.104 = (bf16[512,1024]{1,0:T(8,128)(2,1)S(1)}, s32[1024,3]{1,0:T(8,128)S(1)}) custom-call(s32[8]{0:T(128)S(1)} %bitcast.45, f32[8,128]{1,0:T(8,128)S(1)} %get-tuple-element.27.owners_ref, bf16[128,512]{1,0:T(8,128)(2,1)S(1)} %bitcast.40, bf16[128,512]{1,0:T(8,128)(2,1)S(1)} %collective-permute-done.22.refs_1_, ...), custom_call_target="tpu_custom_call" | custom-call | bytes 2113568 | tf_op jit(solution)/shard_map/pallas_call | solution.py:429
  85.4 0.1 collective-permute-done.15.refs_1_
  85.5 1.7 %shard_map.105 = (bf16[784,256]{1,0:T(8,128)(2,1)S(1)}, bf16[1024,768]{1,0:T(8,128)(2,1)S(1)}, f32[8,256]{1,0:T(8,128)S(1)}) custom-call(bf16[144,256]{1,0:T(8,128)(2,1)S(1)} %get-tuple-element.26.refs_0_, bf16[144,256]{1,0:T(8,128)(2,1)S(1)} %collective-permute-done.15.refs_1_, bf16[144,256]{1,0:T(8,128)(2,1)S(1)} %collective-permute-done.16.refs_2_, ...), custom_call_target="tpu_custom_call" | custom-call | bytes 3633152 | tf_op jit(solution)/shard_map/pallas_call | solution.py:429
  87.3 0.3 collective-permute-start.30
  87.7 2.2 %collective-permute-start.32 = (bf16[64,256]{1,0:T(8,128)(2,1)S(1)}, bf16[64,256]{1,0:T(8,128)(2,1)S(1)}, u32[]{:S(2)}, u32[]{:S(2)}) collective-permute-start(bf16[64,256]{1,0:T(8,128)(2,1)S(1)} %get-tuple-element.43), channel_id=1, source_target_pairs={{0,24},{4,28},{8,16},{12,20},{16,8},{20,12},{24,0},{28,4},{1,25},{... | collective-permute-start | bytes 98312 | tf_op jit(solution)/shard_map/ppermute | solution.py:143
  89.9 1.0 %collective-permute-start.31 = (bf16[64,256]{1,0:T(8,128)(2,1)S(1)}, bf16[64,256]{1,0:T(8,128)(2,1)S(1)}, u32[]{:S(2)}, u32[]{:S(2)}) collective-permute-start(bf16[64,256]{1,0:T(8,128)(2,1)S(1)} %get-tuple-element.44), channel_id=1, source_target_pairs={{0,16},{4,20},{8,24},{12,28},{16,0},{20,4},{24,8},{28,12},{1,17},{... | collective-permute-start | bytes 98312 | tf_op jit(solution)/shard_map/ppermute | solution.py:143
  90.9 0.6 shard_map.107.kept_ref
  91.5 0.6 copy-done.3
  92.0 1.0 %shard_map.106 = bf16[128,512]{1,0:T(8,128)(2,1)} custom-call(bf16[128,512]{1,0:T(8,128)(2,1)S(1)} %bitcast.41, bf16[1024,768]{1,0:T(8,128)(2,1)S(1)} %get-tuple-element.30.windows_ref, bf16[3,512,256]{2,1,0:T(8,128)(2,1)S(1)} %copy-done.3), custom_call_target="tpu_custom_call" | custom-call | bytes 2621440 | tf_op jit(solution)/shard_map/pallas_call | solution.py:429
  93.1 0.1 shard_map.108
  93.2 1.6 %collective-permute-start.26 = (bf16[400,256]{1,0:T(8,128)(2,1)S(1)}, bf16[400,256]{1,0:T(8,128)(2,1)S(1)}, u32[]{:S(2)}, u32[]{:S(2)}) collective-permute-start(bf16[400,256]{1,0:T(8,128)(2,1)S(1)} %get-tuple-element.34), channel_id=1, source_target_pairs={{0,2},{1,3},{2,0},{3,1},{4,6},{5,7},{6,4},{7,5},{8,10},{9,11},{10,... | collective-permute-start | bytes 614408 | tf_op jit(solution)/shard_map/ppermute | solution.py:143
  94.8 0.6 fusion.3
  95.4 4.4 %collective-permute-done.26 = bf16[400,256]{1,0:T(8,128)(2,1)S(1)} collective-permute-done((bf16[400,256]{1,0:T(8,128)(2,1)S(1)}, bf16[400,256]{1,0:T(8,128)(2,1)S(1)}, u32[]{:S(2)}, u32[]{:S(2)}) %collective-permute-start.26) | collective-permute-done | bytes 204832 | tf_op jit(solution)/shard_map/ppermute | solution.py:143
  99.9 0.8 slice_add_fusion.1
  100.7 0.6 copy.11
  (48 shorter events, 0.4 us)
Async XLA Ops:
  0.6 6.7 %collective-permute-start.6 = (bf16[64,256]{1,0:T(8,128)(2,1)}, bf16[64,256]{1,0:T(8,128)(2,1)S(1)}, u32[]{:S(2)}, u32[]{:S(2)}) collective-permute-start(bf16[64,256]{1,0:T(8,128)(2,1)} %bitcast.49), channel_id=1, source_target_pairs={{0,16},{4,20},{8,24},{12,28},{16,0},{20,4},{24,8},{28,12},{1,17},{... | collective-permute-start | bytes 98312 | tf_op jit(solution)/shard_map/ppermute | solution.py:143
  4.7 4.1 %collective-permute-start.5 = (bf16[64,256]{1,0:T(8,128)(2,1)}, bf16[64,256]{1,0:T(8,128)(2,1)S(1)}, u32[]{:S(2)}, u32[]{:S(2)}) collective-permute-start(bf16[64,256]{1,0:T(8,128)(2,1)} %bitcast.50), channel_id=1, source_target_pairs={{0,8},{4,12},{8,0},{12,4},{16,24},{20,28},{24,16},{28,20},{1,9},{5... | collective-permute-start | bytes 98312 | tf_op jit(solution)/shard_map/ppermute | solution.py:143
  6.3 5.9 %collective-permute-start.7 = (bf16[64,256]{1,0:T(8,128)(2,1)}, bf16[64,256]{1,0:T(8,128)(2,1)S(1)}, u32[]{:S(2)}, u32[]{:S(2)}) collective-permute-start(bf16[64,256]{1,0:T(8,128)(2,1)} %bitcast.51), channel_id=1, source_target_pairs={{0,24},{4,28},{8,16},{12,20},{16,8},{20,12},{24,0},{28,4},{1,25},{... | collective-permute-start | bytes 98312 | tf_op jit(solution)/shard_map/ppermute | solution.py:143
  13.0 23.6 %collective-permute-start.10 = (bf16[4,64,256]{2,1,0:T(8,128)(2,1)S(1)}, bf16[4,64,256]{2,1,0:T(8,128)(2,1)S(1)}, u32[]{:S(2)}, u32[]{:S(2)}) collective-permute-start(bf16[4,64,256]{2,1,0:T(8,128)(2,1)S(1)} %pad_maximum_fusion.2.refs_5_), channel_id=1, source_target_pairs={{0,6},{1,7},{2,4},{3,5},{4,2},{5,3},{6,0},{7,1},{8,14},{9,15},{10,... | collective-permute-start | bytes 393224 | tf_op jit(solution)/shard_map/ppermute | solution.py:143
  15.5 21.1 %collective-permute-start.9 = (bf16[4,64,256]{2,1,0:T(8,128)(2,1)S(1)}, bf16[4,64,256]{2,1,0:T(8,128)(2,1)S(1)}, u32[]{:S(2)}, u32[]{:S(2)}) collective-permute-start(bf16[4,64,256]{2,1,0:T(8,128)(2,1)S(1)} %pad_maximum_fusion.2.refs_5_), channel_id=1, source_target_pairs={{0,2},{1,3},{2,0},{3,1},{4,6},{5,7},{6,4},{7,5},{8,10},{9,11},{10,... | collective-permute-start | bytes 393224 | tf_op jit(solution)/shard_map/ppermute | solution.py:143
  16.0 21.1 %collective-permute-start.8 = (bf16[4,64,256]{2,1,0:T(8,128)(2,1)S(1)}, bf16[4,64,256]{2,1,0:T(8,128)(2,1)S(1)}, u32[]{:S(2)}, u32[]{:S(2)}) collective-permute-start(bf16[4,64,256]{2,1,0:T(8,128)(2,1)S(1)} %pad_maximum_fusion.2.refs_5_), channel_id=1, source_target_pairs={{0,4},{4,0},{8,12},{12,8},{16,20},{20,16},{24,28},{28,24},{1,5},{5... | collective-permute-start | bytes 393224 | tf_op jit(solution)/shard_map/ppermute | solution.py:143
  17.3 4.8 %collective-permute-start = (bf16[16,512]{1,0:T(8,128)(2,1)S(1)}, bf16[16,512]{1,0:T(8,128)(2,1)S(1)}, u32[]{:S(2)}, u32[]{:S(2)}) collective-permute-start(bf16[16,512]{1,0:T(8,128)(2,1)S(1)} %slice_bitcast_fusion.4), channel_id=1, source_target_pairs={{0,4},{4,8},{8,12},{12,16},{16,20},{20,24},{24,28},{1,5},{5,9},{9,... | collective-permute-start | bytes 49160 | tf_op jit(solution)/shard_map/ppermute | solution.py:19
  22.1 0.9 copy-start
  23.0 1.1 %copy-start.2 = (bf16[3,512,256]{2,1,0:T(8,128)(2,1)S(1)}, bf16[3,512,256]{2,1,0:T(8,128)(2,1)}, u32[]{:S(2)}) copy-start(bf16[3,512,256]{2,1,0:T(8,128)(2,1)} %w_ref.3) | copy-start | bytes 2359300
  24.1 0.7 copy-start.6
  24.8 0.7 copy-start.8
  25.5 16.6 %copy-start.4 = (bf16[1,136,2048]{2,1,0:T(8,128)(2,1)S(1)}, bf16[1,136,2048]{2,1,0:T(8,128)(2,1)}, u32[]{:S(2)}) copy-start(bf16[1,136,2048]{2,1,0:T(8,128)(2,1)} %param.13) | copy-start | bytes 1671172
  26.7 17.9 %copy-start.1 = (bf16[1,128,512]{2,1,0:T(8,128)(2,1)S(1)}, bf16[1,128,512]{2,1,0:T(8,128)(2,1)}, u32[]{:S(2)}) copy-start(bf16[1,128,512]{2,1,0:T(8,128)(2,1)} %param.7) | copy-start | bytes 393220
  26.8 4.1 %collective-permute-start.1 = (bf16[64,256]{1,0:T(8,128)(2,1)S(1)}, bf16[64,256]{1,0:T(8,128)(2,1)S(1)}, u32[]{:S(2)}, u32[]{:S(2)}) collective-permute-start(bf16[64,256]{1,0:T(8,128)(2,1)S(1)} %get-tuple-element.23), channel_id=1, source_target_pairs={{0,8},{4,12},{8,0},{12,4},{16,24},{20,28},{24,16},{28,20},{1,9},{5... | collective-permute-start | bytes 98312 | tf_op jit(solution)/shard_map/ppermute | solution.py:143
  28.6 4.9 %collective-permute-start.2 = (bf16[64,256]{1,0:T(8,128)(2,1)S(1)}, bf16[64,256]{1,0:T(8,128)(2,1)S(1)}, u32[]{:S(2)}, u32[]{:S(2)}) collective-permute-start(bf16[64,256]{1,0:T(8,128)(2,1)S(1)} %get-tuple-element.24), channel_id=1, source_target_pairs={{0,16},{4,20},{8,24},{12,28},{16,0},{20,4},{24,8},{28,12},{1,17},{... | collective-permute-start | bytes 98312 | tf_op jit(solution)/shard_map/ppermute | solution.py:143
  30.9 5.7 %collective-permute-start.3 = (bf16[64,256]{1,0:T(8,128)(2,1)S(1)}, bf16[64,256]{1,0:T(8,128)(2,1)S(1)}, u32[]{:S(2)}, u32[]{:S(2)}) collective-permute-start(bf16[64,256]{1,0:T(8,128)(2,1)S(1)} %get-tuple-element.25), channel_id=1, source_target_pairs={{0,24},{4,28},{8,16},{12,20},{16,8},{20,12},{24,0},{28,4},{1,25},{... | collective-permute-start | bytes 98312 | tf_op jit(solution)/shard_map/ppermute | solution.py:143
  33.4 8.6 %collective-permute-start.11 = (bf16[4,64,256]{2,1,0:T(8,128)(2,1)S(1)}, bf16[4,64,256]{2,1,0:T(8,128)(2,1)S(1)}, u32[]{:S(2)}, u32[]{:S(2)}) collective-permute-start(bf16[4,64,256]{2,1,0:T(8,128)(2,1)S(1)} %pad_maximum_fusion.2.refs_5_), channel_id=1, source_target_pairs={{0,1},{1,0},{2,3},{3,2},{4,5},{5,4},{6,7},{7,6},{8,9},{9,8},{10,11... | collective-permute-start | bytes 393224 | tf_op jit(solution)/shard_map/ppermute | solution.py:143
  36.6 5.4 %collective-permute-start.14 = (bf16[4,64,256]{2,1,0:T(8,128)(2,1)S(1)}, bf16[4,64,256]{2,1,0:T(8,128)(2,1)S(1)}, u32[]{:S(2)}, u32[]{:S(2)}) collective-permute-start(bf16[4,64,256]{2,1,0:T(8,128)(2,1)S(1)} %collective-permute-done.10.refs_8_), channel_id=1, source_target_pairs={{0,1},{1,0},{2,3},{3,2},{4,5},{5,4},{6,7},{7,6},{8,9},{9,8},{10,11... | collective-permute-start | bytes 393224 | tf_op jit(solution)/shard_map/ppermute | solution.py:143
  36.6 5.4 %collective-permute-start.13 = (bf16[4,64,256]{2,1,0:T(8,128)(2,1)S(1)}, bf16[4,64,256]{2,1,0:T(8,128)(2,1)S(1)}, u32[]{:S(2)}, u32[]{:S(2)}) collective-permute-start(bf16[4,64,256]{2,1,0:T(8,128)(2,1)S(1)} %collective-permute-done.9.refs_7_), channel_id=1, source_target_pairs={{0,1},{1,0},{2,3},{3,2},{4,5},{5,4},{6,7},{7,6},{8,9},{9,8},{10,11... | collective-permute-start | bytes 393224 | tf_op jit(solution)/shard_map/ppermute | solution.py:143
  37.1 4.9 %collective-permute-start.12 = (bf16[4,64,256]{2,1,0:T(8,128)(2,1)S(1)}, bf16[4,64,256]{2,1,0:T(8,128)(2,1)S(1)}, u32[]{:S(2)}, u32[]{:S(2)}) collective-permute-start(bf16[4,64,256]{2,1,0:T(8,128)(2,1)S(1)} %collective-permute-done.8.refs_6_), channel_id=1, source_target_pairs={{0,1},{1,0},{2,3},{3,2},{4,5},{5,4},{6,7},{7,6},{8,9},{9,8},{10,11... | collective-permute-start | bytes 393224 | tf_op jit(solution)/shard_map/ppermute | solution.py:143
  37.2 4.8 %collective-permute-start.4 = (bf16[128,256]{1,0:T(8,128)(2,1)S(1)}, bf16[128,256]{1,0:T(8,128)(2,1)S(1)}, u32[]{:S(2)}, u32[]{:S(2)}) collective-permute-start(bf16[128,256]{1,0:T(8,128)(2,1)S(1)} %pad_maximum_fusion.3), channel_id=1, source_target_pairs={{0,4},{4,0},{8,12},{12,8},{16,20},{20,16},{24,28},{28,24},{1,5},{5... | collective-permute-start | bytes 196616 | tf_op jit(solution)/shard_map/ppermute | solution.py:143
  42.1 0.7 copy-start.5
  44.5 8.7 %collective-permute-start.27 = (bf16[16,64,256]{2,1,0:T(8,128)(2,1)S(1)}, bf16[16,64,256]{2,1,0:T(8,128)(2,1)S(1)}, u32[]{:S(2)}, u32[]{:S(2)}) collective-permute-start(bf16[16,64,256]{2,1,0:T(8,128)(2,1)S(1)} %get-tuple-element.38), channel_id=1, source_target_pairs={{0,1},{1,0},{2,3},{3,2},{4,5},{5,4},{6,7},{7,6},{8,9},{9,8},{10,11... | collective-permute-start | bytes 1572872 | tf_op jit(solution)/shard_map/ppermute | solution.py:143
  44.6 8.5 %collective-permute-start.22 = (bf16[128,512]{1,0:T(8,128)(2,1)S(1)}, bf16[128,512]{1,0:T(8,128)(2,1)S(1)}, u32[]{:S(2)}, u32[]{:S(2)}) collective-permute-start(bf16[128,512]{1,0:T(8,128)(2,1)S(1)} %bitcast.37), channel_id=1, source_target_pairs={{0,16},{4,20},{8,24},{12,28},{16,0},{20,4},{24,8},{28,12},{1,17},{... | collective-permute-start | bytes 393224 | tf_op jit(solution)/shard_map/ppermute | solution.py:143
  53.1 8.3 %collective-permute-start.23 = (bf16[256,512]{1,0:T(8,128)(2,1)S(1)}, bf16[256,512]{1,0:T(8,128)(2,1)S(1)}, u32[]{:S(2)}, u32[]{:S(2)}) collective-permute-start(bf16[256,512]{1,0:T(8,128)(2,1)S(1)} %pad_maximum_fusion.1), channel_id=1, source_target_pairs={{0,8},{4,12},{8,0},{12,4},{16,24},{20,28},{24,16},{28,20},{1,9},{5... | collective-permute-start | bytes 786440 | tf_op jit(solution)/shard_map/ppermute | solution.py:143
  53.4 28.5 %copy-start.7 = (s32[1,8]{1,0:T(1,128)S(1)}, s32[1,8]{1,0:T(1,128)}, u32[]{:S(2)}) copy-start(s32[1,8]{1,0:T(1,128)} %param.8) | copy-start | bytes 100
  53.4 13.5 %collective-permute-start.28 = (bf16[8,64,256]{2,1,0:T(8,128)(2,1)S(1)}, bf16[8,64,256]{2,1,0:T(8,128)(2,1)S(1)}, u32[]{:S(2)}, u32[]{:S(2)}) collective-permute-start(bf16[8,64,256]{2,1,0:T(8,128)(2,1)S(1)} %slice.114), channel_id=1, source_target_pairs={{0,2},{1,3},{2,0},{3,1},{4,6},{5,7},{6,4},{7,5},{8,10},{9,11},{10,... | collective-permute-start | bytes 786440 | tf_op jit(solution)/shard_map/ppermute | solution.py:143
  61.5 19.7 %collective-permute-start.24 = (bf16[512,512]{1,0:T(8,128)(2,1)S(1)}, bf16[512,512]{1,0:T(8,128)(2,1)S(1)}, u32[]{:S(2)}, u32[]{:S(2)}) collective-permute-start(bf16[512,512]{1,0:T(8,128)(2,1)S(1)} %pad_maximum_fusion), channel_id=1, source_target_pairs={{0,4},{4,0},{8,12},{12,8},{16,20},{20,16},{24,28},{28,24},{1,5},{5... | collective-permute-start | bytes 1572872 | tf_op jit(solution)/shard_map/ppermute | solution.py:143
  62.3 7.8 %collective-permute-start.21 = (bf16[144,256]{1,0:T(8,128)(2,1)S(1)}, bf16[144,256]{1,0:T(8,128)(2,1)S(1)}, u32[]{:S(2)}, u32[]{:S(2)}) collective-permute-start(bf16[144,256]{1,0:T(8,128)(2,1)S(1)} %get-tuple-element.26.refs_0_), channel_id=1, source_target_pairs={{0,28},{4,24},{8,20},{12,16},{16,12},{20,8},{24,4},{28,0},{1,29},{... | collective-permute-start | bytes 221192 | tf_op jit(solution)/shard_map/ppermute | solution.py:143
  65.3 6.3 %collective-permute-start.20 = (bf16[144,256]{1,0:T(8,128)(2,1)S(1)}, bf16[144,256]{1,0:T(8,128)(2,1)S(1)}, u32[]{:S(2)}, u32[]{:S(2)}) collective-permute-start(bf16[144,256]{1,0:T(8,128)(2,1)S(1)} %get-tuple-element.26.refs_0_), channel_id=1, source_target_pairs={{0,24},{4,28},{8,16},{12,20},{16,8},{20,12},{24,0},{28,4},{1,25},{... | collective-permute-start | bytes 221192 | tf_op jit(solution)/shard_map/ppermute | solution.py:143
  66.9 9.7 %collective-permute-start.19 = (bf16[144,256]{1,0:T(8,128)(2,1)S(1)}, bf16[144,256]{1,0:T(8,128)(2,1)S(1)}, u32[]{:S(2)}, u32[]{:S(2)}) collective-permute-start(bf16[144,256]{1,0:T(8,128)(2,1)S(1)} %get-tuple-element.26.refs_0_), channel_id=1, source_target_pairs={{0,20},{4,16},{8,28},{12,24},{16,4},{20,0},{24,12},{28,8},{1,21},{... | collective-permute-start | bytes 221192 | tf_op jit(solution)/shard_map/ppermute | solution.py:143
  67.0 20.3 %collective-permute-start.29 = (bf16[4,64,256]{2,1,0:T(8,128)(2,1)S(1)}, bf16[4,64,256]{2,1,0:T(8,128)(2,1)S(1)}, u32[]{:S(2)}, u32[]{:S(2)}) collective-permute-start(bf16[4,64,256]{2,1,0:T(8,128)(2,1)S(1)} %slice.115), channel_id=1, source_target_pairs={{0,4},{4,0},{8,12},{12,8},{16,20},{20,16},{24,28},{28,24},{1,5},{5... | collective-permute-start | bytes 393224 | tf_op jit(solution)/shard_map/ppermute | solution.py:143
  70.1 15.3 %collective-permute-start.18 = (bf16[144,256]{1,0:T(8,128)(2,1)S(1)}, bf16[144,256]{1,0:T(8,128)(2,1)S(1)}, u32[]{:S(2)}, u32[]{:S(2)}) collective-permute-start(bf16[144,256]{1,0:T(8,128)(2,1)S(1)} %get-tuple-element.26.refs_0_), channel_id=1, source_target_pairs={{0,16},{4,20},{8,24},{12,28},{16,0},{20,4},{24,8},{28,12},{1,17},{... | collective-permute-start | bytes 221192 | tf_op jit(solution)/shard_map/ppermute | solution.py:143
  71.7 13.8 %collective-permute-start.17 = (bf16[144,256]{1,0:T(8,128)(2,1)S(1)}, bf16[144,256]{1,0:T(8,128)(2,1)S(1)}, u32[]{:S(2)}, u32[]{:S(2)}) collective-permute-start(bf16[144,256]{1,0:T(8,128)(2,1)S(1)} %get-tuple-element.26.refs_0_), channel_id=1, source_target_pairs={{0,12},{4,8},{8,4},{12,0},{16,28},{20,24},{24,20},{28,16},{1,13},{... | collective-permute-start | bytes 221192 | tf_op jit(solution)/shard_map/ppermute | solution.py:143
  76.6 8.9 %collective-permute-start.16 = (bf16[144,256]{1,0:T(8,128)(2,1)S(1)}, bf16[144,256]{1,0:T(8,128)(2,1)S(1)}, u32[]{:S(2)}, u32[]{:S(2)}) collective-permute-start(bf16[144,256]{1,0:T(8,128)(2,1)S(1)} %get-tuple-element.26.refs_0_), channel_id=1, source_target_pairs={{0,8},{4,12},{8,0},{12,4},{16,24},{20,28},{24,16},{28,20},{1,9},{5... | collective-permute-start | bytes 221192 | tf_op jit(solution)/shard_map/ppermute | solution.py:143
  81.2 4.4 %collective-permute-start.15 = (bf16[144,256]{1,0:T(8,128)(2,1)S(1)}, bf16[144,256]{1,0:T(8,128)(2,1)S(1)}, u32[]{:S(2)}, u32[]{:S(2)}) collective-permute-start(bf16[144,256]{1,0:T(8,128)(2,1)S(1)} %get-tuple-element.26.refs_0_), channel_id=1, source_target_pairs={{0,4},{4,0},{8,12},{12,8},{16,20},{20,16},{24,28},{28,24},{1,5},{5... | collective-permute-start | bytes 221192 | tf_op jit(solution)/shard_map/ppermute | solution.py:143
  87.2 5.9 %collective-permute-start.25 = (bf16[784,256]{1,0:T(8,128)(2,1)S(1)}, bf16[784,256]{1,0:T(8,128)(2,1)S(1)}, u32[]{:S(2)}, u32[]{:S(2)}) collective-permute-start(bf16[784,256]{1,0:T(8,128)(2,1)S(1)} %get-tuple-element.31), channel_id=1, source_target_pairs={{0,1},{1,0},{2,3},{3,2},{4,5},{5,4},{6,7},{7,6},{8,9},{9,8},{10,11... | collective-permute-start | bytes 1204232 | tf_op jit(solution)/shard_map/ppermute | solution.py:143
  87.3 7.4 %collective-permute-start.30 = (bf16[64,256]{1,0:T(8,128)(2,1)S(1)}, bf16[64,256]{1,0:T(8,128)(2,1)S(1)}, u32[]{:S(2)}, u32[]{:S(2)}) collective-permute-start(bf16[64,256]{1,0:T(8,128)(2,1)S(1)} %get-tuple-element.42), channel_id=1, source_target_pairs={{0,8},{4,12},{8,0},{12,4},{16,24},{20,28},{24,16},{28,20},{1,9},{5... | collective-permute-start | bytes 98312 | tf_op jit(solution)/shard_map/ppermute | solution.py:143
  87.7 7.1 %collective-permute-start.32 = (bf16[64,256]{1,0:T(8,128)(2,1)S(1)}, bf16[64,256]{1,0:T(8,128)(2,1)S(1)}, u32[]{:S(2)}, u32[]{:S(2)}) collective-permute-start(bf16[64,256]{1,0:T(8,128)(2,1)S(1)} %get-tuple-element.43), channel_id=1, source_target_pairs={{0,24},{4,28},{8,16},{12,20},{16,8},{20,12},{24,0},{28,4},{1,25},{... | collective-permute-start | bytes 98312 | tf_op jit(solution)/shard_map/ppermute | solution.py:143
  89.9 4.9 %collective-permute-start.31 = (bf16[64,256]{1,0:T(8,128)(2,1)S(1)}, bf16[64,256]{1,0:T(8,128)(2,1)S(1)}, u32[]{:S(2)}, u32[]{:S(2)}) collective-permute-start(bf16[64,256]{1,0:T(8,128)(2,1)S(1)} %get-tuple-element.44), channel_id=1, source_target_pairs={{0,16},{4,20},{8,24},{12,28},{16,0},{20,4},{24,8},{28,12},{1,17},{... | collective-permute-start | bytes 98312 | tf_op jit(solution)/shard_map/ppermute | solution.py:143
  90.9 1.1 %copy-start.3 = (bf16[3,512,256]{2,1,0:T(8,128)(2,1)S(1)}, bf16[3,512,256]{2,1,0:T(8,128)(2,1)}, u32[]{:S(2)}) copy-start(bf16[3,512,256]{2,1,0:T(8,128)(2,1)} %w_ref.3) | copy-start | bytes 2359300
  93.2 6.7 %collective-permute-start.26 = (bf16[400,256]{1,0:T(8,128)(2,1)S(1)}, bf16[400,256]{1,0:T(8,128)(2,1)S(1)}, u32[]{:S(2)}, u32[]{:S(2)}) collective-permute-start(bf16[400,256]{1,0:T(8,128)(2,1)S(1)} %get-tuple-element.34), channel_id=1, source_target_pairs={{0,2},{1,3},{2,0},{3,1},{4,6},{5,7},{6,4},{7,5},{8,10},{9,11},{10,... | collective-permute-start | bytes 614408 | tf_op jit(solution)/shard_map/ppermute | solution.py:143

commit v2 on v1

--- a/solution.py
+++ b/solution.py
@@ -9,6 +9,7 @@
 
 F32 = jnp.float32
 BF16 = jnp.bfloat16
+HEAVY = 20000000000
 VMEM = pl.BlockSpec(memory_space=pltpu.VMEM)
 SMEM = pl.BlockSpec(memory_space=pltpu.SMEM)
 
@@ -183,41 +184,75 @@
     )
 
 
-def encode_kernel(piece, capacity, lengths_ref, feat_ref, edge_ref, owner_ref, w_ref, *rest):
-    out_refs, padded = rest[:-1], rest[-1]
+def activate_kernel(feat_ref, padded_ref, mine_ref, other_ref, turned):
     frames, channels = feat_ref.shape
+    near = jnp.bitwise_and(lax.axis_index("seq"), 1)
+    act = elu_wide(feat_ref[...].astype(F32)).astype(BF16).astype(F32)
+    padded_ref[0:8, :] = jnp.zeros((8, channels), F32)
+    padded_ref[8 : 8 + frames, :] = act
+    padded_ref[8 + frames :, :] = jnp.zeros((16, channels), F32)
+    turned[...] = act.T
+    half = mine_ref.shape[0] // 4
+    for book in range(4):
+        for out_ref, side in ((mine_ref, near), (other_ref, 1 - near)):
+            at = pl.multiple_of((2 * book + side) * half, half)
+            out_ref[book * half : (book + 1) * half, :] = turned[pl.ds(at, half), :].astype(BF16)
+
+
+def encode_kernel(
+    piece, lengths_ref, padded, owner_ref, w_ref, total_ref, placed_ref, edge_ref, named_ref
+):
+    frames = total_ref.shape[0]
     taps = w_ref.shape[0]
-    seq_count = 2 * len(out_refs)
     me = lax.axis_index("seq")
-    edge = elu_wide(edge_ref[...].astype(F32)).astype(BF16).astype(F32)
-    padded[0:8, :] = edge[edge.shape[0] - 8 :, :]
-    padded[8:, :] = elu_wide(feat_ref[...].astype(F32)).astype(BF16).astype(F32)
+    seq_count = placed_ref.shape[0] // piece
+    owner = owner_ref[...]
+    rank = ranks_of(owner, seq_count).astype(jnp.int32)
+    row = jnp.bitwise_xor(owner, me) * piece + rank
+    placed_ref[...] = (iota((seq_count * piece, frames), 0) == row).astype(F32).astype(BF16)
+    named = owner.astype(F32)
+    if named_ref.shape[1] > frames:
+        named = jnp.concatenate([named, jnp.zeros((1, named_ref.shape[1] - frames), F32)], axis=1)
+    named_ref[...] = named
     position = me * frames + iota((frames, 1), 0)
     start_of = start_below(position, lengths_ref)
-    total = jnp.zeros((frames, w_ref.shape[2]), F32)
+    after = (me + 1) * frames + iota((16, 1), 0)
+    start_after = start_below(after, lengths_ref)
+    total = jnp.zeros(total_ref.shape, F32)
+    edge = jnp.zeros((16, total.shape[1]), F32)
     for tap in range(taps):
         window = padded[8 - tap : 8 - tap + frames, :]
         window = jnp.where(position - tap >= start_of, window, 0.0).astype(BF16)
         total = total + jnp.dot(window, w_ref[tap], preferred_element_type=F32)
-    latent = total.astype(BF16)
-    owner = owner_ref[...]
-    rank = ranks_of(owner, seq_count).astype(jnp.int32)
-    row = jnp.bitwise_xor(owner, me) * piece + rank
-    placed = (iota((seq_count * piece, frames), 0) == row).astype(F32).astype(BF16)
-    outgoing = jnp.dot(placed, latent, preferred_element_type=F32)
-    named = owner.astype(F32)
-    if outgoing.shape[1] > frames:
-        named = jnp.concatenate([named, jnp.zeros((1, outgoing.shape[1] - frames), F32)], axis=1)
+        if tap:
+            window = padded[8 + frames - tap : 24 + frames - tap, :]
+            window = jnp.where(after - tap >= start_after, window, 0.0).astype(BF16)
+            edge = edge + jnp.dot(window, w_ref[tap], preferred_element_type=F32)
+    total_ref[...] = total
+    edge_ref[...] = edge[: edge_ref.shape[0]]
+
+
+def place_kernel(piece, total_ref, edge_ref, placed_ref, named_ref, *out_refs):
+    seq_count = 2 * len(out_refs)
+    lines = edge_ref.shape[0]
+    total = total_ref[...]
+    latent = jnp.concatenate([total[:lines] + edge_ref[...], total[lines:]], axis=0).astype(BF16)
+    outgoing = jnp.dot(placed_ref[...], latent, preferred_element_type=F32)
     last = iota((seq_count * piece, 1), 0) % piece == piece - 1
-    outgoing = jnp.where(last, named, outgoing).astype(BF16)
+    outgoing = jnp.where(last, named_ref[...], outgoing).astype(BF16)
     for far, out_ref in enumerate(out_refs):
         out_ref[...] = outgoing[2 * far * piece : 2 * (far + 1) * piece]
 
 
-def middle_kernel(piece, capacity, frames, count, *refs):
+def join_rows_kernel(skip, *refs):
+    rows = refs[0].shape[0] - skip
+    for index, ref in enumerate(refs[:-1]):
+        refs[-1][index * rows : (index + 1) * rows, :] = ref[skip:, :]
+
+
+def middle_kernel(piece, capacity, frames, count, columns, *refs):
     far_count = count // 2
-    latents = refs[:far_count]
-    near = refs[far_count]
+    landed, near = refs[:far_count], refs[far_count]
     w_refs = refs[far_count + 1 : far_count + 9]
     gain_ref, cot_ref, back_ref, hg_ref, arrived_ref, owners_ref = refs[far_count + 9 : far_count + 15]
     gathered, w_full, hidden, back = refs[far_count + 15 :]
@@ -226,21 +261,22 @@
     latent_width = back_ref.shape[1]
     seq, book = lax.axis_index("seq"), lax.axis_index("book")
     for far in range(far_count):
-        gathered[2 * far * piece : (2 * far + 1) * piece, :] = latents[far][0:piece, :]
+        gathered[2 * far * piece : (2 * far + 1) * piece, :] = landed[far][0:piece, :]
         gathered[(2 * far + 1) * piece : (2 * far + 2) * piece, :] = near[
             far * piece : (far + 1) * piece, :
         ]
     for rel in range(count):
         line = gathered[rel * piece : (rel + 1) * piece, 0:frames].astype(F32)
         owners_ref[pl.ds(jnp.bitwise_xor(seq, rel), 1), :] = line[piece - 1 : piece, :]
-    columns = w_refs[0].shape[1]
     for index, w_ref in enumerate(w_refs):
         near_seq, near_y, near_core = index & 1, (index >> 1) & 1, index >> 2
         for far in range(far_count):
             at = jnp.bitwise_xor(seq, 2 * far + near_seq) * 4 + jnp.bitwise_xor(
                 book, near_y * 2 + near_core
             )
-            w_full[pl.ds(pl.multiple_of(at * columns, columns), columns), :] = w_ref[far]
+            w_full[pl.ds(pl.multiple_of(at * columns, columns), columns), :] = w_ref[
+                far * columns : (far + 1) * columns, :
+            ]
     slot = iota((rows, 1), 0)
     source = jnp.zeros_like(slot)
     for block in range(1, count):
@@ -301,43 +337,40 @@
         keep_ref[place] = jnp.where(core == 0, low, high).astype(BF16)
 
 
-def prepare_kernel(capacity, rows, orders, lengths_ref, owners_ref, *refs):
-    f_refs = refs[: len(orders)]
-    turned_ref, facts_ref = refs[len(orders) :]
+def prepare_kernel(capacity, rows, lengths_ref, owners_ref, facts_ref):
     count, frames = owners_ref.shape
+    taps = facts_ref.shape[1]
     me = lax.axis_index("seq")
-    for f_ref, order in zip(f_refs, orders):
-        for index, rel in enumerate(order):
-            act = elu_wide(f_ref[index * frames : (index + 1) * frames, :].astype(F32))
-            at = jnp.bitwise_xor(me, rel) * frames
-            turned_ref[:, pl.ds(pl.multiple_of(at, frames), frames)] = act.T.astype(BF16)
     owners = owners_ref[...]
     ranks = ranks_of(owners, count)
+    position = iota((count, frames), 0) * frames + iota((count, frames), 1)
+    rows_of = [jnp.bitwise_xor(owners.astype(jnp.int32), me).astype(F32), ranks]
+    for tap in range(1, taps):
+        later = position + tap
+        valid = (later < count * frames) & (position >= start_below(later, lengths_ref))
+        rows_of.append(valid.astype(F32))
     eye = (iota((frames, frames), 0) == iota((frames, frames), 1)).astype(BF16)
-    dims = (((1,), (1,)), ((), ()))
-    owner_cols = lax.dot_general(eye, owners.astype(BF16), dims, preferred_element_type=F32)
-    rank_cols = lax.dot_general(eye, ranks.astype(BF16), dims, preferred_element_type=F32)
-    lane = iota((frames, facts_ref.shape[1]), 1)
+    owner, rank, *valid = [
+        lax.dot_general(
+            eye, lines.astype(BF16), (((1,), (1,)), ((), ())), preferred_element_type=F32
+        )
+        for lines in rows_of
+    ]
+    lane = iota((frames, taps), 1)
     for block in range(count):
-        owner = owner_cols[:, block : block + 1].astype(jnp.int32)
-        rank = rank_cols[:, block : block + 1].astype(jnp.int32)
-        slot = jnp.bitwise_xor(owner, me) * rows + block * capacity + rank
-        position = block * frames + iota((frames, 1), 0)
-        facts = slot
-        for tap in range(1, facts_ref.shape[1]):
-            later = position + tap
-            valid = (later < count * frames) & (position >= start_below(later, lengths_ref))
-            facts = jnp.where(lane == tap, valid.astype(jnp.int32), facts)
-        facts_ref[block * frames : (block + 1) * frames, :] = facts
-
-
-def spread_kernel(count, frames, taps, *refs):
-    backs = refs[:count]
-    facts_ref, turned_ref, send_ref, windows_ref, gain_ref, gathered, wide = refs[count:]
+        here = slice(block, block + 1)
+        facts = owner[:, here] * rows + (rank[:, here] + block * capacity)
+        for tap in range(1, taps):
+            facts = jnp.where(lane == tap, valid[tap - 1][:, here], facts)
+        facts_ref[block * frames : (block + 1) * frames, :] = facts.astype(jnp.int32)
+
+
+def spread_kernel(orders, count, frames, taps, *refs):
+    backs, turned_refs = refs[:count], refs[count : count + len(orders)]
+    facts_ref, send_ref, windows_ref, gain_ref, gathered, wide, lhs = refs[count + len(orders) :]
     rows, latent_width = backs[0].shape
-    share = turned_ref.shape[0] // 4
+    share = turned_refs[0].shape[1] // 4
     gain_rows = gain_ref.shape[0]
-    book = lax.axis_index("book")
     gain = jnp.zeros((gain_rows, latent_width), F32)
     for rel, back_ref in enumerate(backs):
         gathered[rel * rows : (rel + 1) * rows, :] = back_ref[...]
@@ -357,7 +390,7 @@
             later = wide[block * frames + tap : (block + 1) * frames + tap, :]
             later = jnp.where(facts_ref[here, tap : tap + 1] > 0, later, 0.0)
             windows_ref[here, tap * latent_width : (tap + 1) * latent_width] = later.astype(BF16)
-    part = kernel_part(turned_ref, windows_ref, book, share, 1)
+    part = kernel_part(orders, turned_refs, windows_ref, lhs, share, 1)
     for y in (0, 1):
         for tap in range(taps):
             at = (y * taps + tap) * share
@@ -371,19 +404,24 @@
     ).astype(BF16)
 
 
-def kernel_part(turned_ref, windows_ref, book, share, core):
-    blocks = []
-    for y in (0, 1):
-        at = jnp.bitwise_xor(book, 2 * y + core) * share
-        blocks.append(turned_ref[pl.ds(pl.multiple_of(at, share), share), :])
-    return jnp.dot(
-        jnp.concatenate(blocks, axis=0), windows_ref[...], preferred_element_type=F32
-    )
-
-
-def own_part_kernel(taps, turned_ref, windows_ref, out_ref):
-    share, latent_width = turned_ref.shape[0] // 4, out_ref.shape[1]
-    part = kernel_part(turned_ref, windows_ref, lax.axis_index("book"), share, 0)
+def kernel_part(orders, turned_refs, windows_ref, lhs, share, core):
+    seq, book = lax.axis_index("seq"), lax.axis_index("book")
+    for turned_ref, order in zip(turned_refs, orders):
+        frames = turned_ref.shape[2]
+        for index, rel in enumerate(order):
+            lanes = pl.ds(pl.multiple_of(jnp.bitwise_xor(seq, rel) * frames, frames), frames)
+            for y in (0, 1):
+                at = jnp.bitwise_xor(book, 2 * y + core) * share
+                lhs[y * share : (y + 1) * share, lanes] = turned_ref[
+                    index, pl.ds(pl.multiple_of(at, share), share), :
+                ]
+    return jnp.dot(lhs[...], windows_ref[...], preferred_element_type=F32)
+
+
+def own_part_kernel(orders, taps, *refs):
+    turned_refs, (windows_ref, out_ref, lhs) = refs[: len(orders)], refs[len(orders) :]
+    share, latent_width = turned_refs[0].shape[1] // 4, out_ref.shape[1]
+    part = kernel_part(orders, turned_refs, windows_ref, lhs, share, 0)
     for y in (0, 1):
         for tap in range(taps):
             at = (y * taps + tap) * share
@@ -405,6 +443,29 @@
     send_ref[half : half + 2 * gain_rows, :] = jnp.concatenate(
         [high, gain - high], axis=0
     ).astype(BF16)
+
+
+def finish_kernel(mine_ref, got_ref, gain_ref, send_ref, out_ref, gain_out_ref):
+    half, gain_rows = mine_ref.shape[0], gain_ref.shape[0]
+    total = mine_ref[...] + got_ref[0:half, :].astype(F32)
+    out_ref[...] = total
+    send_ref[...] = total.astype(BF16)
+    pair = got_ref[half : half + 2 * gain_rows, :].astype(F32)
+    gain = gain_ref[...] + (pair[:gain_rows] + pair[gain_rows:])
+    step = gain.shape[1]
+    for line in range(gain_rows):
+        gain_out_ref[:, line * step : (line + 1) * step] = gain[line : line + 1]
+
+
+def join_kernel(mine_ref, got_ref, out_ref):
+    taps, share = out_ref.shape[:2]
+    half = share // 2
+    near = jnp.bitwise_and(lax.axis_index("seq"), 1)
+    for tap in range(taps):
+        here = slice(tap * half, (tap + 1) * half)
+        mine, got = mine_ref[here, :], got_ref[here, :].astype(F32)
+        out_ref[tap, 0:half, :] = jnp.where(near == 0, mine, got)
+        out_ref[tap, half:, :] = jnp.where(near == 0, got, mine)
 
 
 def feature_kernel(feat_ref, windows_ref, w_ref, out_ref):
@@ -425,7 +486,6 @@
 
 
 def call(kernel, outs, operands, scratch=(), smem=0, flops=0):
-    moved = sum(x.size * x.dtype.itemsize for x in (*outs, *operands))
     return pl.pallas_call(
         kernel,
         out_shape=outs,
@@ -433,7 +493,7 @@
         out_specs=jax.tree.map(lambda _: VMEM, outs),
         scratch_shapes=list(scratch),
         compiler_params=pltpu.CompilerParams(vmem_limit_bytes=24 * 2**20),
-        cost_estimate=pl.CostEstimate(flops=flops, bytes_accessed=moved, transcendentals=0),
+        cost_estimate=pl.CostEstimate(flops=flops, bytes_accessed=1024, transcendentals=0),
     )(*operands)
 
 
@@ -455,30 +515,69 @@
     piece = round_up(capacity + 1, 16)
     gain_rows = width // latent_width
     rows = round_up(slots + gain_rows, 16)
-    share = channels // 4
-
-    edge = shifted(feats[frames - 16 :], "seq", 1)
-    w_own = w_in.T
+    half = channels // 8
+
+    columns = w_in.shape[1]
+    padded, mine, other = call(
+        activate_kernel,
+        [
+            shape((24 + frames, channels), F32),
+            shape((channels // 2, frames)),
+            shape((channels // 2, frames)),
+        ],
+        (feats,),
+        scratch=[pltpu.VMEM((channels, frames), F32)],
+        flops=HEAVY // 10,
+    )
+    total, placed, edge, named = call(
+        functools.partial(encode_kernel, piece),
+        [
+            shape((frames, latent_width), F32),
+            shape((count * piece, frames)),
+            shape((8, latent_width), F32),
+            shape((1, latent_width), F32),
+        ],
+        (book_lengths, padded, owner[0].T, w_enc),
+        smem=1,
+    )
+    w_own, edge, other = lax.optimization_barrier((w_in.T, edge, other))
+    edge = shifted(edge, "seq", 1)
     w_far = [w_own] + [swap(w_own, "seq", 2 * far) for far in fars]
-    w_line = jnp.stack(w_far)
+    held = jnp.stack([mine, swap(other, "seq", 1)])
+    sent = call(
+        functools.partial(place_kernel, piece),
+        [shape((2 * piece, latent_width))] * far_count,
+        (total, edge, placed, named),
+    )
+    w_far, held, sent = lax.optimization_barrier((w_far, held, sent))
+    landed = [sent[0]] + [swap(sent[far], "seq", 2 * far) for far in fars]
+    (w_line,) = call(
+        functools.partial(join_rows_kernel, 0),
+        [shape((far_count * columns, latent_width))],
+        tuple(w_far),
+        flops=HEAVY,
+    )
     w_near = swap(w_line, "seq", 1)
     w_side = swap(w_line, "book", 2)
     w_diag = swap(w_line, ("seq", "book"), 4 + 2)
+    got = swap(held, "seq", 4)
+    (near,) = call(
+        functools.partial(join_rows_kernel, piece),
+        [shape((far_count * piece, latent_width))],
+        tuple(landed),
+        flops=HEAVY,
+    )
+    near = swap(near, "seq", 1)
     w_chips = [w_line, w_near, w_side, w_diag]
+    w_chips, got = lax.optimization_barrier((w_chips, got))
+    held = jnp.concatenate([held, got])
     w_pieces = w_chips + [swap(block, "book", 1) for block in w_chips]
-
-    sent = call(
-        functools.partial(encode_kernel, piece, capacity),
-        [shape((2 * piece, latent_width))] * far_count,
-        (book_lengths, feats, edge, owner[0].T, w_enc),
-        scratch=[pltpu.VMEM((8 + frames, channels), F32)],
-        smem=1,
-    )
-    landed = [sent[0]] + [swap(sent[far], "seq", 2 * far) for far in fars]
-    near = swap(jnp.concatenate([block[piece:] for block in landed]), "seq", 1)
+    second = swap(held, "seq", 2)
+    turned_all = [held, second]
+    orders = [[0, 1, 4, 5], [2, 3, 6, 7]]
 
     back, hidden_grad, arrived, owners = call(
-        functools.partial(middle_kernel, piece, capacity, frames, count),
+        functools.partial(middle_kernel, piece, capacity, frames, count, columns),
         [
             shape((rows, latent_width)),
             shape((rows, width)),
@@ -492,77 +591,87 @@
             pltpu.VMEM((slots, width), F32),
             pltpu.VMEM((rows, latent_width), F32),
         ],
+        flops=HEAVY,
     )
     backs = [back] + [swap(back, "seq", rel) for rel in range(1, count)]
 
-    gathered, orders, mask, held, order = [feats], [[0]], far_count, feats, [0]
-    while mask:
-        got = swap(held, "seq", mask)
-        gathered.append(got)
-        orders.append([rel ^ mask for rel in order])
-        order = order + orders[-1]
-        mask //= 2
-        if mask:
-            held = jnp.concatenate([held, got])
-
+    (facts,) = call(
+        functools.partial(prepare_kernel, capacity, rows),
+        [shape((count * frames, taps), jnp.int32)],
+        (book_lengths, owners),
+        smem=1,
+        flops=HEAVY,
+    )
     w_send, w_keep = call(
         functools.partial(projection_kernel, count),
-        [shape((2 * count, w_in.shape[1], latent_width))] * 2,
+        [shape((2 * count, columns, latent_width))] * 2,
         (hidden_grad, arrived),
     )
-    w_sum = w_keep.astype(F32) + swap(w_send, "book", 1).astype(F32)
+    w_got, facts = lax.optimization_barrier((swap(w_send, "book", 1), facts))
+    w_sum = w_keep.astype(F32) + w_got.astype(F32)
     w_sum = w_sum[:count] + swap(w_sum[count:].astype(BF16), "book", 2).astype(F32)
     w_sum = w_sum[:far_count] + swap(w_sum[far_count:].astype(BF16), "seq", 1).astype(F32)
     w_total = w_sum[0]
     for far in fars:
         w_total = w_total + swap(w_sum[far].astype(BF16), "seq", 2 * far).astype(F32)
 
-    turned, facts = call(
-        functools.partial(prepare_kernel, capacity, rows, orders),
-        [shape((channels, count * frames)), shape((count * frames, taps), jnp.int32)],
-        (book_lengths, owners, *gathered),
-        smem=1,
-    )
-    message = 2 * taps * share + 2 * gain_rows
+    message = 2 * taps * half + 2 * gain_rows
     k_send, windows, gain_seq = call(
-        functools.partial(spread_kernel, count, frames, taps),
+        functools.partial(spread_kernel, orders, count, frames, taps),
         [
             shape((message, latent_width)),
             shape((count * frames, taps * latent_width)),
             shape((gain_rows, latent_width), F32),
         ],
-        (*backs, facts, turned),
+        (*backs, *turned_all, facts),
         scratch=[
             pltpu.VMEM((count * rows, latent_width), BF16),
             pltpu.VMEM((count * frames + 8, latent_width), F32),
-        ],
+            pltpu.VMEM((2 * half, count * frames), BF16),
+        ],
+        flops=HEAVY,
     )
     k_got = swap(k_send, "book", 1)
     (k_kept,) = call(
-        functools.partial(own_part_kernel, taps),
-        [shape((2 * taps * share, latent_width), F32)],
-        (turned, windows),
+        functools.partial(own_part_kernel, orders, taps),
+        [shape((2 * taps * half, latent_width), F32)],
+        (*turned_all, windows),
+        scratch=[pltpu.VMEM((2 * half, count * frames), BF16)],
+        flops=HEAVY,
     )
     y_send, k_mine, gain_pair = call(
         fold_kernel,
         [
-            shape((taps * share + 2 * gain_rows, latent_width)),
-            shape((taps * share, latent_width), F32),
+            shape((taps * half + 2 * gain_rows, latent_width)),
+            shape((taps * half, latent_width), F32),
             shape((gain_rows, latent_width), F32),
         ],
         (k_kept, k_got, gain_seq),
     )
     y_got = swap(y_send, "book", 2)
-    (feature_grad,) = call(feature_kernel, [shape(feats.shape)], (feats, windows, w_enc))
-    y_wide = y_got.astype(F32)
-    kernel_mine = k_mine + y_wide[: taps * share]
-    tail = y_wide[taps * share :]
-    gain_total = (gain_pair + (tail[:gain_rows] + tail[gain_rows:])).reshape(width)
+    (feature_grad,) = call(
+        feature_kernel, [shape(feats.shape)], (feats, windows, w_enc), flops=HEAVY
+    )
+    y_got, feature_grad = lax.optimization_barrier((y_got, feature_grad))
+    x_back, kernel_half, gain_total = call(
+        finish_kernel,
+        [
+            shape((taps * half, latent_width)),
+            shape((taps * half, latent_width), F32),
+            shape((1, width), F32),
+        ],
+        (k_mine, y_got, gain_pair),
+    )
+    (kernel_mine,) = call(
+        join_kernel,
+        [shape((taps, 2 * half, latent_width), F32)],
+        (kernel_half, swap(x_back, "seq", 1)),
+    )
     return (
         feature_grad[None],
-        kernel_mine.reshape(taps, share, latent_width),
+        kernel_mine,
         w_total.T,
-        gain_total,
+        gain_total[0],
     )
 
 

time: 102 us -> 77.5 us (0.76)
  waiting for transfers between devices: 42.9 us -> 22.3 us
  local copies, waits for them, and re-layouts: 5.99 us -> 1.81 us
  starting transfers between devices: 39.1 us -> 42.6 us
  other arithmetic: 2.56 us -> 0.9 us
    ppermute x32 -> x33, waiting for transfers between devices: 41.4 us -> 22.3 us  [swap(): lax.ppermute(block, axis, [(i, i ^ mask) for i in range(lax.axis_size(axi...]
    ppermute x32 -> x33, starting transfers between devices: 35.7 us -> 40.6 us  [swap(): lax.ppermute(block, axis, [(i, i ^ mask) for i in range(lax.axis_size(axi...]
    unnamed x19 -> x17, local copies, waits for them, and re-layouts: 5.21 us -> 1.74 us
    ppermute x1, starting transfers between devices: 3.38 us -> 1.92 us  [shifted(): return lax.ppermute(block, axis, route)]
    ppermute x1, waiting for transfers between devices: 1.43 us -> 0.01 us  [shifted(): return lax.ppermute(block, axis, route)]
    pallas_call x8 -> x14, Pallas kernels: 9.9 us -> 8.92 us  [call(): pl.pallas_call(kernel, out_shape=outs, in_specs=[SMEM] * smem + [VMEM] *...]
  transfers between devices with their start and end apart: 33 -> 34, of which waited for: 16 -> 15; matrix products, arithmetic and copies ran while one was open for 2% -> 0% of each run, Pallas kernels for 8% -> 10%
where the time goes in v2:
time: 77.5 us; the launch traced here: 77.3 us
  starting transfers between devices  42.6 us (55%)
  waiting for transfers between devices  22.3 us (29%)
  Pallas kernels  8.92 us (12%)
  local copies, waits for them, and re-layouts  1.81 us (2%)
  other arithmetic  0.9 us (1%)
  between operations  0.89 us (1%)
    ppermute x33, starting transfers between devices, swap(): lax.ppermute(block, axis, [(i, i ^ mask) for i in range(lax.axis_size(axi...  40.6 us
    ppermute x33, waiting for transfers between devices, swap(): lax.ppermute(block, axis, [(i, i ^ mask) for i in range(lax.axis_size(axi...  22.3 us
    pallas_call x14, Pallas kernels, call(): pl.pallas_call(kernel, out_shape=outs, in_specs=[SMEM] * smem + [VMEM] *...  8.92 us
    ppermute x1, starting transfers between devices, shifted(): return lax.ppermute(block, axis, route)  1.92 us
    unnamed x17, local copies, waits for them, and re-layouts  1.74 us
  transfers between devices with their start and end apart: 34, of which 15 were waited for; matrix products, arithmetic and copies ran while one was open for 0% of the time, Pallas kernels for 10%

profile of v2, /device:TPU:0, one launch (start us, length us, event | category | flops | bytes accessed | tf_op | source)
XLA Modules:
  0.0 77.3 jit_solution(3602171269694278411)
XLA Ops:
  0.6 0.9 %copy-done.4 = bf16[1,128,512]{2,1,0:T(8,128)(2,1)S(1)} copy-done((bf16[1,128,512]{2,1,0:T(8,128)(2,1)S(1)}, bf16[1,128,512]{2,1,0:T(8,128)(2,1)}, u32[]{:S(2)}) %copy-start.4) | copy-done | bytes 131096
  1.6 0.3 shard_map.102
  1.9 0.8 %copy-done = bf16[3,512,256]{2,1,0:T(8,128)(2,1)S(1)} copy-done((bf16[3,512,256]{2,1,0:T(8,128)(2,1)S(1)}, bf16[3,512,256]{2,1,0:T(8,128)(2,1)}, u32[]{:S(2)}) %copy-start) | copy-done | bytes 786456
  2.7 0.9 %shard_map.103 = (f32[128,256]{1,0:T(8,128)S(1)}, bf16[256,128]{1,0:T(8,128)(2,1)S(1)}, f32[8,256]{1,0:T(8,128)S(1)}, f32[1,256]{1,0:T(1,128)S(1)}) custom-call(s32[8]{0:T(128)S(1)} %bitcast.30, f32[152,512]{1,0:T(8,128)S(1)} %get-tuple-element.51.padded, s32[1,128]{1,0:T(1,128)S(1)} %bitcast.29, bf16[3,512,256]{2,1,0:T(8,128)(2,1)S(1)} %copy-done), custom_call_target="tpu_custom_call" | custom-call | bytes 1024 | tf_op jit(solution)/shard_map/pallas_call | solution.py:489
  3.6 3.0 %collective-permute-start.3 = (bf16[256,128]{1,0:T(8,128)(2,1)S(1)}, bf16[256,128]{1,0:T(8,128)(2,1)S(1)}, u32[]{:S(2)}, u32[]{:S(2)}) collective-permute-start(bf16[256,128]{1,0:T(8,128)(2,1)S(1)} %get-tuple-element.56), channel_id=1, source_target_pairs={{0,4},{4,0},{8,12},{12,8},{16,20},{20,16},{24,28},{28,24},{1,5},{5... | collective-permute-start | bytes 196616 | tf_op jit(solution)/shard_map/ppermute | solution.py:144
  6.6 1.9 %collective-permute-start.4 = (f32[8,256]{1,0:T(8,128)S(1)}, f32[8,256]{1,0:T(8,128)S(1)}, u32[]{:S(2)}, u32[]{:S(2)}) collective-permute-start(f32[8,256]{1,0:T(8,128)S(1)} %get-tuple-element.58), channel_id=1, source_target_pairs={{0,4},{4,8},{8,12},{12,16},{16,20},{20,24},{24,28},{1,5},{5,9},{9,... | collective-permute-start | bytes 24584 | tf_op jit(solution)/shard_map/ppermute | solution.py:20
  8.5 2.2 %collective-permute-start = (bf16[64,256]{1,0:T(8,128)(2,1)S(1)}, bf16[64,256]{1,0:T(8,128)(2,1)S(1)}, u32[]{:S(2)}, u32[]{:S(2)}) collective-permute-start(bf16[64,256]{1,0:T(8,128)(2,1)S(1)} %bitcast.35), channel_id=1, source_target_pairs={{0,8},{4,12},{8,0},{12,4},{16,24},{20,28},{24,16},{28,20},{1,9},{5... | collective-permute-start | bytes 98312 | tf_op jit(solution)/shard_map/ppermute | solution.py:144
  10.7 2.6 %collective-permute-start.1 = (bf16[64,256]{1,0:T(8,128)(2,1)S(1)}, bf16[64,256]{1,0:T(8,128)(2,1)S(1)}, u32[]{:S(2)}, u32[]{:S(2)}) collective-permute-start(bf16[64,256]{1,0:T(8,128)(2,1)S(1)} %bitcast.36), channel_id=1, source_target_pairs={{0,16},{4,20},{8,24},{12,28},{16,0},{20,4},{24,8},{28,12},{1,17},{... | collective-permute-start | bytes 98312 | tf_op jit(solution)/shard_map/ppermute | solution.py:144
  13.3 0.2 shard_map.104
  13.5 2.2 %collective-permute-done.1.refs_2_ = bf16[64,256]{1,0:T(8,128)(2,1)S(1)} collective-permute-done((bf16[64,256]{1,0:T(8,128)(2,1)S(1)}, bf16[64,256]{1,0:T(8,128)(2,1)S(1)}, u32[]{:S(2)}, u32[]{:S(2)}) %collective-permute-start.1) | collective-permute-done | bytes 32800 | tf_op jit(solution)/shard_map/ppermute | solution.py:144
  15.7 3.2 %collective-permute-done.2.refs_3_ = bf16[64,256]{1,0:T(8,128)(2,1)S(1)} collective-permute-done((bf16[64,256]{1,0:T(8,128)(2,1)S(1)}, bf16[64,256]{1,0:T(8,128)(2,1)S(1)}, u32[]{:S(2)}, u32[]{:S(2)}) %collective-permute-start.2) | collective-permute-done | bytes 32800 | tf_op jit(solution)/shard_map/ppermute | solution.py:144
  19.0 1.1 %collective-permute-start.5 = (bf16[256,256]{1,0:T(8,128)(2,1)S(1)}, bf16[256,256]{1,0:T(8,128)(2,1)S(1)}, u32[]{:S(2)}, u32[]{:S(2)}) collective-permute-start(bf16[256,256]{1,0:T(8,128)(2,1)S(1)} %shard_map.105.refs_5_), channel_id=1, source_target_pairs={{0,4},{4,0},{8,12},{12,8},{16,20},{20,16},{24,28},{28,24},{1,5},{5... | collective-permute-start | bytes 393224 | tf_op jit(solution)/shard_map/ppermute | solution.py:144
  20.1 1.5 %collective-permute-start.6 = (bf16[256,256]{1,0:T(8,128)(2,1)S(1)}, bf16[256,256]{1,0:T(8,128)(2,1)S(1)}, u32[]{:S(2)}, u32[]{:S(2)}) collective-permute-start(bf16[256,256]{1,0:T(8,128)(2,1)S(1)} %shard_map.105.refs_5_), channel_id=1, source_target_pairs={{0,2},{1,3},{2,0},{3,1},{4,6},{5,7},{6,4},{7,5},{8,10},{9,11},{10,... | collective-permute-start | bytes 393224 | tf_op jit(solution)/shard_map/ppermute | solution.py:144
  21.6 1.0 %collective-permute-start.7 = (bf16[256,256]{1,0:T(8,128)(2,1)S(1)}, bf16[256,256]{1,0:T(8,128)(2,1)S(1)}, u32[]{:S(2)}, u32[]{:S(2)}) collective-permute-start(bf16[256,256]{1,0:T(8,128)(2,1)S(1)} %shard_map.105.refs_5_), channel_id=1, source_target_pairs={{0,6},{1,7},{2,4},{3,5},{4,2},{5,3},{6,0},{7,1},{8,14},{9,15},{10,... | collective-permute-start | bytes 393224 | tf_op jit(solution)/shard_map/ppermute | solution.py:144
  22.6 1.3 %collective-permute-start.10 = (bf16[64,256]{1,0:T(8,128)(2,1)S(1)}, bf16[64,256]{1,0:T(8,128)(2,1)S(1)}, u32[]{:S(2)}, u32[]{:S(2)}) collective-permute-start(bf16[64,256]{1,0:T(8,128)(2,1)S(1)} %get-tuple-element.72), channel_id=1, source_target_pairs={{0,8},{4,12},{8,0},{12,4},{16,24},{20,28},{24,16},{28,20},{1,9},{5... | collective-permute-start | bytes 98312 | tf_op jit(solution)/shard_map/ppermute | solution.py:144
  23.9 0.6 collective-permute-done.5.refs_6_
  24.5 1.0 %collective-permute-start.11 = (bf16[64,256]{1,0:T(8,128)(2,1)S(1)}, bf16[64,256]{1,0:T(8,128)(2,1)S(1)}, u32[]{:S(2)}, u32[]{:S(2)}) collective-permute-start(bf16[64,256]{1,0:T(8,128)(2,1)S(1)} %get-tuple-element.73), channel_id=1, source_target_pairs={{0,16},{4,20},{8,24},{12,28},{16,0},{20,4},{24,8},{28,12},{1,17},{... | collective-permute-start | bytes 98312 | tf_op jit(solution)/shard_map/ppermute | solution.py:144
  25.5 0.0 collective-permute-done.6.refs_7_
  25.5 1.7 %collective-permute-start.12 = (bf16[64,256]{1,0:T(8,128)(2,1)S(1)}, bf16[64,256]{1,0:T(8,128)(2,1)S(1)}, u32[]{:S(2)}, u32[]{:S(2)}) collective-permute-start(bf16[64,256]{1,0:T(8,128)(2,1)S(1)} %get-tuple-element.74), channel_id=1, source_target_pairs={{0,24},{4,28},{8,16},{12,20},{16,8},{20,12},{24,0},{28,4},{1,25},{... | collective-permute-start | bytes 98312 | tf_op jit(solution)/shard_map/ppermute | solution.py:144
  27.2 0.0 copy-start.3
  27.2 0.0 copy-start.7
  27.2 0.2 collective-permute-done.7.refs_8_
  27.5 1.8 %collective-permute-done.8 = bf16[2,256,128]{2,1,0:T(8,128)(2,1)S(1)} collective-permute-done((bf16[2,256,128]{2,1,0:T(8,128)(2,1)S(1)}, bf16[2,256,128]{2,1,0:T(8,128)(2,1)S(1)}, u32[]{:S(2)}, u32[]{:S(2)}) %collective-permute-start.8) | collective-permute-done | bytes 131104 | tf_op jit(solution)/shard_map/ppermute | solution.py:144
  29.3 0.5 collective-permute-start.15
  29.8 0.5 collective-permute-start.17
  30.3 0.9 %collective-permute-done.12.refs_3_ = bf16[64,256]{1,0:T(8,128)(2,1)S(1)} collective-permute-done((bf16[64,256]{1,0:T(8,128)(2,1)S(1)}, bf16[64,256]{1,0:T(8,128)(2,1)S(1)}, u32[]{:S(2)}, u32[]{:S(2)}) %collective-permute-start.12) | collective-permute-done | bytes 32800 | tf_op jit(solution)/shard_map/ppermute | solution.py:144
  31.2 1.1 %collective-permute-start.13 = (bf16[128,256]{1,0:T(8,128)(2,1)S(1)}, bf16[128,256]{1,0:T(8,128)(2,1)S(1)}, u32[]{:S(2)}, u32[]{:S(2)}) collective-permute-start(bf16[128,256]{1,0:T(8,128)(2,1)S(1)} %shard_map.106), channel_id=1, source_target_pairs={{0,4},{4,0},{8,12},{12,8},{16,20},{20,16},{24,28},{28,24},{1,5},{5... | collective-permute-start | bytes 196616 | tf_op jit(solution)/shard_map/ppermute | solution.py:144
  32.4 3.1 %collective-permute-done.13.refs_4_ = bf16[128,256]{1,0:T(8,128)(2,1)S(1)} collective-permute-done((bf16[128,256]{1,0:T(8,128)(2,1)S(1)}, bf16[128,256]{1,0:T(8,128)(2,1)S(1)}, u32[]{:S(2)}, u32[]{:S(2)}) %collective-permute-start.13) | collective-permute-done | bytes 65568 | tf_op jit(solution)/shard_map/ppermute | solution.py:144
  35.5 0.2 collective-permute-start.9
  35.7 1.2 %shard_map.107 = (bf16[144,256]{1,0:T(8,128)(2,1)S(1)}, bf16[144,2048]{1,0:T(8,128)(2,1)S(1)}, bf16[144,256]{1,0:T(8,128)(2,1)S(1)}, f32[8,128]{1,0:T(8,128)S(1)}) custom-call(bf16[64,256]{1,0:T(8,128)(2,1)S(1)} %get-tuple-element.71.refs_0_, bf16[64,256]{1,0:T(8,128)(2,1)S(1)} %collective-permute-done.10.refs_1_, ...), custom_call_target="tpu_custom_call" | custom-call | flops 20000000000 | bytes 1024 | tf_op jit(solution)/shard_map/pallas_call | solution.py:489
  37.0 1.1 %collective-permute-start.18 = (bf16[144,256]{1,0:T(8,128)(2,1)S(1)}, bf16[144,256]{1,0:T(8,128)(2,1)S(1)}, u32[]{:S(2)}, u32[]{:S(2)}) collective-permute-start(bf16[144,256]{1,0:T(8,128)(2,1)S(1)} %get-tuple-element.79.refs_0_), channel_id=1, source_target_pairs={{0,4},{4,0},{8,12},{12,8},{16,20},{20,16},{24,28},{28,24},{1,5},{5... | collective-permute-start | bytes 221192 | tf_op jit(solution)/shard_map/ppermute | solution.py:144
  38.1 1.9 %collective-permute-start.19 = (bf16[144,256]{1,0:T(8,128)(2,1)S(1)}, bf16[144,256]{1,0:T(8,128)(2,1)S(1)}, u32[]{:S(2)}, u32[]{:S(2)}) collective-permute-start(bf16[144,256]{1,0:T(8,128)(2,1)S(1)} %get-tuple-element.79.refs_0_), channel_id=1, source_target_pairs={{0,8},{4,12},{8,0},{12,4},{16,24},{20,28},{24,16},{28,20},{1,9},{5... | collective-permute-start | bytes 221192 | tf_op jit(solution)/shard_map/ppermute | solution.py:144
  40.0 0.5 collective-permute-start.20
  40.5 0.5 shard_map.108
  41.1 0.1 collective-permute-start.25
  41.1 1.3 %shard_map.109.refs_10_ = s32[1024,3]{1,0:T(8,128)S(1)} custom-call(s32[8]{0:T(128)S(1)} %bitcast.31, f32[8,128]{1,0:T(8,128)S(1)} %get-tuple-element.83.owners_ref), custom_call_target="tpu_custom_call" | custom-call | flops 20000000000 | bytes 1024 | tf_op jit(solution)/shard_map/pallas_call | solution.py:489
  42.4 0.6 collective-permute-done.25
  43.0 2.0 %collective-permute-start.21 = (bf16[144,256]{1,0:T(8,128)(2,1)S(1)}, bf16[144,256]{1,0:T(8,128)(2,1)S(1)}, u32[]{:S(2)}, u32[]{:S(2)}) collective-permute-start(bf16[144,256]{1,0:T(8,128)(2,1)S(1)} %get-tuple-element.79.refs_0_), channel_id=1, source_target_pairs={{0,16},{4,20},{8,24},{12,28},{16,0},{20,4},{24,8},{28,12},{1,17},{... | collective-permute-start | bytes 221192 | tf_op jit(solution)/shard_map/ppermute | solution.py:144
  45.1 1.3 %collective-permute-start.22 = (bf16[144,256]{1,0:T(8,128)(2,1)S(1)}, bf16[144,256]{1,0:T(8,128)(2,1)S(1)}, u32[]{:S(2)}, u32[]{:S(2)}) collective-permute-start(bf16[144,256]{1,0:T(8,128)(2,1)S(1)} %get-tuple-element.79.refs_0_), channel_id=1, source_target_pairs={{0,20},{4,16},{8,28},{12,24},{16,4},{20,0},{24,12},{28,8},{1,21},{... | collective-permute-start | bytes 221192 | tf_op jit(solution)/shard_map/ppermute | solution.py:144
  46.4 1.7 %collective-permute-start.23 = (bf16[144,256]{1,0:T(8,128)(2,1)S(1)}, bf16[144,256]{1,0:T(8,128)(2,1)S(1)}, u32[]{:S(2)}, u32[]{:S(2)}) collective-permute-start(bf16[144,256]{1,0:T(8,128)(2,1)S(1)} %get-tuple-element.79.refs_0_), channel_id=1, source_target_pairs={{0,24},{4,28},{8,16},{12,20},{16,8},{20,12},{24,0},{28,4},{1,25},{... | collective-permute-start | bytes 221192 | tf_op jit(solution)/shard_map/ppermute | solution.py:144
  48.2 2.5 %collective-permute-start.24 = (bf16[144,256]{1,0:T(8,128)(2,1)S(1)}, bf16[144,256]{1,0:T(8,128)(2,1)S(1)}, u32[]{:S(2)}, u32[]{:S(2)}) collective-permute-start(bf16[144,256]{1,0:T(8,128)(2,1)S(1)} %get-tuple-element.79.refs_0_), channel_id=1, source_target_pairs={{0,28},{4,24},{8,20},{12,16},{16,12},{20,8},{24,4},{28,0},{1,29},{... | collective-permute-start | bytes 221192 | tf_op jit(solution)/shard_map/ppermute | solution.py:144
  50.7 0.1 convert_add_fusion
  50.9 3.9 %collective-permute-done.21.refs_4_ = bf16[144,256]{1,0:T(8,128)(2,1)S(1)} collective-permute-done((bf16[144,256]{1,0:T(8,128)(2,1)S(1)}, bf16[144,256]{1,0:T(8,128)(2,1)S(1)}, u32[]{:S(2)}, u32[]{:S(2)}) %collective-permute-start.21) | collective-permute-done | bytes 73760 | tf_op jit(solution)/shard_map/ppermute | solution.py:144
  54.8 1.5 %collective-permute-start.29 = (bf16[8,64,256]{2,1,0:T(8,128)(2,1)S(1)}, bf16[8,64,256]{2,1,0:T(8,128)(2,1)S(1)}, u32[]{:S(2)}, u32[]{:S(2)}) collective-permute-start(bf16[8,64,256]{2,1,0:T(8,128)(2,1)S(1)} %slice.61), channel_id=1, source_target_pairs={{0,2},{1,3},{2,0},{3,1},{4,6},{5,7},{6,4},{7,5},{8,10},{9,11},{10,... | collective-permute-start | bytes 786440 | tf_op jit(solution)/shard_map/ppermute | solution.py:144
  56.4 0.3 collective-permute-done.22.refs_5_
  56.7 1.6 %shard_map.110 = (bf16[400,256]{1,0:T(8,128)(2,1)S(1)}, bf16[1024,768]{1,0:T(8,128)(2,1)S(1)}, f32[8,256]{1,0:T(8,128)S(1)}) custom-call(bf16[144,256]{1,0:T(8,128)(2,1)S(1)} %get-tuple-element.79.refs_0_, bf16[144,256]{1,0:T(8,128)(2,1)S(1)} %collective-permute-done.18.refs_1_, bf16[144,256]{1,0:T(8,128)(2,1)S(1)} %collective-permute-done.19.refs_2_, ...), custom_call_target="tpu_custom_call" | custom-call | flops 20000000000 | bytes 1024 | tf_op jit(solution)/shard_map/pallas_call | solution.py:489
  58.3 0.1 collective-permute-start.26
  58.4 0.4 shard_map.111.kept_ref
  58.8 1.0 %collective-permute-done.26.got_ref = bf16[400,256]{1,0:T(8,128)(2,1)S(1)} collective-permute-done((bf16[400,256]{1,0:T(8,128)(2,1)S(1)}, bf16[400,256]{1,0:T(8,128)(2,1)S(1)}, u32[]{:S(2)}, u32[]{:S(2)}) %collective-permute-start.26) | collective-permute-done | bytes 204832 | tf_op jit(solution)/shard_map/ppermute | solution.py:144
  59.9 1.6 %collective-permute-start.27 = (bf16[208,256]{1,0:T(8,128)(2,1)S(1)}, bf16[208,256]{1,0:T(8,128)(2,1)S(1)}, u32[]{:S(2)}, u32[]{:S(2)}) collective-permute-start(bf16[208,256]{1,0:T(8,128)(2,1)S(1)} %get-tuple-element.88), channel_id=1, source_target_pairs={{0,2},{1,3},{2,0},{3,1},{4,6},{5,7},{6,4},{7,5},{8,10},{9,11},{10,... | collective-permute-start | bytes 319496 | tf_op jit(solution)/shard_map/ppermute | solution.py:144
  61.5 0.1 slice_add_fusion
  61.6 1.2 %collective-permute-start.30 = (bf16[4,64,256]{2,1,0:T(8,128)(2,1)S(1)}, bf16[4,64,256]{2,1,0:T(8,128)(2,1)S(1)}, u32[]{:S(2)}, u32[]{:S(2)}) collective-permute-start(bf16[4,64,256]{2,1,0:T(8,128)(2,1)S(1)} %slice.62), channel_id=1, source_target_pairs={{0,4},{4,0},{8,12},{12,8},{16,20},{20,16},{24,28},{28,24},{1,5},{5... | collective-permute-start | bytes 393224 | tf_op jit(solution)/shard_map/ppermute | solution.py:144
  62.8 1.1 %shard_map.113 = bf16[128,512]{1,0:T(8,128)(2,1)} custom-call(bf16[128,512]{1,0:T(8,128)(2,1)S(1)} %bitcast.34, bf16[1024,768]{1,0:T(8,128)(2,1)S(1)} %get-tuple-element.85.refs_2_.windows_ref, bf16[3,512,256]{2,1,0:T(8,128)(2,1)S(1)} %copy-done), custom_call_target="tpu_custom_call" | custom-call | flops 20000000000 | bytes 1024 | tf_op jit(solution)/shard_map/pallas_call | solution.py:489
  63.9 1.1 %collective-permute-done.27.got_ref = bf16[208,256]{1,0:T(8,128)(2,1)S(1)} collective-permute-done((bf16[208,256]{1,0:T(8,128)(2,1)S(1)}, bf16[208,256]{1,0:T(8,128)(2,1)S(1)}, u32[]{:S(2)}, u32[]{:S(2)}) %collective-permute-start.27) | collective-permute-done | bytes 106528 | tf_op jit(solution)/shard_map/ppermute | solution.py:144
  64.9 0.6 shard_map.114
  65.6 1.2 %collective-permute-start.28 = (bf16[192,256]{1,0:T(8,128)(2,1)S(1)}, bf16[192,256]{1,0:T(8,128)(2,1)S(1)}, u32[]{:S(2)}, u32[]{:S(2)}) collective-permute-start(bf16[192,256]{1,0:T(8,128)(2,1)S(1)} %get-tuple-element.94), channel_id=1, source_target_pairs={{0,4},{4,0},{8,12},{12,8},{16,20},{20,16},{24,28},{28,24},{1,5},{5... | collective-permute-start | bytes 294920 | tf_op jit(solution)/shard_map/ppermute | solution.py:144
  66.7 0.2 collective-permute-done.30
  67.0 3.7 %collective-permute-start.31 = (bf16[64,256]{1,0:T(8,128)(2,1)S(1)}, bf16[64,256]{1,0:T(8,128)(2,1)S(1)}, u32[]{:S(2)}, u32[]{:S(2)}) collective-permute-start(bf16[64,256]{1,0:T(8,128)(2,1)S(1)} %get-tuple-element.100), channel_id=1, source_target_pairs={{0,8},{4,12},{8,0},{12,4},{16,24},{20,28},{24,16},{28,20},{1,9},{5... | collective-permute-start | bytes 98312 | tf_op jit(solution)/shard_map/ppermute | solution.py:144
  70.6 0.3 collective-permute-start.32
  71.0 2.1 %collective-permute-start.33 = (bf16[64,256]{1,0:T(8,128)(2,1)S(1)}, bf16[64,256]{1,0:T(8,128)(2,1)S(1)}, u32[]{:S(2)}, u32[]{:S(2)}) collective-permute-start(bf16[64,256]{1,0:T(8,128)(2,1)S(1)} %get-tuple-element.101), channel_id=1, source_target_pairs={{0,24},{4,28},{8,16},{12,20},{16,8},{20,12},{24,0},{28,4},{1,25},{... | collective-permute-start | bytes 98312 | tf_op jit(solution)/shard_map/ppermute | solution.py:144
  73.1 0.8 %shard_map.115 = f32[3,128,256]{2,1,0:T(8,128)} custom-call(f32[192,256]{1,0:T(8,128)S(1)} %get-tuple-element.93.mine_ref, bf16[192,256]{1,0:T(8,128)(2,1)S(1)} %collective-permute-done.28.got_ref), custom_call_target="tpu_custom_call" | custom-call | bytes 1024 | tf_op jit(solution)/shard_map/pallas_call | solution.py:489
  73.9 1.6 %collective-permute-done.32 = bf16[64,256]{1,0:T(8,128)(2,1)S(1)} collective-permute-done((bf16[64,256]{1,0:T(8,128)(2,1)S(1)}, bf16[64,256]{1,0:T(8,128)(2,1)S(1)}, u32[]{:S(2)}, u32[]{:S(2)}) %collective-permute-start.32) | collective-permute-done | bytes 32800 | tf_op jit(solution)/shard_map/ppermute | solution.py:144
  75.4 1.2 %collective-permute-done.33 = bf16[64,256]{1,0:T(8,128)(2,1)S(1)} collective-permute-done((bf16[64,256]{1,0:T(8,128)(2,1)S(1)}, bf16[64,256]{1,0:T(8,128)(2,1)S(1)}, u32[]{:S(2)}, u32[]{:S(2)}) %collective-permute-start.33) | collective-permute-done | bytes 32800 | tf_op jit(solution)/shard_map/ppermute | solution.py:144
  76.7 0.6 fusion.3
  (44 shorter events, 0.3 us)
Async XLA Ops:
  0.6 0.9 %copy-start.4 = (bf16[1,128,512]{2,1,0:T(8,128)(2,1)S(1)}, bf16[1,128,512]{2,1,0:T(8,128)(2,1)}, u32[]{:S(2)}) copy-start(bf16[1,128,512]{2,1,0:T(8,128)(2,1)} %param.7) | copy-start | bytes 393220
  1.5 1.1 %copy-start = (bf16[3,512,256]{2,1,0:T(8,128)(2,1)S(1)}, bf16[3,512,256]{2,1,0:T(8,128)(2,1)}, u32[]{:S(2)}) copy-start(bf16[3,512,256]{2,1,0:T(8,128)(2,1)} %w_ref.3) | copy-start | bytes 2359300
  1.5 1.1 %copy-start.1 = (s32[1,128,1]{1,2,0:T(1,128)S(1)}, s32[1,128,1]{1,2,0:T(1,128)}, u32[]{:S(2)}) copy-start(s32[1,128,1]{1,2,0:T(1,128)} %param.9) | copy-start | bytes 1540
  1.5 1.1 %copy-start.2 = (s32[1,8]{1,0:T(1,128)S(1)}, s32[1,8]{1,0:T(1,128)}, u32[]{:S(2)}) copy-start(s32[1,8]{1,0:T(1,128)} %param.8) | copy-start | bytes 100
  1.5 7.0 %copy-start.6 = (bf16[256,64]{0,1:T(8,128)(2,1)S(1)}, bf16[256,64]{0,1:T(8,128)(2,1)}, u32[]{:S(2)}) copy-start(bf16[256,64]{0,1:T(8,128)(2,1)} %param.11) | copy-start | bytes 98308
  3.6 9.9 %collective-permute-start.3 = (bf16[256,128]{1,0:T(8,128)(2,1)S(1)}, bf16[256,128]{1,0:T(8,128)(2,1)S(1)}, u32[]{:S(2)}, u32[]{:S(2)}) collective-permute-start(bf16[256,128]{1,0:T(8,128)(2,1)S(1)} %get-tuple-element.56), channel_id=1, source_target_pairs={{0,4},{4,0},{8,12},{12,8},{16,20},{20,16},{24,28},{28,24},{1,5},{5... | collective-permute-start | bytes 196616 | tf_op jit(solution)/shard_map/ppermute | solution.py:144
  6.6 6.7 %collective-permute-start.4 = (f32[8,256]{1,0:T(8,128)S(1)}, f32[8,256]{1,0:T(8,128)S(1)}, u32[]{:S(2)}, u32[]{:S(2)}) collective-permute-start(f32[8,256]{1,0:T(8,128)S(1)} %get-tuple-element.58), channel_id=1, source_target_pairs={{0,4},{4,8},{8,12},{12,16},{16,20},{20,24},{24,28},{1,5},{5,9},{9,... | collective-permute-start | bytes 24584 | tf_op jit(solution)/shard_map/ppermute | solution.py:20
  8.5 5.0 %collective-permute-start = (bf16[64,256]{1,0:T(8,128)(2,1)S(1)}, bf16[64,256]{1,0:T(8,128)(2,1)S(1)}, u32[]{:S(2)}, u32[]{:S(2)}) collective-permute-start(bf16[64,256]{1,0:T(8,128)(2,1)S(1)} %bitcast.35), channel_id=1, source_target_pairs={{0,8},{4,12},{8,0},{12,4},{16,24},{20,28},{24,16},{28,20},{1,9},{5... | collective-permute-start | bytes 98312 | tf_op jit(solution)/shard_map/ppermute | solution.py:144
  10.7 5.1 %collective-permute-start.1 = (bf16[64,256]{1,0:T(8,128)(2,1)S(1)}, bf16[64,256]{1,0:T(8,128)(2,1)S(1)}, u32[]{:S(2)}, u32[]{:S(2)}) collective-permute-start(bf16[64,256]{1,0:T(8,128)(2,1)S(1)} %bitcast.36), channel_id=1, source_target_pairs={{0,16},{4,20},{8,24},{12,28},{16,0},{20,4},{24,8},{28,12},{1,17},{... | collective-permute-start | bytes 98312 | tf_op jit(solution)/shard_map/ppermute | solution.py:144
  13.3 5.7 %collective-permute-start.2 = (bf16[64,256]{1,0:T(8,128)(2,1)S(1)}, bf16[64,256]{1,0:T(8,128)(2,1)S(1)}, u32[]{:S(2)}, u32[]{:S(2)}) collective-permute-start(bf16[64,256]{1,0:T(8,128)(2,1)S(1)} %bitcast.37), channel_id=1, source_target_pairs={{0,24},{4,28},{8,16},{12,20},{16,8},{20,12},{24,0},{28,4},{1,25},{... | collective-permute-start | bytes 98312 | tf_op jit(solution)/shard_map/ppermute | solution.py:144
  19.0 5.5 %collective-permute-start.5 = (bf16[256,256]{1,0:T(8,128)(2,1)S(1)}, bf16[256,256]{1,0:T(8,128)(2,1)S(1)}, u32[]{:S(2)}, u32[]{:S(2)}) collective-permute-start(bf16[256,256]{1,0:T(8,128)(2,1)S(1)} %shard_map.105.refs_5_), channel_id=1, source_target_pairs={{0,4},{4,0},{8,12},{12,8},{16,20},{20,16},{24,28},{28,24},{1,5},{5... | collective-permute-start | bytes 393224 | tf_op jit(solution)/shard_map/ppermute | solution.py:144
  20.1 5.4 %collective-permute-start.6 = (bf16[256,256]{1,0:T(8,128)(2,1)S(1)}, bf16[256,256]{1,0:T(8,128)(2,1)S(1)}, u32[]{:S(2)}, u32[]{:S(2)}) collective-permute-start(bf16[256,256]{1,0:T(8,128)(2,1)S(1)} %shard_map.105.refs_5_), channel_id=1, source_target_pairs={{0,2},{1,3},{2,0},{3,1},{4,6},{5,7},{6,4},{7,5},{8,10},{9,11},{10,... | collective-permute-start | bytes 393224 | tf_op jit(solution)/shard_map/ppermute | solution.py:144
  21.6 5.9 %collective-permute-start.7 = (bf16[256,256]{1,0:T(8,128)(2,1)S(1)}, bf16[256,256]{1,0:T(8,128)(2,1)S(1)}, u32[]{:S(2)}, u32[]{:S(2)}) collective-permute-start(bf16[256,256]{1,0:T(8,128)(2,1)S(1)} %shard_map.105.refs_5_), channel_id=1, source_target_pairs={{0,6},{1,7},{2,4},{3,5},{4,2},{5,3},{6,0},{7,1},{8,14},{9,15},{10,... | collective-permute-start | bytes 393224 | tf_op jit(solution)/shard_map/ppermute | solution.py:144
  22.6 6.7 %collective-permute-start.8 = (bf16[2,256,128]{2,1,0:T(8,128)(2,1)S(1)}, bf16[2,256,128]{2,1,0:T(8,128)(2,1)S(1)}, u32[]{:S(2)}, u32[]{:S(2)}) collective-permute-start(bf16[2,256,128]{2,1,0:T(8,128)(2,1)S(1)} %pad_maximum_fusion), channel_id=1, source_target_pairs={{0,16},{4,20},{8,24},{12,28},{16,0},{20,4},{24,8},{28,12},{1,17},{... | collective-permute-start | bytes 393224 | tf_op jit(solution)/shard_map/ppermute | solution.py:144
  22.6 7.2 %collective-permute-start.10 = (bf16[64,256]{1,0:T(8,128)(2,1)S(1)}, bf16[64,256]{1,0:T(8,128)(2,1)S(1)}, u32[]{:S(2)}, u32[]{:S(2)}) collective-permute-start(bf16[64,256]{1,0:T(8,128)(2,1)S(1)} %get-tuple-element.72), channel_id=1, source_target_pairs={{0,8},{4,12},{8,0},{12,4},{16,24},{20,28},{24,16},{28,20},{1,9},{5... | collective-permute-start | bytes 98312 | tf_op jit(solution)/shard_map/ppermute | solution.py:144
  24.5 5.3 %collective-permute-start.11 = (bf16[64,256]{1,0:T(8,128)(2,1)S(1)}, bf16[64,256]{1,0:T(8,128)(2,1)S(1)}, u32[]{:S(2)}, u32[]{:S(2)}) collective-permute-start(bf16[64,256]{1,0:T(8,128)(2,1)S(1)} %get-tuple-element.73), channel_id=1, source_target_pairs={{0,16},{4,20},{8,24},{12,28},{16,0},{20,4},{24,8},{28,12},{1,17},{... | collective-permute-start | bytes 98312 | tf_op jit(solution)/shard_map/ppermute | solution.py:144
  25.5 5.7 %collective-permute-start.12 = (bf16[64,256]{1,0:T(8,128)(2,1)S(1)}, bf16[64,256]{1,0:T(8,128)(2,1)S(1)}, u32[]{:S(2)}, u32[]{:S(2)}) collective-permute-start(bf16[64,256]{1,0:T(8,128)(2,1)S(1)} %get-tuple-element.74), channel_id=1, source_target_pairs={{0,24},{4,28},{8,16},{12,20},{16,8},{20,12},{24,0},{28,4},{1,25},{... | collective-permute-start | bytes 98312 | tf_op jit(solution)/shard_map/ppermute | solution.py:144
  27.2 8.5 %copy-start.3 = (bf16[1,136,2048]{2,1,0:T(8,128)(2,1)S(1)}, bf16[1,136,2048]{2,1,0:T(8,128)(2,1)}, u32[]{:S(2)}) copy-start(bf16[1,136,2048]{2,1,0:T(8,128)(2,1)} %param.13) | copy-start | bytes 1671172
  27.2 8.5 %copy-start.7 = (f32[2048]{0:T(1024)S(1)}, f32[2048]{0:T(1024)}, u32[]{:S(2)}) copy-start(f32[2048]{0:T(1024)} %param.12) | copy-start | bytes 24580
  29.3 6.4 %collective-permute-start.14 = (bf16[256,256]{1,0:T(8,128)(2,1)S(1)}, bf16[256,256]{1,0:T(8,128)(2,1)S(1)}, u32[]{:S(2)}, u32[]{:S(2)}) collective-permute-start(bf16[256,256]{1,0:T(8,128)(2,1)S(1)} %shard_map.105.refs_5_), channel_id=1, source_target_pairs={{0,1},{1,0},{2,3},{3,2},{4,5},{5,4},{6,7},{7,6},{8,9},{9,8},{10,11... | collective-permute-start | bytes 393224 | tf_op jit(solution)/shard_map/ppermute | solution.py:144
  29.3 6.4 %collective-permute-start.15 = (bf16[256,256]{1,0:T(8,128)(2,1)S(1)}, bf16[256,256]{1,0:T(8,128)(2,1)S(1)}, u32[]{:S(2)}, u32[]{:S(2)}) collective-permute-start(bf16[256,256]{1,0:T(8,128)(2,1)S(1)} %collective-permute-done.5.refs_6_), channel_id=1, source_target_pairs={{0,1},{1,0},{2,3},{3,2},{4,5},{5,4},{6,7},{7,6},{8,9},{9,8},{10,11... | collective-permute-start | bytes 393224 | tf_op jit(solution)/shard_map/ppermute | solution.py:144
  29.8 5.9 %collective-permute-start.16 = (bf16[256,256]{1,0:T(8,128)(2,1)S(1)}, bf16[256,256]{1,0:T(8,128)(2,1)S(1)}, u32[]{:S(2)}, u32[]{:S(2)}) collective-permute-start(bf16[256,256]{1,0:T(8,128)(2,1)S(1)} %collective-permute-done.6.refs_7_), channel_id=1, source_target_pairs={{0,1},{1,0},{2,3},{3,2},{4,5},{5,4},{6,7},{7,6},{8,9},{9,8},{10,11... | collective-permute-start | bytes 393224 | tf_op jit(solution)/shard_map/ppermute | solution.py:144
  29.8 5.9 %collective-permute-start.17 = (bf16[256,256]{1,0:T(8,128)(2,1)S(1)}, bf16[256,256]{1,0:T(8,128)(2,1)S(1)}, u32[]{:S(2)}, u32[]{:S(2)}) collective-permute-start(bf16[256,256]{1,0:T(8,128)(2,1)S(1)} %collective-permute-done.7.refs_8_), channel_id=1, source_target_pairs={{0,1},{1,0},{2,3},{3,2},{4,5},{5,4},{6,7},{7,6},{8,9},{9,8},{10,11... | collective-permute-start | bytes 393224 | tf_op jit(solution)/shard_map/ppermute | solution.py:144
  31.2 4.3 %collective-permute-start.13 = (bf16[128,256]{1,0:T(8,128)(2,1)S(1)}, bf16[128,256]{1,0:T(8,128)(2,1)S(1)}, u32[]{:S(2)}, u32[]{:S(2)}) collective-permute-start(bf16[128,256]{1,0:T(8,128)(2,1)S(1)} %shard_map.106), channel_id=1, source_target_pairs={{0,4},{4,0},{8,12},{12,8},{16,20},{20,16},{24,28},{28,24},{1,5},{5... | collective-permute-start | bytes 196616 | tf_op jit(solution)/shard_map/ppermute | solution.py:144
  35.5 21.2 %collective-permute-start.9 = (bf16[4,256,128]{2,1,0:T(8,128)(2,1)S(1)}, bf16[4,256,128]{2,1,0:T(8,128)(2,1)S(1)}, u32[]{:S(2)}, u32[]{:S(2)}) collective-permute-start(bf16[4,256,128]{2,1,0:T(8,128)(2,1)S(1)} %constant_dynamic-update-slice_fusion.refs_8_.refs_0_), channel_id=1, source_target_pairs={{0,8},{4,12},{8,0},{12,4},{16,24},{20,28},{24,16},{28,20},{1,9},{5... | collective-permute-start | bytes 786440 | tf_op jit(solution)/shard_map/ppermute | solution.py:144
  37.0 8.1 %collective-permute-start.18 = (bf16[144,256]{1,0:T(8,128)(2,1)S(1)}, bf16[144,256]{1,0:T(8,128)(2,1)S(1)}, u32[]{:S(2)}, u32[]{:S(2)}) collective-permute-start(bf16[144,256]{1,0:T(8,128)(2,1)S(1)} %get-tuple-element.79.refs_0_), channel_id=1, source_target_pairs={{0,4},{4,0},{8,12},{12,8},{16,20},{20,16},{24,28},{28,24},{1,5},{5... | collective-permute-start | bytes 221192 | tf_op jit(solution)/shard_map/ppermute | solution.py:144
  38.1 8.4 %collective-permute-start.19 = (bf16[144,256]{1,0:T(8,128)(2,1)S(1)}, bf16[144,256]{1,0:T(8,128)(2,1)S(1)}, u32[]{:S(2)}, u32[]{:S(2)}) collective-permute-start(bf16[144,256]{1,0:T(8,128)(2,1)S(1)} %get-tuple-element.79.refs_0_), channel_id=1, source_target_pairs={{0,8},{4,12},{8,0},{12,4},{16,24},{20,28},{24,16},{28,20},{1,9},{5... | collective-permute-start | bytes 221192 | tf_op jit(solution)/shard_map/ppermute | solution.py:144
  40.0 8.1 %collective-permute-start.20 = (bf16[144,256]{1,0:T(8,128)(2,1)S(1)}, bf16[144,256]{1,0:T(8,128)(2,1)S(1)}, u32[]{:S(2)}, u32[]{:S(2)}) collective-permute-start(bf16[144,256]{1,0:T(8,128)(2,1)S(1)} %get-tuple-element.79.refs_0_), channel_id=1, source_target_pairs={{0,12},{4,8},{8,4},{12,0},{16,28},{20,24},{24,20},{28,16},{1,13},{... | collective-permute-start | bytes 221192 | tf_op jit(solution)/shard_map/ppermute | solution.py:144
  41.1 2.0 %collective-permute-start.25 = (bf16[16,64,256]{2,1,0:T(8,128)(2,1)S(1)}, bf16[16,64,256]{2,1,0:T(8,128)(2,1)S(1)}, u32[]{:S(2)}, u32[]{:S(2)}) collective-permute-start(bf16[16,64,256]{2,1,0:T(8,128)(2,1)S(1)} %get-tuple-element.82), channel_id=1, source_target_pairs={{0,1},{1,0},{2,3},{3,2},{4,5},{5,4},{6,7},{7,6},{8,9},{9,8},{10,11... | collective-permute-start | bytes 1572872 | tf_op jit(solution)/shard_map/ppermute | solution.py:144
  43.0 11.8 %collective-permute-start.21 = (bf16[144,256]{1,0:T(8,128)(2,1)S(1)}, bf16[144,256]{1,0:T(8,128)(2,1)S(1)}, u32[]{:S(2)}, u32[]{:S(2)}) collective-permute-start(bf16[144,256]{1,0:T(8,128)(2,1)S(1)} %get-tuple-element.79.refs_0_), channel_id=1, source_target_pairs={{0,16},{4,20},{8,24},{12,28},{16,0},{20,4},{24,8},{28,12},{1,17},{... | collective-permute-start | bytes 221192 | tf_op jit(solution)/shard_map/ppermute | solution.py:144
  45.1 11.6 %collective-permute-start.22 = (bf16[144,256]{1,0:T(8,128)(2,1)S(1)}, bf16[144,256]{1,0:T(8,128)(2,1)S(1)}, u32[]{:S(2)}, u32[]{:S(2)}) collective-permute-start(bf16[144,256]{1,0:T(8,128)(2,1)S(1)} %get-tuple-element.79.refs_0_), channel_id=1, source_target_pairs={{0,20},{4,16},{8,28},{12,24},{16,4},{20,0},{24,12},{28,8},{1,21},{... | collective-permute-start | bytes 221192 | tf_op jit(solution)/shard_map/ppermute | solution.py:144
  46.4 10.3 %collective-permute-start.23 = (bf16[144,256]{1,0:T(8,128)(2,1)S(1)}, bf16[144,256]{1,0:T(8,128)(2,1)S(1)}, u32[]{:S(2)}, u32[]{:S(2)}) collective-permute-start(bf16[144,256]{1,0:T(8,128)(2,1)S(1)} %get-tuple-element.79.refs_0_), channel_id=1, source_target_pairs={{0,24},{4,28},{8,16},{12,20},{16,8},{20,12},{24,0},{28,4},{1,25},{... | collective-permute-start | bytes 221192 | tf_op jit(solution)/shard_map/ppermute | solution.py:144
  48.2 8.6 %collective-permute-start.24 = (bf16[144,256]{1,0:T(8,128)(2,1)S(1)}, bf16[144,256]{1,0:T(8,128)(2,1)S(1)}, u32[]{:S(2)}, u32[]{:S(2)}) collective-permute-start(bf16[144,256]{1,0:T(8,128)(2,1)S(1)} %get-tuple-element.79.refs_0_), channel_id=1, source_target_pairs={{0,28},{4,24},{8,20},{12,16},{16,12},{20,8},{24,4},{28,0},{1,29},{... | collective-permute-start | bytes 221192 | tf_op jit(solution)/shard_map/ppermute | solution.py:144
  54.8 6.7 %collective-permute-start.29 = (bf16[8,64,256]{2,1,0:T(8,128)(2,1)S(1)}, bf16[8,64,256]{2,1,0:T(8,128)(2,1)S(1)}, u32[]{:S(2)}, u32[]{:S(2)}) collective-permute-start(bf16[8,64,256]{2,1,0:T(8,128)(2,1)S(1)} %slice.61), channel_id=1, source_target_pairs={{0,2},{1,3},{2,0},{3,1},{4,6},{5,7},{6,4},{7,5},{8,10},{9,11},{10,... | collective-permute-start | bytes 786440 | tf_op jit(solution)/shard_map/ppermute | solution.py:144
  58.3 1.5 %collective-permute-start.26 = (bf16[400,256]{1,0:T(8,128)(2,1)S(1)}, bf16[400,256]{1,0:T(8,128)(2,1)S(1)}, u32[]{:S(2)}, u32[]{:S(2)}) collective-permute-start(bf16[400,256]{1,0:T(8,128)(2,1)S(1)} %get-tuple-element.86), channel_id=1, source_target_pairs={{0,1},{1,0},{2,3},{3,2},{4,5},{5,4},{6,7},{7,6},{8,9},{9,8},{10,11... | collective-permute-start | bytes 614408 | tf_op jit(solution)/shard_map/ppermute | solution.py:144
  58.8 4.0 %copy-start.5 = (bf16[1,128,512]{2,1,0:T(8,128)(2,1)S(1)}, bf16[1,128,512]{2,1,0:T(8,128)(2,1)}, u32[]{:S(2)}) copy-start(bf16[1,128,512]{2,1,0:T(8,128)(2,1)} %param.7) | copy-start | bytes 393220
  59.9 5.1 %collective-permute-start.27 = (bf16[208,256]{1,0:T(8,128)(2,1)S(1)}, bf16[208,256]{1,0:T(8,128)(2,1)S(1)}, u32[]{:S(2)}, u32[]{:S(2)}) collective-permute-start(bf16[208,256]{1,0:T(8,128)(2,1)S(1)} %get-tuple-element.88), channel_id=1, source_target_pairs={{0,2},{1,3},{2,0},{3,1},{4,6},{5,7},{6,4},{7,5},{8,10},{9,11},{10,... | collective-permute-start | bytes 319496 | tf_op jit(solution)/shard_map/ppermute | solution.py:144
  61.6 5.3 %collective-permute-start.30 = (bf16[4,64,256]{2,1,0:T(8,128)(2,1)S(1)}, bf16[4,64,256]{2,1,0:T(8,128)(2,1)S(1)}, u32[]{:S(2)}, u32[]{:S(2)}) collective-permute-start(bf16[4,64,256]{2,1,0:T(8,128)(2,1)S(1)} %slice.62), channel_id=1, source_target_pairs={{0,4},{4,0},{8,12},{12,8},{16,20},{20,16},{24,28},{28,24},{1,5},{5... | collective-permute-start | bytes 393224 | tf_op jit(solution)/shard_map/ppermute | solution.py:144
  65.6 7.5 %collective-permute-start.28 = (bf16[192,256]{1,0:T(8,128)(2,1)S(1)}, bf16[192,256]{1,0:T(8,128)(2,1)S(1)}, u32[]{:S(2)}, u32[]{:S(2)}) collective-permute-start(bf16[192,256]{1,0:T(8,128)(2,1)S(1)} %get-tuple-element.94), channel_id=1, source_target_pairs={{0,4},{4,0},{8,12},{12,8},{16,20},{20,16},{24,28},{28,24},{1,5},{5... | collective-permute-start | bytes 294920 | tf_op jit(solution)/shard_map/ppermute | solution.py:144
  67.0 6.9 %collective-permute-start.31 = (bf16[64,256]{1,0:T(8,128)(2,1)S(1)}, bf16[64,256]{1,0:T(8,128)(2,1)S(1)}, u32[]{:S(2)}, u32[]{:S(2)}) collective-permute-start(bf16[64,256]{1,0:T(8,128)(2,1)S(1)} %get-tuple-element.100), channel_id=1, source_target_pairs={{0,8},{4,12},{8,0},{12,4},{16,24},{20,28},{24,16},{28,20},{1,9},{5... | collective-permute-start | bytes 98312 | tf_op jit(solution)/shard_map/ppermute | solution.py:144
  70.6 4.8 %collective-permute-start.32 = (bf16[64,256]{1,0:T(8,128)(2,1)S(1)}, bf16[64,256]{1,0:T(8,128)(2,1)S(1)}, u32[]{:S(2)}, u32[]{:S(2)}) collective-permute-start(bf16[64,256]{1,0:T(8,128)(2,1)S(1)} %get-tuple-element.102), channel_id=1, source_target_pairs={{0,16},{4,20},{8,24},{12,28},{16,0},{20,4},{24,8},{28,12},{1,17},{... | collective-permute-start | bytes 98312 | tf_op jit(solution)/shard_map/ppermute | solution.py:144
  71.0 5.7 %collective-permute-start.33 = (bf16[64,256]{1,0:T(8,128)(2,1)S(1)}, bf16[64,256]{1,0:T(8,128)(2,1)S(1)}, u32[]{:S(2)}, u32[]{:S(2)}) collective-permute-start(bf16[64,256]{1,0:T(8,128)(2,1)S(1)} %get-tuple-element.101), channel_id=1, source_target_pairs={{0,24},{4,28},{8,16},{12,20},{16,8},{20,12},{24,0},{28,4},{1,25},{... | collective-permute-start | bytes 98312 | tf_op jit(solution)/shard_map/ppermute | solution.py:144

commit v3 on v2

--- a/solution.py
+++ b/solution.py
@@ -144,6 +144,10 @@
     return lax.ppermute(block, axis, [(i, i ^ mask) for i in range(lax.axis_size(axis))])
 
 
+def after(block, *others):
+    return lax.optimization_barrier((block, *others))[0]
+
+
 def iota(shape, dim):
     return lax.broadcasted_iota(jnp.int32, shape, dim)
 
@@ -184,19 +188,13 @@
     )
 
 
-def activate_kernel(feat_ref, padded_ref, mine_ref, other_ref, turned):
+def activate_kernel(feat_ref, padded_ref, turned_ref):
     frames, channels = feat_ref.shape
-    near = jnp.bitwise_and(lax.axis_index("seq"), 1)
     act = elu_wide(feat_ref[...].astype(F32)).astype(BF16).astype(F32)
     padded_ref[0:8, :] = jnp.zeros((8, channels), F32)
     padded_ref[8 : 8 + frames, :] = act
     padded_ref[8 + frames :, :] = jnp.zeros((16, channels), F32)
-    turned[...] = act.T
-    half = mine_ref.shape[0] // 4
-    for book in range(4):
-        for out_ref, side in ((mine_ref, near), (other_ref, 1 - near)):
-            at = pl.multiple_of((2 * book + side) * half, half)
-            out_ref[book * half : (book + 1) * half, :] = turned[pl.ds(at, half), :].astype(BF16)
+    turned_ref[...] = act.T.astype(BF16)
 
 
 def encode_kernel(
@@ -216,8 +214,8 @@
     named_ref[...] = named
     position = me * frames + iota((frames, 1), 0)
     start_of = start_below(position, lengths_ref)
-    after = (me + 1) * frames + iota((16, 1), 0)
-    start_after = start_below(after, lengths_ref)
+    beyond = (me + 1) * frames + iota((16, 1), 0)
+    start_beyond = start_below(beyond, lengths_ref)
     total = jnp.zeros(total_ref.shape, F32)
     edge = jnp.zeros((16, total.shape[1]), F32)
     for tap in range(taps):
@@ -226,7 +224,7 @@
         total = total + jnp.dot(window, w_ref[tap], preferred_element_type=F32)
         if tap:
             window = padded[8 + frames - tap : 24 + frames - tap, :]
-            window = jnp.where(after - tap >= start_after, window, 0.0).astype(BF16)
+            window = jnp.where(beyond - tap >= start_beyond, window, 0.0).astype(BF16)
             edge = edge + jnp.dot(window, w_ref[tap], preferred_element_type=F32)
     total_ref[...] = total
     edge_ref[...] = edge[: edge_ref.shape[0]]
@@ -344,7 +342,9 @@
     owners = owners_ref[...]
     ranks = ranks_of(owners, count)
     position = iota((count, frames), 0) * frames + iota((count, frames), 1)
-    rows_of = [jnp.bitwise_xor(owners.astype(jnp.int32), me).astype(F32), ranks]
+    relative = jnp.bitwise_xor(owners.astype(jnp.int32), me)
+    relative = (relative >> 1) + (relative & 1) * (count // 2)
+    rows_of = [relative.astype(F32), ranks]
     for tap in range(1, taps):
         later = position + tap
         valid = (later < count * frames) & (position >= start_below(later, lengths_ref))
@@ -365,16 +365,19 @@
         facts_ref[block * frames : (block + 1) * frames, :] = facts.astype(jnp.int32)
 
 
-def spread_kernel(orders, count, frames, taps, *refs):
-    backs, turned_refs = refs[:count], refs[count : count + len(orders)]
-    facts_ref, send_ref, windows_ref, gain_ref, gathered, wide, lhs = refs[count + len(orders) :]
+def spread_kernel(count, frames, taps, *refs):
+    backs = refs[: count // 2 + 1]
+    lines_ref, facts_ref, send_ref, windows_ref, gain_ref, gathered, wide = refs[len(backs) :]
     rows, latent_width = backs[0].shape
-    share = turned_refs[0].shape[1] // 4
+    share = lines_ref.shape[0] // 2
     gain_rows = gain_ref.shape[0]
     gain = jnp.zeros((gain_rows, latent_width), F32)
-    for rel, back_ref in enumerate(backs):
-        gathered[rel * rows : (rel + 1) * rows, :] = back_ref[...]
-        gain = gain + back_ref[...].astype(F32)[rows - gain_rows :]
+    for far, back_ref in enumerate(backs[:-1]):
+        gathered[far * rows : (far + 1) * rows, :] = back_ref[...]
+    far_count = count // 2
+    gathered[far_count * rows :, :] = backs[-1][...]
+    for rel in range(count):
+        gain = gain + gathered[rel * rows : (rel + 1) * rows, :].astype(F32)[rows - gain_rows :]
     gain_ref[...] = gain
     for block in range(count):
         here = slice(block * frames, (block + 1) * frames)
@@ -390,7 +393,7 @@
             later = wide[block * frames + tap : (block + 1) * frames + tap, :]
             later = jnp.where(facts_ref[here, tap : tap + 1] > 0, later, 0.0)
             windows_ref[here, tap * latent_width : (tap + 1) * latent_width] = later.astype(BF16)
-    part = kernel_part(orders, turned_refs, windows_ref, lhs, share, 1)
+    part = jnp.dot(lines_ref[...], windows_ref[...], preferred_element_type=F32)
     for y in (0, 1):
         for tap in range(taps):
             at = (y * taps + tap) * share
@@ -404,24 +407,25 @@
     ).astype(BF16)
 
 
-def kernel_part(orders, turned_refs, windows_ref, lhs, share, core):
+def channel_kernel(orders, *refs):
+    turned_refs, out_refs = refs[: len(orders)], refs[len(orders) :]
     seq, book = lax.axis_index("seq"), lax.axis_index("book")
+    share = turned_refs[0].shape[1] // 4
     for turned_ref, order in zip(turned_refs, orders):
         frames = turned_ref.shape[2]
         for index, rel in enumerate(order):
             lanes = pl.ds(pl.multiple_of(jnp.bitwise_xor(seq, rel) * frames, frames), frames)
-            for y in (0, 1):
-                at = jnp.bitwise_xor(book, 2 * y + core) * share
-                lhs[y * share : (y + 1) * share, lanes] = turned_ref[
-                    index, pl.ds(pl.multiple_of(at, share), share), :
-                ]
-    return jnp.dot(lhs[...], windows_ref[...], preferred_element_type=F32)
-
-
-def own_part_kernel(orders, taps, *refs):
-    turned_refs, (windows_ref, out_ref, lhs) = refs[: len(orders)], refs[len(orders) :]
-    share, latent_width = turned_refs[0].shape[1] // 4, out_ref.shape[1]
-    part = kernel_part(orders, turned_refs, windows_ref, lhs, share, 0)
+            for core, out_ref in enumerate(out_refs):
+                for y in (0, 1):
+                    at = jnp.bitwise_xor(book, 2 * y + core) * share
+                    out_ref[y * share : (y + 1) * share, lanes] = turned_ref[
+                        index, pl.ds(pl.multiple_of(at, share), share), :
+                    ]
+
+
+def own_part_kernel(taps, lines_ref, windows_ref, out_ref):
+    share, latent_width = lines_ref.shape[0] // 2, out_ref.shape[1]
+    part = jnp.dot(lines_ref[...], windows_ref[...], preferred_element_type=F32)
     for y in (0, 1):
         for tap in range(taps):
             at = (y * taps + tap) * share
@@ -445,27 +449,14 @@
     ).astype(BF16)
 
 
-def finish_kernel(mine_ref, got_ref, gain_ref, send_ref, out_ref, gain_out_ref):
+def finish_kernel(mine_ref, got_ref, gain_ref, out_ref, gain_out_ref):
     half, gain_rows = mine_ref.shape[0], gain_ref.shape[0]
-    total = mine_ref[...] + got_ref[0:half, :].astype(F32)
-    out_ref[...] = total
-    send_ref[...] = total.astype(BF16)
+    out_ref[...] = mine_ref[...] + got_ref[0:half, :].astype(F32)
     pair = got_ref[half : half + 2 * gain_rows, :].astype(F32)
     gain = gain_ref[...] + (pair[:gain_rows] + pair[gain_rows:])
     step = gain.shape[1]
     for line in range(gain_rows):
         gain_out_ref[:, line * step : (line + 1) * step] = gain[line : line + 1]
-
-
-def join_kernel(mine_ref, got_ref, out_ref):
-    taps, share = out_ref.shape[:2]
-    half = share // 2
-    near = jnp.bitwise_and(lax.axis_index("seq"), 1)
-    for tap in range(taps):
-        here = slice(tap * half, (tap + 1) * half)
-        mine, got = mine_ref[here, :], got_ref[here, :].astype(F32)
-        out_ref[tap, 0:half, :] = jnp.where(near == 0, mine, got)
-        out_ref[tap, half:, :] = jnp.where(near == 0, got, mine)
 
 
 def feature_kernel(feat_ref, windows_ref, w_ref, out_ref):
@@ -515,18 +506,13 @@
     piece = round_up(capacity + 1, 16)
     gain_rows = width // latent_width
     rows = round_up(slots + gain_rows, 16)
-    half = channels // 8
+    half = channels // 4
 
     columns = w_in.shape[1]
-    padded, mine, other = call(
+    padded, turned = call(
         activate_kernel,
-        [
-            shape((24 + frames, channels), F32),
-            shape((channels // 2, frames)),
-            shape((channels // 2, frames)),
-        ],
+        [shape((24 + frames, channels), F32), shape((channels, frames))],
         (feats,),
-        scratch=[pltpu.VMEM((channels, frames), F32)],
         flops=HEAVY // 10,
     )
     total, placed, edge, named = call(
@@ -540,17 +526,18 @@
         (book_lengths, padded, owner[0].T, w_enc),
         smem=1,
     )
-    w_own, edge, other = lax.optimization_barrier((w_in.T, edge, other))
+    w_own, edge, turned = lax.optimization_barrier((w_in.T, edge, turned))
     edge = shifted(edge, "seq", 1)
     w_far = [w_own] + [swap(w_own, "seq", 2 * far) for far in fars]
-    held = jnp.stack([mine, swap(other, "seq", 1)])
+    held = jnp.stack([turned, swap(turned, "seq", 4)])
     sent = call(
         functools.partial(place_kernel, piece),
         [shape((2 * piece, latent_width))] * far_count,
         (total, edge, placed, named),
     )
-    w_far, held, sent = lax.optimization_barrier((w_far, held, sent))
+    held, sent = lax.optimization_barrier((held, sent))
     landed = [sent[0]] + [swap(sent[far], "seq", 2 * far) for far in fars]
+    w_far = after(w_far, landed[1], landed[2])
     (w_line,) = call(
         functools.partial(join_rows_kernel, 0),
         [shape((far_count * columns, latent_width))],
@@ -560,7 +547,7 @@
     w_near = swap(w_line, "seq", 1)
     w_side = swap(w_line, "book", 2)
     w_diag = swap(w_line, ("seq", "book"), 4 + 2)
-    got = swap(held, "seq", 4)
+    got = swap(held, "seq", 2)
     (near,) = call(
         functools.partial(join_rows_kernel, piece),
         [shape((far_count * piece, latent_width))],
@@ -572,9 +559,9 @@
     w_chips, got = lax.optimization_barrier((w_chips, got))
     held = jnp.concatenate([held, got])
     w_pieces = w_chips + [swap(block, "book", 1) for block in w_chips]
-    second = swap(held, "seq", 2)
+    second = swap(held, "seq", 1)
     turned_all = [held, second]
-    orders = [[0, 1, 4, 5], [2, 3, 6, 7]]
+    orders = [[0, 4, 2, 6], [1, 5, 3, 7]]
 
     back, hidden_grad, arrived, owners = call(
         functools.partial(middle_kernel, piece, capacity, frames, count, columns),
@@ -593,7 +580,14 @@
         ],
         flops=HEAVY,
     )
-    backs = [back] + [swap(back, "seq", rel) for rel in range(1, count)]
+    backs = [back] + [swap(back, "seq", 2 * far) for far in fars]
+    (near_backs,) = call(
+        functools.partial(join_rows_kernel, 0),
+        [shape((far_count * rows, latent_width))],
+        tuple(backs),
+        flops=HEAVY,
+    )
+    near_backs = swap(near_backs, "seq", 1)
 
     (facts,) = call(
         functools.partial(prepare_kernel, capacity, rows),
@@ -609,34 +603,36 @@
     )
     w_got, facts = lax.optimization_barrier((swap(w_send, "book", 1), facts))
     w_sum = w_keep.astype(F32) + w_got.astype(F32)
-    w_sum = w_sum[:count] + swap(w_sum[count:].astype(BF16), "book", 2).astype(F32)
-    w_sum = w_sum[:far_count] + swap(w_sum[far_count:].astype(BF16), "seq", 1).astype(F32)
-    w_total = w_sum[0]
-    for far in fars:
-        w_total = w_total + swap(w_sum[far].astype(BF16), "seq", 2 * far).astype(F32)
-
+    w_parts = [w_sum[at : at + far_count].astype(BF16) for at in range(0, 2 * count, far_count)]
+    w_sum = w_sum[:far_count] + swap(w_parts[1], "seq", 1).astype(F32)
+    w_sum = w_sum + swap(w_parts[2], "book", 2).astype(F32)
+    w_sum = w_sum + swap(w_parts[3], ("seq", "book"), 4 + 2).astype(F32)
+    own_lines, sent_lines = call(
+        functools.partial(channel_kernel, orders),
+        [shape((2 * half, count * frames))] * 2,
+        tuple(after(turned_all, *w_parts)),
+        flops=HEAVY,
+    )
     message = 2 * taps * half + 2 * gain_rows
     k_send, windows, gain_seq = call(
-        functools.partial(spread_kernel, orders, count, frames, taps),
+        functools.partial(spread_kernel, count, frames, taps),
         [
             shape((message, latent_width)),
             shape((count * frames, taps * latent_width)),
             shape((gain_rows, latent_width), F32),
         ],
-        (*backs, *turned_all, facts),
+        (*backs, near_backs, sent_lines, facts),
         scratch=[
             pltpu.VMEM((count * rows, latent_width), BF16),
             pltpu.VMEM((count * frames + 8, latent_width), F32),
-            pltpu.VMEM((2 * half, count * frames), BF16),
         ],
         flops=HEAVY,
     )
     k_got = swap(k_send, "book", 1)
     (k_kept,) = call(
-        functools.partial(own_part_kernel, orders, taps),
+        functools.partial(own_part_kernel, taps),
         [shape((2 * taps * half, latent_width), F32)],
-        (*turned_all, windows),
-        scratch=[pltpu.VMEM((2 * half, count * frames), BF16)],
+        (own_lines, windows),
         flops=HEAVY,
     )
     y_send, k_mine, gain_pair = call(
@@ -649,27 +645,26 @@
         (k_kept, k_got, gain_seq),
     )
     y_got = swap(y_send, "book", 2)
+    w_far = [w_sum[far].astype(BF16) for far in fars]
+    w_far = [after(block, k_send) for block in w_far[:0]] + [after(block, y_send) for block in w_far[0:]]
+    w_total = w_sum[0]
+    for far in fars:
+        w_total = w_total + swap(w_far[far - 1], "seq", 2 * far).astype(F32)
     (feature_grad,) = call(
-        feature_kernel, [shape(feats.shape)], (feats, windows, w_enc), flops=HEAVY
-    )
-    y_got, feature_grad = lax.optimization_barrier((y_got, feature_grad))
-    x_back, kernel_half, gain_total = call(
+        feature_kernel,
+        [shape(feats.shape)],
+        (feats, after(windows, y_send), w_enc),
+        flops=HEAVY,
+    )
+    y_got = after(y_got, feature_grad)
+    kernel_mine, gain_total = call(
         finish_kernel,
-        [
-            shape((taps * half, latent_width)),
-            shape((taps * half, latent_width), F32),
-            shape((1, width), F32),
-        ],
+        [shape((taps * half, latent_width), F32), shape((1, width), F32)],
         (k_mine, y_got, gain_pair),
-    )
-    (kernel_mine,) = call(
-        join_kernel,
-        [shape((taps, 2 * half, latent_width), F32)],
-        (kernel_half, swap(x_back, "seq", 1)),
     )
     return (
         feature_grad[None],
-        kernel_mine,
+        kernel_mine.reshape(taps, half, latent_width),
         w_total.T,
         gain_total[0],
     )

time: 77.5 us -> 72.8 us (0.939)
  waiting for transfers between devices: 22.3 us -> 17.5 us
    ppermute x33 -> x30, waiting for transfers between devices: 22.3 us -> 17.5 us  [swap(): lax.ppermute(block, axis, [(i, i ^ mask) for i in range(lax.axis_size(axi...]
    ppermute x1, starting transfers between devices: 1.92 us -> 3.38 us  [shifted(): return lax.ppermute(block, axis, route)]
    ppermute x33 -> x30, starting transfers between devices: 40.6 us -> 39.2 us  [swap(): lax.ppermute(block, axis, [(i, i ^ mask) for i in range(lax.axis_size(axi...]
    unnamed x17 -> x19, local copies, waits for them, and re-layouts: 1.74 us -> 1.78 us
    pallas_call x14 -> x15, Pallas kernels: 8.92 us -> 8.95 us  [call(): pl.pallas_call(kernel, out_shape=outs, in_specs=[SMEM] * smem + [VMEM] *...]
  transfers between devices with their start and end apart: 34 -> 31, of which waited for: 15 -> 11; matrix products, arithmetic and copies ran while one was open for 0% -> 1% of each run, Pallas kernels for 10% -> 9%
where the time goes in v3:
time: 72.8 us; the launch traced here: 72.7 us
  starting transfers between devices  42.6 us (59%)
  waiting for transfers between devices  17.5 us (24%)
  Pallas kernels  8.95 us (12%)
  local copies, waits for them, and re-layouts  1.85 us (3%)
  between operations  0.93 us (1%)
  other arithmetic  0.92 us (1%)
    ppermute x30, starting transfers between devices, swap(): lax.ppermute(block, axis, [(i, i ^ mask) for i in range(lax.axis_size(axi...  39.2 us
    ppermute x30, waiting for transfers between devices, swap(): lax.ppermute(block, axis, [(i, i ^ mask) for i in range(lax.axis_size(axi...  17.5 us
    pallas_call x15, Pallas kernels, call(): pl.pallas_call(kernel, out_shape=outs, in_specs=[SMEM] * smem + [VMEM] *...  8.95 us
    ppermute x1, starting transfers between devices, shifted(): return lax.ppermute(block, axis, route)  3.38 us
    unnamed x19, local copies, waits for them, and re-layouts  1.78 us
  transfers between devices with their start and end apart: 31, of which 11 were waited for; matrix products, arithmetic and copies ran while one was open for 1% of the time, Pallas kernels for 9%

profile of v3, /device:TPU:0, one launch (start us, length us, event | category | flops | bytes accessed | tf_op | source)
XLA Modules:
  0.0 72.7 jit_solution(14086853883088634331)
XLA Ops:
  0.6 0.0 copy-start.5
  0.6 0.9 %copy-done.5 = bf16[1,128,512]{2,1,0:T(8,128)(2,1)S(1)} copy-done((bf16[1,128,512]{2,1,0:T(8,128)(2,1)S(1)}, bf16[1,128,512]{2,1,0:T(8,128)(2,1)}, u32[]{:S(2)}) %copy-start.5) | copy-done | bytes 131096
  1.6 0.3 shard_map.102
  1.9 0.8 %copy-done = bf16[3,512,256]{2,1,0:T(8,128)(2,1)S(1)} copy-done((bf16[3,512,256]{2,1,0:T(8,128)(2,1)S(1)}, bf16[3,512,256]{2,1,0:T(8,128)(2,1)}, u32[]{:S(2)}) %copy-start) | copy-done | bytes 786456
  2.7 0.9 %shard_map.103 = (f32[128,256]{1,0:T(8,128)S(1)}, bf16[256,128]{1,0:T(8,128)(2,1)S(1)}, f32[8,256]{1,0:T(8,128)S(1)}, f32[1,256]{1,0:T(1,128)S(1)}) custom-call(s32[8]{0:T(128)S(1)} %bitcast.31, f32[152,512]{1,0:T(8,128)S(1)} %get-tuple-element.56.padded, s32[1,128]{1,0:T(1,128)S(1)} %bitcast.30, bf16[3,512,256]{2,1,0:T(8,128)(2,1)S(1)} %copy-done), custom_call_target="tpu_custom_call" | custom-call | bytes 1024 | tf_op jit(solution)/shard_map/pallas_call | solution.py:480
  3.6 4.1 %collective-permute-start = (bf16[512,128]{1,0:T(8,128)(2,1)S(1)}, bf16[512,128]{1,0:T(8,128)(2,1)S(1)}, u32[]{:S(2)}, u32[]{:S(2)}) collective-permute-start(bf16[512,128]{1,0:T(8,128)(2,1)S(1)} %get-tuple-element.59), channel_id=1, source_target_pairs={{0,16},{4,20},{8,24},{12,28},{16,0},{20,4},{24,8},{28,12},{1,17},{... | collective-permute-start | bytes 393224 | tf_op jit(solution)/shard_map/ppermute | solution.py:144
  7.7 3.4 %collective-permute-start.1 = (f32[8,256]{1,0:T(8,128)S(1)}, f32[8,256]{1,0:T(8,128)S(1)}, u32[]{:S(2)}, u32[]{:S(2)}) collective-permute-start(f32[8,256]{1,0:T(8,128)S(1)} %get-tuple-element.61), channel_id=1, source_target_pairs={{0,4},{4,8},{8,12},{12,16},{16,20},{20,24},{24,28},{1,5},{5,9},{9,... | collective-permute-start | bytes 24584 | tf_op jit(solution)/shard_map/ppermute | solution.py:20
  11.1 1.6 %collective-permute-start.6 = (bf16[64,256]{1,0:T(8,128)(2,1)S(1)}, bf16[64,256]{1,0:T(8,128)(2,1)S(1)}, u32[]{:S(2)}, u32[]{:S(2)}) collective-permute-start(bf16[64,256]{1,0:T(8,128)(2,1)S(1)} %bitcast.36), channel_id=1, source_target_pairs={{0,8},{4,12},{8,0},{12,4},{16,24},{20,28},{24,16},{28,20},{1,9},{5... | collective-permute-start | bytes 98312 | tf_op jit(solution)/shard_map/ppermute | solution.py:144
  12.8 0.3 collective-permute-start.7
  13.1 2.5 %collective-permute-start.8 = (bf16[64,256]{1,0:T(8,128)(2,1)S(1)}, bf16[64,256]{1,0:T(8,128)(2,1)S(1)}, u32[]{:S(2)}, u32[]{:S(2)}) collective-permute-start(bf16[64,256]{1,0:T(8,128)(2,1)S(1)} %bitcast.38), channel_id=1, source_target_pairs={{0,24},{4,28},{8,16},{12,20},{16,8},{20,12},{24,0},{28,4},{1,25},{... | collective-permute-start | bytes 98312 | tf_op jit(solution)/shard_map/ppermute | solution.py:144
  15.6 0.2 shard_map.104
  15.8 0.7 %collective-permute-start.2 = (bf16[64,256]{1,0:T(8,128)(2,1)S(1)}, bf16[64,256]{1,0:T(8,128)(2,1)S(1)}, u32[]{:S(2)}, u32[]{:S(2)}) collective-permute-start(bf16[64,256]{1,0:T(8,128)(2,1)S(1)} %get-tuple-element.69), channel_id=1, source_target_pairs={{0,8},{4,12},{8,0},{12,4},{16,24},{20,28},{24,16},{28,20},{1,9},{5... | collective-permute-start | bytes 98312 | tf_op jit(solution)/shard_map/ppermute | solution.py:144
  16.5 2.4 %collective-permute-start.3 = (bf16[64,256]{1,0:T(8,128)(2,1)S(1)}, bf16[64,256]{1,0:T(8,128)(2,1)S(1)}, u32[]{:S(2)}, u32[]{:S(2)}) collective-permute-start(bf16[64,256]{1,0:T(8,128)(2,1)S(1)} %get-tuple-element.70), channel_id=1, source_target_pairs={{0,16},{4,20},{8,24},{12,28},{16,0},{20,4},{24,8},{28,12},{1,17},{... | collective-permute-start | bytes 98312 | tf_op jit(solution)/shard_map/ppermute | solution.py:144
  18.9 1.9 %collective-permute-start.12 = (bf16[2,512,128]{2,1,0:T(8,128)(2,1)S(1)}, bf16[2,512,128]{2,1,0:T(8,128)(2,1)S(1)}, u32[]{:S(2)}, u32[]{:S(2)}) collective-permute-start(bf16[2,512,128]{2,1,0:T(8,128)(2,1)S(1)} %pad_maximum_fusion), channel_id=1, source_target_pairs={{0,8},{4,12},{8,0},{12,4},{16,24},{20,28},{24,16},{28,20},{1,9},{5... | collective-permute-start | bytes 786440 | tf_op jit(solution)/shard_map/ppermute | solution.py:144
  20.9 0.0 collective-permute-done.7.refs_2_
  20.9 0.8 %collective-permute-done.3.refs_2_ = bf16[64,256]{1,0:T(8,128)(2,1)S(1)} collective-permute-done((bf16[64,256]{1,0:T(8,128)(2,1)S(1)}, bf16[64,256]{1,0:T(8,128)(2,1)S(1)}, u32[]{:S(2)}, u32[]{:S(2)}) %collective-permute-start.3) | collective-permute-done | bytes 32800 | tf_op jit(solution)/shard_map/ppermute | solution.py:144
  21.7 1.6 %collective-permute-start.10 = (bf16[256,256]{1,0:T(8,128)(2,1)S(1)}, bf16[256,256]{1,0:T(8,128)(2,1)S(1)}, u32[]{:S(2)}, u32[]{:S(2)}) collective-permute-start(bf16[256,256]{1,0:T(8,128)(2,1)S(1)} %shard_map.106.refs_5_), channel_id=1, source_target_pairs={{0,2},{1,3},{2,0},{3,1},{4,6},{5,7},{6,4},{7,5},{8,10},{9,11},{10,... | collective-permute-start | bytes 393224 | tf_op jit(solution)/shard_map/ppermute | solution.py:144
  23.3 0.6 collective-permute-start.11
  23.9 1.4 %collective-permute-start.9 = (bf16[256,256]{1,0:T(8,128)(2,1)S(1)}, bf16[256,256]{1,0:T(8,128)(2,1)S(1)}, u32[]{:S(2)}, u32[]{:S(2)}) collective-permute-start(bf16[256,256]{1,0:T(8,128)(2,1)S(1)} %shard_map.106.refs_5_), channel_id=1, source_target_pairs={{0,4},{4,0},{8,12},{12,8},{16,20},{20,16},{24,28},{28,24},{1,5},{5... | collective-permute-start | bytes 393224 | tf_op jit(solution)/shard_map/ppermute | solution.py:144
  25.3 3.5 %collective-permute-start.4 = (bf16[64,256]{1,0:T(8,128)(2,1)S(1)}, bf16[64,256]{1,0:T(8,128)(2,1)S(1)}, u32[]{:S(2)}, u32[]{:S(2)}) collective-permute-start(bf16[64,256]{1,0:T(8,128)(2,1)S(1)} %get-tuple-element.71), channel_id=1, source_target_pairs={{0,24},{4,28},{8,16},{12,20},{16,8},{20,12},{24,0},{28,4},{1,25},{... | collective-permute-start | bytes 98312 | tf_op jit(solution)/shard_map/ppermute | solution.py:144
  28.9 0.0 copy-start.4
  28.9 0.0 copy-start.8
  28.9 0.3 collective-permute-done.11.refs_8_
  29.2 0.4 collective-permute-done.9.refs_6_
  29.6 0.5 collective-permute-start.14
  30.2 0.0 collective-permute-start.15
  30.2 0.5 collective-permute-start.16
  30.7 0.4 collective-permute-done.4.refs_3_
  31.1 1.0 %collective-permute-start.5 = (bf16[128,256]{1,0:T(8,128)(2,1)S(1)}, bf16[128,256]{1,0:T(8,128)(2,1)S(1)}, u32[]{:S(2)}, u32[]{:S(2)}) collective-permute-start(bf16[128,256]{1,0:T(8,128)(2,1)S(1)} %shard_map.105), channel_id=1, source_target_pairs={{0,4},{4,0},{8,12},{12,8},{16,20},{20,16},{24,28},{28,24},{1,5},{5... | collective-permute-start | bytes 196616 | tf_op jit(solution)/shard_map/ppermute | solution.py:144
  32.2 3.2 %collective-permute-done.5.refs_4_ = bf16[128,256]{1,0:T(8,128)(2,1)S(1)} collective-permute-done((bf16[128,256]{1,0:T(8,128)(2,1)S(1)}, bf16[128,256]{1,0:T(8,128)(2,1)S(1)}, u32[]{:S(2)}, u32[]{:S(2)}) %collective-permute-start.5) | collective-permute-done | bytes 65568 | tf_op jit(solution)/shard_map/ppermute | solution.py:144
  35.4 1.0 %collective-permute-start.21 = (bf16[4,512,128]{2,1,0:T(8,128)(2,1)S(1)}, bf16[4,512,128]{2,1,0:T(8,128)(2,1)S(1)}, u32[]{:S(2)}, u32[]{:S(2)}) collective-permute-start(bf16[4,512,128]{2,1,0:T(8,128)(2,1)S(1)} %constant_dynamic-update-slice_fusion.refs_0_), channel_id=1, source_target_pairs={{0,4},{4,0},{8,12},{12,8},{16,20},{20,16},{24,28},{28,24},{1,5},{5... | collective-permute-start | bytes 1572872 | tf_op jit(solution)/shard_map/ppermute | solution.py:144
  36.4 1.2 %shard_map.107 = (bf16[144,256]{1,0:T(8,128)(2,1)S(1)}, bf16[144,2048]{1,0:T(8,128)(2,1)S(1)}, bf16[144,256]{1,0:T(8,128)(2,1)S(1)}, f32[8,128]{1,0:T(8,128)S(1)}) custom-call(bf16[64,256]{1,0:T(8,128)(2,1)S(1)} %get-tuple-element.68.refs_0_, bf16[64,256]{1,0:T(8,128)(2,1)S(1)} %collective-permute-done.2.refs_1_, ...), custom_call_target="tpu_custom_call" | custom-call | flops 20000000000 | bytes 1024 | tf_op jit(solution)/shard_map/pallas_call | solution.py:480
  37.7 1.6 %collective-permute-start.17 = (bf16[144,256]{1,0:T(8,128)(2,1)S(1)}, bf16[144,256]{1,0:T(8,128)(2,1)S(1)}, u32[]{:S(2)}, u32[]{:S(2)}) collective-permute-start(bf16[144,256]{1,0:T(8,128)(2,1)S(1)} %get-tuple-element.82.refs_0_), channel_id=1, source_target_pairs={{0,8},{4,12},{8,0},{12,4},{16,24},{20,28},{24,16},{28,20},{1,9},{5... | collective-permute-start | bytes 221192 | tf_op jit(solution)/shard_map/ppermute | solution.py:144
  39.2 1.9 %collective-permute-start.18 = (bf16[144,256]{1,0:T(8,128)(2,1)S(1)}, bf16[144,256]{1,0:T(8,128)(2,1)S(1)}, u32[]{:S(2)}, u32[]{:S(2)}) collective-permute-start(bf16[144,256]{1,0:T(8,128)(2,1)S(1)} %get-tuple-element.82.refs_0_), channel_id=1, source_target_pairs={{0,16},{4,20},{8,24},{12,28},{16,0},{20,4},{24,8},{28,12},{1,17},{... | collective-permute-start | bytes 221192 | tf_op jit(solution)/shard_map/ppermute | solution.py:144
  41.1 1.0 %collective-permute-start.19 = (bf16[144,256]{1,0:T(8,128)(2,1)S(1)}, bf16[144,256]{1,0:T(8,128)(2,1)S(1)}, u32[]{:S(2)}, u32[]{:S(2)}) collective-permute-start(bf16[144,256]{1,0:T(8,128)(2,1)S(1)} %get-tuple-element.82.refs_0_), channel_id=1, source_target_pairs={{0,24},{4,28},{8,16},{12,20},{16,8},{20,12},{24,0},{28,4},{1,25},{... | collective-permute-start | bytes 221192 | tf_op jit(solution)/shard_map/ppermute | solution.py:144
  42.1 0.5 shard_map.109
  42.7 0.1 collective-permute-start.22
  42.7 1.3 %shard_map.110.refs_6_ = s32[1024,3]{1,0:T(8,128)S(1)} custom-call(s32[8]{0:T(128)S(1)} %bitcast.32, f32[8,128]{1,0:T(8,128)S(1)} %get-tuple-element.88.owners_ref), custom_call_target="tpu_custom_call" | custom-call | flops 20000000000 | bytes 1024 | tf_op jit(solution)/shard_map/pallas_call | solution.py:480
  44.0 1.9 %collective-permute-done.18.refs_2_ = bf16[144,256]{1,0:T(8,128)(2,1)S(1)} collective-permute-done((bf16[144,256]{1,0:T(8,128)(2,1)S(1)}, bf16[144,256]{1,0:T(8,128)(2,1)S(1)}, u32[]{:S(2)}, u32[]{:S(2)}) %collective-permute-start.18) | collective-permute-done | bytes 73760 | tf_op jit(solution)/shard_map/ppermute | solution.py:144
  46.0 1.4 %collective-permute-done.19.refs_3_ = bf16[144,256]{1,0:T(8,128)(2,1)S(1)} collective-permute-done((bf16[144,256]{1,0:T(8,128)(2,1)S(1)}, bf16[144,256]{1,0:T(8,128)(2,1)S(1)}, u32[]{:S(2)}, u32[]{:S(2)}) %collective-permute-start.19) | collective-permute-done | bytes 73760 | tf_op jit(solution)/shard_map/ppermute | solution.py:144
  47.4 1.6 %collective-permute-start.20 = (bf16[576,256]{1,0:T(8,128)(2,1)S(1)}, bf16[576,256]{1,0:T(8,128)(2,1)S(1)}, u32[]{:S(2)}, u32[]{:S(2)}) collective-permute-start(bf16[576,256]{1,0:T(8,128)(2,1)S(1)} %shard_map.108), channel_id=1, source_target_pairs={{0,4},{4,0},{8,12},{12,8},{16,20},{20,16},{24,28},{28,24},{1,5},{5... | collective-permute-start | bytes 884744 | tf_op jit(solution)/shard_map/ppermute | solution.py:144
  49.0 0.2 convert_add_fusion
  49.2 0.5 collective-permute-start.25
  49.8 1.5 %collective-permute-start.26 = (bf16[4,64,256]{2,1,0:T(8,128)(2,1)S(1)}, bf16[4,64,256]{2,1,0:T(8,128)(2,1)S(1)}, u32[]{:S(2)}, u32[]{:S(2)}) collective-permute-start(bf16[4,64,256]{2,1,0:T(8,128)(2,1)S(1)} %get-tuple-element.113), channel_id=1, source_target_pairs={{0,2},{1,3},{2,0},{3,1},{4,6},{5,7},{6,4},{7,5},{8,10},{9,11},{10,... | collective-permute-start | bytes 393224 | tf_op jit(solution)/shard_map/ppermute | solution.py:144
  51.3 1.5 %collective-permute-start.27 = (bf16[4,64,256]{2,1,0:T(8,128)(2,1)S(1)}, bf16[4,64,256]{2,1,0:T(8,128)(2,1)S(1)}, u32[]{:S(2)}, u32[]{:S(2)}) collective-permute-start(bf16[4,64,256]{2,1,0:T(8,128)(2,1)S(1)} %get-tuple-element.112), channel_id=1, source_target_pairs={{0,6},{1,7},{2,4},{3,5},{4,2},{5,3},{6,0},{7,1},{8,14},{9,15},{10,... | collective-permute-start | bytes 393224 | tf_op jit(solution)/shard_map/ppermute | solution.py:144
  52.8 0.3 shard_map.111
  53.1 3.7 %collective-permute-done.20.refs_4_ = bf16[576,256]{1,0:T(8,128)(2,1)S(1)} collective-permute-done((bf16[576,256]{1,0:T(8,128)(2,1)S(1)}, bf16[576,256]{1,0:T(8,128)(2,1)S(1)}, u32[]{:S(2)}, u32[]{:S(2)}) %collective-permute-start.20) | collective-permute-done | bytes 294944 | tf_op jit(solution)/shard_map/ppermute | solution.py:144
  56.8 1.7 %shard_map.112 = (bf16[784,256]{1,0:T(8,128)(2,1)S(1)}, bf16[1024,768]{1,0:T(8,128)(2,1)S(1)}, f32[8,256]{1,0:T(8,128)S(1)}) custom-call(bf16[144,256]{1,0:T(8,128)(2,1)S(1)} %get-tuple-element.82.refs_0_, bf16[144,256]{1,0:T(8,128)(2,1)S(1)} %collective-permute-done.17.refs_1_, bf16[144,256]{1,0:T(8,128)(2,1)S(1)} %collective-permute-done.18.refs_2_, ...), custom_call_target="tpu_custom_call" | custom-call | flops 20000000000 | bytes 1024 | tf_op jit(solution)/shard_map/pallas_call | solution.py:480
  58.5 0.1 collective-permute-start.23
  58.6 0.6 shard_map.113.kept_ref
  59.2 0.0 copy-start.1
  59.2 0.0 copy-start.6
  59.2 1.3 %collective-permute-done.27 = bf16[4,64,256]{2,1,0:T(8,128)(2,1)S(1)} collective-permute-done((bf16[4,64,256]{2,1,0:T(8,128)(2,1)S(1)}, bf16[4,64,256]{2,1,0:T(8,128)(2,1)S(1)}, u32[]{:S(2)}, u32[]{:S(2)}) %collective-permute-start.27) | collective-permute-done | bytes 131104 | tf_op jit(solution)/shard_map/ppermute | solution.py:144
  60.6 0.1 fusion.7
  60.7 0.1 shard_map.114
  60.8 1.2 %collective-permute-start.24 = (bf16[400,256]{1,0:T(8,128)(2,1)S(1)}, bf16[400,256]{1,0:T(8,128)(2,1)S(1)}, u32[]{:S(2)}, u32[]{:S(2)}) collective-permute-start(bf16[400,256]{1,0:T(8,128)(2,1)S(1)} %get-tuple-element.98), channel_id=1, source_target_pairs={{0,2},{1,3},{2,0},{3,1},{4,6},{5,7},{6,4},{7,5},{8,10},{9,11},{10,... | collective-permute-start | bytes 614408 | tf_op jit(solution)/shard_map/ppermute | solution.py:144
  62.0 1.5 %collective-permute-start.28 = (bf16[64,256]{1,0:T(8,128)(2,1)S(1)}, bf16[64,256]{1,0:T(8,128)(2,1)S(1)}, u32[]{:S(2)}, u32[]{:S(2)}) collective-permute-start(bf16[64,256]{1,0:T(8,128)(2,1)S(1)} %get-tuple-element.104), channel_id=1, source_target_pairs={{0,8},{4,12},{8,0},{12,4},{16,24},{20,28},{24,16},{28,20},{1,9},{5... | collective-permute-start | bytes 98312 | tf_op jit(solution)/shard_map/ppermute | solution.py:144
  63.5 2.0 %collective-permute-start.29 = (bf16[64,256]{1,0:T(8,128)(2,1)S(1)}, bf16[64,256]{1,0:T(8,128)(2,1)S(1)}, u32[]{:S(2)}, u32[]{:S(2)}) collective-permute-start(bf16[64,256]{1,0:T(8,128)(2,1)S(1)} %get-tuple-element.105), channel_id=1, source_target_pairs={{0,16},{4,20},{8,24},{12,28},{16,0},{20,4},{24,8},{28,12},{1,17},{... | collective-permute-start | bytes 98312 | tf_op jit(solution)/shard_map/ppermute | solution.py:144
  65.5 0.9 %collective-permute-start.30 = (bf16[64,256]{1,0:T(8,128)(2,1)S(1)}, bf16[64,256]{1,0:T(8,128)(2,1)S(1)}, u32[]{:S(2)}, u32[]{:S(2)}) collective-permute-start(bf16[64,256]{1,0:T(8,128)(2,1)S(1)} %get-tuple-element.106), channel_id=1, source_target_pairs={{0,24},{4,28},{8,16},{12,20},{16,8},{20,12},{24,0},{28,4},{1,25},{... | collective-permute-start | bytes 98312 | tf_op jit(solution)/shard_map/ppermute | solution.py:144
  66.4 1.1 %shard_map.115 = bf16[128,512]{1,0:T(8,128)(2,1)} custom-call(bf16[128,512]{1,0:T(8,128)(2,1)S(1)} %bitcast.35, bf16[1024,768]{1,0:T(8,128)(2,1)S(1)} %get-tuple-element.99.windows_ref, bf16[3,512,256]{2,1,0:T(8,128)(2,1)S(1)} %copy-done.1), custom_call_target="tpu_custom_call" | custom-call | flops 20000000000 | bytes 1024 | tf_op jit(solution)/shard_map/pallas_call | solution.py:480
  67.5 1.6 %collective-permute-done.29 = bf16[64,256]{1,0:T(8,128)(2,1)S(1)} collective-permute-done((bf16[64,256]{1,0:T(8,128)(2,1)S(1)}, bf16[64,256]{1,0:T(8,128)(2,1)S(1)}, u32[]{:S(2)}, u32[]{:S(2)}) %collective-permute-start.29) | collective-permute-done | bytes 32800 | tf_op jit(solution)/shard_map/ppermute | solution.py:144
  69.0 2.2 %collective-permute-done.30 = bf16[64,256]{1,0:T(8,128)(2,1)S(1)} collective-permute-done((bf16[64,256]{1,0:T(8,128)(2,1)S(1)}, bf16[64,256]{1,0:T(8,128)(2,1)S(1)}, u32[]{:S(2)}, u32[]{:S(2)}) %collective-permute-start.30) | collective-permute-done | bytes 32800 | tf_op jit(solution)/shard_map/ppermute | solution.py:144
  71.2 0.6 fusion.5
  71.9 0.8 %shard_map.116 = (f32[384,256]{1,0:T(8,128)}, f32[1,2048]{1,0:T(1,128)}) custom-call(f32[384,256]{1,0:T(8,128)S(1)} %get-tuple-element.100.mine_ref, bf16[400,256]{1,0:T(8,128)(2,1)S(1)} %collective-permute-done.24.got_ref, f32[8,256]{1,0:T(8,128)S(1)} %get-tuple-element.102.gain_ref), custom_call_target="tpu_custom_call" | custom-call | bytes 1024 | tf_op jit(solution)/shard_map/pallas_call | solution.py:480
  (39 shorter events, 0.2 us)
Async XLA Ops:
  0.6 0.9 %copy-start.5 = (bf16[1,128,512]{2,1,0:T(8,128)(2,1)S(1)}, bf16[1,128,512]{2,1,0:T(8,128)(2,1)}, u32[]{:S(2)}) copy-start(bf16[1,128,512]{2,1,0:T(8,128)(2,1)} %param.7) | copy-start | bytes 393220
  1.5 1.1 %copy-start = (bf16[3,512,256]{2,1,0:T(8,128)(2,1)S(1)}, bf16[3,512,256]{2,1,0:T(8,128)(2,1)}, u32[]{:S(2)}) copy-start(bf16[3,512,256]{2,1,0:T(8,128)(2,1)} %w_ref.3) | copy-start | bytes 2359300
  1.5 1.1 %copy-start.2 = (s32[1,128,1]{1,2,0:T(1,128)S(1)}, s32[1,128,1]{1,2,0:T(1,128)}, u32[]{:S(2)}) copy-start(s32[1,128,1]{1,2,0:T(1,128)} %param.9) | copy-start | bytes 1540
  1.5 1.1 %copy-start.3 = (s32[1,8]{1,0:T(1,128)S(1)}, s32[1,8]{1,0:T(1,128)}, u32[]{:S(2)}) copy-start(s32[1,8]{1,0:T(1,128)} %param.8) | copy-start | bytes 100
  1.5 9.6 %copy-start.7 = (bf16[256,64]{0,1:T(8,128)(2,1)S(1)}, bf16[256,64]{0,1:T(8,128)(2,1)}, u32[]{:S(2)}) copy-start(bf16[256,64]{0,1:T(8,128)(2,1)} %param.11) | copy-start | bytes 98308
  3.6 12.1 %collective-permute-start = (bf16[512,128]{1,0:T(8,128)(2,1)S(1)}, bf16[512,128]{1,0:T(8,128)(2,1)S(1)}, u32[]{:S(2)}, u32[]{:S(2)}) collective-permute-start(bf16[512,128]{1,0:T(8,128)(2,1)S(1)} %get-tuple-element.59), channel_id=1, source_target_pairs={{0,16},{4,20},{8,24},{12,28},{16,0},{20,4},{24,8},{28,12},{1,17},{... | collective-permute-start | bytes 393224 | tf_op jit(solution)/shard_map/ppermute | solution.py:144
  7.7 7.9 %collective-permute-start.1 = (f32[8,256]{1,0:T(8,128)S(1)}, f32[8,256]{1,0:T(8,128)S(1)}, u32[]{:S(2)}, u32[]{:S(2)}) collective-permute-start(f32[8,256]{1,0:T(8,128)S(1)} %get-tuple-element.61), channel_id=1, source_target_pairs={{0,4},{4,8},{8,12},{12,16},{16,20},{20,24},{24,28},{1,5},{5,9},{9,... | collective-permute-start | bytes 24584 | tf_op jit(solution)/shard_map/ppermute | solution.py:20
  11.1 7.8 %collective-permute-start.6 = (bf16[64,256]{1,0:T(8,128)(2,1)S(1)}, bf16[64,256]{1,0:T(8,128)(2,1)S(1)}, u32[]{:S(2)}, u32[]{:S(2)}) collective-permute-start(bf16[64,256]{1,0:T(8,128)(2,1)S(1)} %bitcast.36), channel_id=1, source_target_pairs={{0,8},{4,12},{8,0},{12,4},{16,24},{20,28},{24,16},{28,20},{1,9},{5... | collective-permute-start | bytes 98312 | tf_op jit(solution)/shard_map/ppermute | solution.py:144
  12.8 8.1 %collective-permute-start.7 = (bf16[64,256]{1,0:T(8,128)(2,1)S(1)}, bf16[64,256]{1,0:T(8,128)(2,1)S(1)}, u32[]{:S(2)}, u32[]{:S(2)}) collective-permute-start(bf16[64,256]{1,0:T(8,128)(2,1)S(1)} %bitcast.37), channel_id=1, source_target_pairs={{0,16},{4,20},{8,24},{12,28},{16,0},{20,4},{24,8},{28,12},{1,17},{... | collective-permute-start | bytes 98312 | tf_op jit(solution)/shard_map/ppermute | solution.py:144
  13.1 7.8 %collective-permute-start.8 = (bf16[64,256]{1,0:T(8,128)(2,1)S(1)}, bf16[64,256]{1,0:T(8,128)(2,1)S(1)}, u32[]{:S(2)}, u32[]{:S(2)}) collective-permute-start(bf16[64,256]{1,0:T(8,128)(2,1)S(1)} %bitcast.38), channel_id=1, source_target_pairs={{0,24},{4,28},{8,16},{12,20},{16,8},{20,12},{24,0},{28,4},{1,25},{... | collective-permute-start | bytes 98312 | tf_op jit(solution)/shard_map/ppermute | solution.py:144
  15.8 5.1 %collective-permute-start.2 = (bf16[64,256]{1,0:T(8,128)(2,1)S(1)}, bf16[64,256]{1,0:T(8,128)(2,1)S(1)}, u32[]{:S(2)}, u32[]{:S(2)}) collective-permute-start(bf16[64,256]{1,0:T(8,128)(2,1)S(1)} %get-tuple-element.69), channel_id=1, source_target_pairs={{0,8},{4,12},{8,0},{12,4},{16,24},{20,28},{24,16},{28,20},{1,9},{5... | collective-permute-start | bytes 98312 | tf_op jit(solution)/shard_map/ppermute | solution.py:144
  16.5 5.2 %collective-permute-start.3 = (bf16[64,256]{1,0:T(8,128)(2,1)S(1)}, bf16[64,256]{1,0:T(8,128)(2,1)S(1)}, u32[]{:S(2)}, u32[]{:S(2)}) collective-permute-start(bf16[64,256]{1,0:T(8,128)(2,1)S(1)} %get-tuple-element.70), channel_id=1, source_target_pairs={{0,16},{4,20},{8,24},{12,28},{16,0},{20,4},{24,8},{28,12},{1,17},{... | collective-permute-start | bytes 98312 | tf_op jit(solution)/shard_map/ppermute | solution.py:144
  18.9 10.7 %collective-permute-start.12 = (bf16[2,512,128]{2,1,0:T(8,128)(2,1)S(1)}, bf16[2,512,128]{2,1,0:T(8,128)(2,1)S(1)}, u32[]{:S(2)}, u32[]{:S(2)}) collective-permute-start(bf16[2,512,128]{2,1,0:T(8,128)(2,1)S(1)} %pad_maximum_fusion), channel_id=1, source_target_pairs={{0,8},{4,12},{8,0},{12,4},{16,24},{20,28},{24,16},{28,20},{1,9},{5... | collective-permute-start | bytes 786440 | tf_op jit(solution)/shard_map/ppermute | solution.py:144
  21.7 7.2 %collective-permute-start.10 = (bf16[256,256]{1,0:T(8,128)(2,1)S(1)}, bf16[256,256]{1,0:T(8,128)(2,1)S(1)}, u32[]{:S(2)}, u32[]{:S(2)}) collective-permute-start(bf16[256,256]{1,0:T(8,128)(2,1)S(1)} %shard_map.106.refs_5_), channel_id=1, source_target_pairs={{0,2},{1,3},{2,0},{3,1},{4,6},{5,7},{6,4},{7,5},{8,10},{9,11},{10,... | collective-permute-start | bytes 393224 | tf_op jit(solution)/shard_map/ppermute | solution.py:144
  23.3 5.9 %collective-permute-start.11 = (bf16[256,256]{1,0:T(8,128)(2,1)S(1)}, bf16[256,256]{1,0:T(8,128)(2,1)S(1)}, u32[]{:S(2)}, u32[]{:S(2)}) collective-permute-start(bf16[256,256]{1,0:T(8,128)(2,1)S(1)} %shard_map.106.refs_5_), channel_id=1, source_target_pairs={{0,6},{1,7},{2,4},{3,5},{4,2},{5,3},{6,0},{7,1},{8,14},{9,15},{10,... | collective-permute-start | bytes 393224 | tf_op jit(solution)/shard_map/ppermute | solution.py:144
  23.9 5.7 %collective-permute-start.9 = (bf16[256,256]{1,0:T(8,128)(2,1)S(1)}, bf16[256,256]{1,0:T(8,128)(2,1)S(1)}, u32[]{:S(2)}, u32[]{:S(2)}) collective-permute-start(bf16[256,256]{1,0:T(8,128)(2,1)S(1)} %shard_map.106.refs_5_), channel_id=1, source_target_pairs={{0,4},{4,0},{8,12},{12,8},{16,20},{20,16},{24,28},{28,24},{1,5},{5... | collective-permute-start | bytes 393224 | tf_op jit(solution)/shard_map/ppermute | solution.py:144
  25.3 5.8 %collective-permute-start.4 = (bf16[64,256]{1,0:T(8,128)(2,1)S(1)}, bf16[64,256]{1,0:T(8,128)(2,1)S(1)}, u32[]{:S(2)}, u32[]{:S(2)}) collective-permute-start(bf16[64,256]{1,0:T(8,128)(2,1)S(1)} %get-tuple-element.71), channel_id=1, source_target_pairs={{0,24},{4,28},{8,16},{12,20},{16,8},{20,12},{24,0},{28,4},{1,25},{... | collective-permute-start | bytes 98312 | tf_op jit(solution)/shard_map/ppermute | solution.py:144
  28.9 7.6 %copy-start.4 = (bf16[1,136,2048]{2,1,0:T(8,128)(2,1)S(1)}, bf16[1,136,2048]{2,1,0:T(8,128)(2,1)}, u32[]{:S(2)}) copy-start(bf16[1,136,2048]{2,1,0:T(8,128)(2,1)} %param.13) | copy-start | bytes 1671172
  28.9 7.6 %copy-start.8 = (f32[2048]{0:T(1024)S(1)}, f32[2048]{0:T(1024)}, u32[]{:S(2)}) copy-start(f32[2048]{0:T(1024)} %param.12) | copy-start | bytes 24580
  29.6 6.8 %collective-permute-start.13 = (bf16[256,256]{1,0:T(8,128)(2,1)S(1)}, bf16[256,256]{1,0:T(8,128)(2,1)S(1)}, u32[]{:S(2)}, u32[]{:S(2)}) collective-permute-start(bf16[256,256]{1,0:T(8,128)(2,1)S(1)} %shard_map.106.refs_5_), channel_id=1, source_target_pairs={{0,1},{1,0},{2,3},{3,2},{4,5},{5,4},{6,7},{7,6},{8,9},{9,8},{10,11... | collective-permute-start | bytes 393224 | tf_op jit(solution)/shard_map/ppermute | solution.py:144
  29.6 6.8 %collective-permute-start.14 = (bf16[256,256]{1,0:T(8,128)(2,1)S(1)}, bf16[256,256]{1,0:T(8,128)(2,1)S(1)}, u32[]{:S(2)}, u32[]{:S(2)}) collective-permute-start(bf16[256,256]{1,0:T(8,128)(2,1)S(1)} %collective-permute-done.9.refs_6_), channel_id=1, source_target_pairs={{0,1},{1,0},{2,3},{3,2},{4,5},{5,4},{6,7},{7,6},{8,9},{9,8},{10,11... | collective-permute-start | bytes 393224 | tf_op jit(solution)/shard_map/ppermute | solution.py:144
  30.2 6.3 %collective-permute-start.15 = (bf16[256,256]{1,0:T(8,128)(2,1)S(1)}, bf16[256,256]{1,0:T(8,128)(2,1)S(1)}, u32[]{:S(2)}, u32[]{:S(2)}) collective-permute-start(bf16[256,256]{1,0:T(8,128)(2,1)S(1)} %collective-permute-done.10.refs_7_), channel_id=1, source_target_pairs={{0,1},{1,0},{2,3},{3,2},{4,5},{5,4},{6,7},{7,6},{8,9},{9,8},{10,11... | collective-permute-start | bytes 393224 | tf_op jit(solution)/shard_map/ppermute | solution.py:144
  30.2 6.3 %collective-permute-start.16 = (bf16[256,256]{1,0:T(8,128)(2,1)S(1)}, bf16[256,256]{1,0:T(8,128)(2,1)S(1)}, u32[]{:S(2)}, u32[]{:S(2)}) collective-permute-start(bf16[256,256]{1,0:T(8,128)(2,1)S(1)} %collective-permute-done.11.refs_8_), channel_id=1, source_target_pairs={{0,1},{1,0},{2,3},{3,2},{4,5},{5,4},{6,7},{7,6},{8,9},{9,8},{10,11... | collective-permute-start | bytes 393224 | tf_op jit(solution)/shard_map/ppermute | solution.py:144
  31.1 4.3 %collective-permute-start.5 = (bf16[128,256]{1,0:T(8,128)(2,1)S(1)}, bf16[128,256]{1,0:T(8,128)(2,1)S(1)}, u32[]{:S(2)}, u32[]{:S(2)}) collective-permute-start(bf16[128,256]{1,0:T(8,128)(2,1)S(1)} %shard_map.105), channel_id=1, source_target_pairs={{0,4},{4,0},{8,12},{12,8},{16,20},{20,16},{24,28},{28,24},{1,5},{5... | collective-permute-start | bytes 196616 | tf_op jit(solution)/shard_map/ppermute | solution.py:144
  35.4 17.4 %collective-permute-start.21 = (bf16[4,512,128]{2,1,0:T(8,128)(2,1)S(1)}, bf16[4,512,128]{2,1,0:T(8,128)(2,1)S(1)}, u32[]{:S(2)}, u32[]{:S(2)}) collective-permute-start(bf16[4,512,128]{2,1,0:T(8,128)(2,1)S(1)} %constant_dynamic-update-slice_fusion.refs_0_), channel_id=1, source_target_pairs={{0,4},{4,0},{8,12},{12,8},{16,20},{20,16},{24,28},{28,24},{1,5},{5... | collective-permute-start | bytes 1572872 | tf_op jit(solution)/shard_map/ppermute | solution.py:144
  37.7 6.3 %collective-permute-start.17 = (bf16[144,256]{1,0:T(8,128)(2,1)S(1)}, bf16[144,256]{1,0:T(8,128)(2,1)S(1)}, u32[]{:S(2)}, u32[]{:S(2)}) collective-permute-start(bf16[144,256]{1,0:T(8,128)(2,1)S(1)} %get-tuple-element.82.refs_0_), channel_id=1, source_target_pairs={{0,8},{4,12},{8,0},{12,4},{16,24},{20,28},{24,16},{28,20},{1,9},{5... | collective-permute-start | bytes 221192 | tf_op jit(solution)/shard_map/ppermute | solution.py:144
  39.2 6.7 %collective-permute-start.18 = (bf16[144,256]{1,0:T(8,128)(2,1)S(1)}, bf16[144,256]{1,0:T(8,128)(2,1)S(1)}, u32[]{:S(2)}, u32[]{:S(2)}) collective-permute-start(bf16[144,256]{1,0:T(8,128)(2,1)S(1)} %get-tuple-element.82.refs_0_), channel_id=1, source_target_pairs={{0,16},{4,20},{8,24},{12,28},{16,0},{20,4},{24,8},{28,12},{1,17},{... | collective-permute-start | bytes 221192 | tf_op jit(solution)/shard_map/ppermute | solution.py:144
  41.1 6.3 %collective-permute-start.19 = (bf16[144,256]{1,0:T(8,128)(2,1)S(1)}, bf16[144,256]{1,0:T(8,128)(2,1)S(1)}, u32[]{:S(2)}, u32[]{:S(2)}) collective-permute-start(bf16[144,256]{1,0:T(8,128)(2,1)S(1)} %get-tuple-element.82.refs_0_), channel_id=1, source_target_pairs={{0,24},{4,28},{8,16},{12,20},{16,8},{20,12},{24,0},{28,4},{1,25},{... | collective-permute-start | bytes 221192 | tf_op jit(solution)/shard_map/ppermute | solution.py:144
  42.7 6.3 %collective-permute-start.22 = (bf16[16,64,256]{2,1,0:T(8,128)(2,1)S(1)}, bf16[16,64,256]{2,1,0:T(8,128)(2,1)S(1)}, u32[]{:S(2)}, u32[]{:S(2)}) collective-permute-start(bf16[16,64,256]{2,1,0:T(8,128)(2,1)S(1)} %get-tuple-element.87), channel_id=1, source_target_pairs={{0,1},{1,0},{2,3},{3,2},{4,5},{5,4},{6,7},{7,6},{8,9},{9,8},{10,11... | collective-permute-start | bytes 1572872 | tf_op jit(solution)/shard_map/ppermute | solution.py:144
  47.4 9.4 %collective-permute-start.20 = (bf16[576,256]{1,0:T(8,128)(2,1)S(1)}, bf16[576,256]{1,0:T(8,128)(2,1)S(1)}, u32[]{:S(2)}, u32[]{:S(2)}) collective-permute-start(bf16[576,256]{1,0:T(8,128)(2,1)S(1)} %shard_map.108), channel_id=1, source_target_pairs={{0,4},{4,0},{8,12},{12,8},{16,20},{20,16},{24,28},{28,24},{1,5},{5... | collective-permute-start | bytes 884744 | tf_op jit(solution)/shard_map/ppermute | solution.py:144
  49.2 10.0 %collective-permute-start.25 = (bf16[4,64,256]{2,1,0:T(8,128)(2,1)S(1)}, bf16[4,64,256]{2,1,0:T(8,128)(2,1)S(1)}, u32[]{:S(2)}, u32[]{:S(2)}) collective-permute-start(bf16[4,64,256]{2,1,0:T(8,128)(2,1)S(1)} %get-tuple-element.114), channel_id=1, source_target_pairs={{0,4},{4,0},{8,12},{12,8},{16,20},{20,16},{24,28},{28,24},{1,5},{5... | collective-permute-start | bytes 393224 | tf_op jit(solution)/shard_map/ppermute | solution.py:144
  49.8 9.5 %collective-permute-start.26 = (bf16[4,64,256]{2,1,0:T(8,128)(2,1)S(1)}, bf16[4,64,256]{2,1,0:T(8,128)(2,1)S(1)}, u32[]{:S(2)}, u32[]{:S(2)}) collective-permute-start(bf16[4,64,256]{2,1,0:T(8,128)(2,1)S(1)} %get-tuple-element.113), channel_id=1, source_target_pairs={{0,2},{1,3},{2,0},{3,1},{4,6},{5,7},{6,4},{7,5},{8,10},{9,11},{10,... | collective-permute-start | bytes 393224 | tf_op jit(solution)/shard_map/ppermute | solution.py:144
  51.3 9.3 %collective-permute-start.27 = (bf16[4,64,256]{2,1,0:T(8,128)(2,1)S(1)}, bf16[4,64,256]{2,1,0:T(8,128)(2,1)S(1)}, u32[]{:S(2)}, u32[]{:S(2)}) collective-permute-start(bf16[4,64,256]{2,1,0:T(8,128)(2,1)S(1)} %get-tuple-element.112), channel_id=1, source_target_pairs={{0,6},{1,7},{2,4},{3,5},{4,2},{5,3},{6,0},{7,1},{8,14},{9,15},{10,... | collective-permute-start | bytes 393224 | tf_op jit(solution)/shard_map/ppermute | solution.py:144
  58.5 2.1 %collective-permute-start.23 = (bf16[784,256]{1,0:T(8,128)(2,1)S(1)}, bf16[784,256]{1,0:T(8,128)(2,1)S(1)}, u32[]{:S(2)}, u32[]{:S(2)}) collective-permute-start(bf16[784,256]{1,0:T(8,128)(2,1)S(1)} %get-tuple-element.96), channel_id=1, source_target_pairs={{0,1},{1,0},{2,3},{3,2},{4,5},{5,4},{6,7},{7,6},{8,9},{9,8},{10,11... | collective-permute-start | bytes 1204232 | tf_op jit(solution)/shard_map/ppermute | solution.py:144
  59.2 7.2 %copy-start.1 = (bf16[3,512,256]{2,1,0:T(8,128)(2,1)S(1)}, bf16[3,512,256]{2,1,0:T(8,128)(2,1)}, u32[]{:S(2)}) copy-start(bf16[3,512,256]{2,1,0:T(8,128)(2,1)} %w_ref.3) | copy-start | bytes 2359300
  59.2 7.2 %copy-start.6 = (bf16[1,128,512]{2,1,0:T(8,128)(2,1)S(1)}, bf16[1,128,512]{2,1,0:T(8,128)(2,1)}, u32[]{:S(2)}) copy-start(bf16[1,128,512]{2,1,0:T(8,128)(2,1)} %param.7) | copy-start | bytes 393220
  60.8 11.1 %collective-permute-start.24 = (bf16[400,256]{1,0:T(8,128)(2,1)S(1)}, bf16[400,256]{1,0:T(8,128)(2,1)S(1)}, u32[]{:S(2)}, u32[]{:S(2)}) collective-permute-start(bf16[400,256]{1,0:T(8,128)(2,1)S(1)} %get-tuple-element.98), channel_id=1, source_target_pairs={{0,2},{1,3},{2,0},{3,1},{4,6},{5,7},{6,4},{7,5},{8,10},{9,11},{10,... | collective-permute-start | bytes 614408 | tf_op jit(solution)/shard_map/ppermute | solution.py:144
  62.0 5.4 %collective-permute-start.28 = (bf16[64,256]{1,0:T(8,128)(2,1)S(1)}, bf16[64,256]{1,0:T(8,128)(2,1)S(1)}, u32[]{:S(2)}, u32[]{:S(2)}) collective-permute-start(bf16[64,256]{1,0:T(8,128)(2,1)S(1)} %get-tuple-element.104), channel_id=1, source_target_pairs={{0,8},{4,12},{8,0},{12,4},{16,24},{20,28},{24,16},{28,20},{1,9},{5... | collective-permute-start | bytes 98312 | tf_op jit(solution)/shard_map/ppermute | solution.py:144
  63.5 5.5 %collective-permute-start.29 = (bf16[64,256]{1,0:T(8,128)(2,1)S(1)}, bf16[64,256]{1,0:T(8,128)(2,1)S(1)}, u32[]{:S(2)}, u32[]{:S(2)}) collective-permute-start(bf16[64,256]{1,0:T(8,128)(2,1)S(1)} %get-tuple-element.105), channel_id=1, source_target_pairs={{0,16},{4,20},{8,24},{12,28},{16,0},{20,4},{24,8},{28,12},{1,17},{... | collective-permute-start | bytes 98312 | tf_op jit(solution)/shard_map/ppermute | solution.py:144
  65.5 5.7 %collective-permute-start.30 = (bf16[64,256]{1,0:T(8,128)(2,1)S(1)}, bf16[64,256]{1,0:T(8,128)(2,1)S(1)}, u32[]{:S(2)}, u32[]{:S(2)}) collective-permute-start(bf16[64,256]{1,0:T(8,128)(2,1)S(1)} %get-tuple-element.106), channel_id=1, source_target_pairs={{0,24},{4,28},{8,16},{12,20},{16,8},{20,12},{24,0},{28,4},{1,25},{... | collective-permute-start | bytes 98312 | tf_op jit(solution)/shard_map/ppermute | solution.py:144

commit v4 on v3

--- a/solution.py
+++ b/solution.py
@@ -197,27 +197,29 @@
     turned_ref[...] = act.T.astype(BF16)
 
 
-def encode_kernel(
-    piece, lengths_ref, padded, owner_ref, w_ref, total_ref, placed_ref, edge_ref, named_ref
-):
-    frames = total_ref.shape[0]
+def collect_kernel(plan, *refs):
+    out_ref, at = refs[-1], 0
+    for index, start, rows in plan:
+        out_ref[at : at + rows, :] = refs[index][start : start + rows, :]
+        at += rows
+
+
+def encode_kernel(piece, lengths_ref, padded, owner_ref, w_ref, out_ref, extra):
+    frames, latent_width = owner_ref.shape[1], out_ref.shape[1]
     taps = w_ref.shape[0]
+    edges = taps - 1
     me = lax.axis_index("seq")
-    seq_count = placed_ref.shape[0] // piece
+    seq_count = out_ref.shape[0] // piece
     owner = owner_ref[...]
     rank = ranks_of(owner, seq_count).astype(jnp.int32)
     row = jnp.bitwise_xor(owner, me) * piece + rank
-    placed_ref[...] = (iota((seq_count * piece, frames), 0) == row).astype(F32).astype(BF16)
-    named = owner.astype(F32)
-    if named_ref.shape[1] > frames:
-        named = jnp.concatenate([named, jnp.zeros((1, named_ref.shape[1] - frames), F32)], axis=1)
-    named_ref[...] = named
+    placed = (iota((seq_count * piece, frames), 0) == row).astype(F32).astype(BF16)
     position = me * frames + iota((frames, 1), 0)
     start_of = start_below(position, lengths_ref)
     beyond = (me + 1) * frames + iota((16, 1), 0)
     start_beyond = start_below(beyond, lengths_ref)
-    total = jnp.zeros(total_ref.shape, F32)
-    edge = jnp.zeros((16, total.shape[1]), F32)
+    total = jnp.zeros((frames, latent_width), F32)
+    edge = jnp.zeros((16, latent_width), F32)
     for tap in range(taps):
         window = padded[8 - tap : 8 - tap + frames, :]
         window = jnp.where(position - tap >= start_of, window, 0.0).astype(BF16)
@@ -226,20 +228,19 @@
             window = padded[8 + frames - tap : 24 + frames - tap, :]
             window = jnp.where(beyond - tap >= start_beyond, window, 0.0).astype(BF16)
             edge = edge + jnp.dot(window, w_ref[tap], preferred_element_type=F32)
-    total_ref[...] = total
-    edge_ref[...] = edge[: edge_ref.shape[0]]
-
-
-def place_kernel(piece, total_ref, edge_ref, placed_ref, named_ref, *out_refs):
-    seq_count = 2 * len(out_refs)
-    lines = edge_ref.shape[0]
-    total = total_ref[...]
-    latent = jnp.concatenate([total[:lines] + edge_ref[...], total[lines:]], axis=0).astype(BF16)
-    outgoing = jnp.dot(placed_ref[...], latent, preferred_element_type=F32)
-    last = iota((seq_count * piece, 1), 0) % piece == piece - 1
-    outgoing = jnp.where(last, named_ref[...], outgoing).astype(BF16)
-    for far, out_ref in enumerate(out_refs):
-        out_ref[...] = outgoing[2 * far * piece : 2 * (far + 1) * piece]
+    latent = total.astype(BF16)
+    outgoing = jnp.dot(placed, latent, preferred_element_type=F32)
+    first, edge = total[:edges], edge[:edges]
+    high = edge.astype(BF16).astype(F32)
+    extra[...] = jnp.zeros_like(extra)
+    at = piece - 1 - 3 * edges
+    extra[at : at + edges, :] = first - latent[:8].astype(F32)[:edges]
+    extra[at + edges : at + 2 * edges, :] = high
+    extra[at + 2 * edges : at + 3 * edges, :] = edge - high
+    extra[piece - 1 : piece, 0:frames] = owner.astype(F32)
+    for rel in range(seq_count):
+        here = slice(rel * piece, (rel + 1) * piece)
+        out_ref[here, :] = (outgoing[here] + extra[...]).astype(BF16)
 
 
 def join_rows_kernel(skip, *refs):
@@ -248,21 +249,14 @@
         refs[-1][index * rows : (index + 1) * rows, :] = ref[skip:, :]
 
 
-def middle_kernel(piece, capacity, frames, count, columns, *refs):
+def middle_kernel(piece, capacity, frames, count, columns, edges, *refs):
     far_count = count // 2
-    landed, near = refs[:far_count], refs[far_count]
-    w_refs = refs[far_count + 1 : far_count + 9]
-    gain_ref, cot_ref, back_ref, hg_ref, arrived_ref, owners_ref = refs[far_count + 9 : far_count + 15]
-    gathered, w_full, hidden, back = refs[far_count + 15 :]
+    gathered, w_refs = refs[0], refs[1:9]
+    gain_ref, cot_ref, back_ref, hg_ref, arrived_ref, owners_ref, w_full, hidden, back = refs[9:]
     slots, width = cot_ref.shape
     rows = back_ref.shape[0]
     latent_width = back_ref.shape[1]
     seq, book = lax.axis_index("seq"), lax.axis_index("book")
-    for far in range(far_count):
-        gathered[2 * far * piece : (2 * far + 1) * piece, :] = landed[far][0:piece, :]
-        gathered[(2 * far + 1) * piece : (2 * far + 2) * piece, :] = near[
-            far * piece : (far + 1) * piece, :
-        ]
     for rel in range(count):
         line = gathered[rel * piece : (rel + 1) * piece, 0:frames].astype(F32)
         owners_ref[pl.ds(jnp.bitwise_xor(seq, rel), 1), :] = line[piece - 1 : piece, :]
@@ -279,9 +273,25 @@
     source = jnp.zeros_like(slot)
     for block in range(1, count):
         source = source + (slot >= block * capacity).astype(jnp.int32)
-    wanted = jnp.bitwise_xor(source, seq) * piece + slot - source * capacity
-    wanted = jnp.where(slot < slots, wanted, -1)
-    picked = (iota((rows, count * piece), 1) == wanted).astype(F32).astype(BF16)
+    place = slot - source * capacity
+    base = jnp.bitwise_xor(source, seq) * piece
+    before = jnp.bitwise_xor(source - 1, seq) * piece
+    column = iota((rows, count * piece), 1)
+    picked = column == jnp.where(slot < slots, base + place, -1)
+    taken = jnp.zeros_like(slot)
+    at = piece - 1 - 3 * edges
+    for edge in range(edges):
+        owner = jnp.zeros((rows, 1), F32)
+        for block in range(count):
+            owner = jnp.where(source == block, owners_ref[block : block + 1, edge : edge + 1], owner)
+        mine = (owner == seq.astype(F32)) & (slot < slots)
+        here = mine & (place == taken)
+        taken = taken + mine.astype(jnp.int32)
+        rest = jnp.where(here, base + at + edge, -1)
+        share = jnp.where(here & (source > 0), before + at + edges + edge, -1)
+        share_rest = jnp.where(share >= 0, share + edges, -1)
+        picked = picked | (column == rest) | (column == share) | (column == share_rest)
+    picked = picked.astype(F32).astype(BF16)
     arrived = jnp.dot(picked, gathered[...], preferred_element_type=F32).astype(BF16)
     arrived_ref[...] = arrived
     step = latent_width
@@ -366,16 +376,16 @@
 
 
 def spread_kernel(count, frames, taps, *refs):
-    backs = refs[: count // 2 + 1]
+    backs = refs[: count // 2 + 2]
     lines_ref, facts_ref, send_ref, windows_ref, gain_ref, gathered, wide = refs[len(backs) :]
     rows, latent_width = backs[0].shape
     share = lines_ref.shape[0] // 2
     gain_rows = gain_ref.shape[0]
     gain = jnp.zeros((gain_rows, latent_width), F32)
-    for far, back_ref in enumerate(backs[:-1]):
-        gathered[far * rows : (far + 1) * rows, :] = back_ref[...]
-    far_count = count // 2
-    gathered[far_count * rows :, :] = backs[-1][...]
+    at = 0
+    for back_ref in backs:
+        gathered[at : at + back_ref.shape[0], :] = back_ref[...]
+        at += back_ref.shape[0]
     for rel in range(count):
         gain = gain + gathered[rel * rows : (rel + 1) * rows, :].astype(F32)[rows - gain_rows :]
     gain_ref[...] = gain
@@ -488,6 +498,23 @@
     )(*operands)
 
 
+def collect(blocks, flops=0):
+    arrays, plan = [], []
+    for array, start, rows in blocks:
+        found = [i for i, known in enumerate(arrays) if known is array]
+        if not found:
+            arrays.append(array)
+        plan.append((found[0] if found else len(arrays) - 1, start, rows))
+    total = sum(rows for _, _, rows in plan)
+    (out,) = call(
+        functools.partial(collect_kernel, tuple(plan)),
+        [shape((total, arrays[0].shape[1]), arrays[0].dtype)],
+        tuple(arrays),
+        flops=flops,
+    )
+    return out
+
+
 def shape(dims, dtype=BF16):
     return jax.ShapeDtypeStruct(dims, dtype)
 
@@ -503,7 +530,7 @@
     far_count = count // 2
     fars = range(1, far_count)
     capacity = max(2, frames // count + 1)
-    piece = round_up(capacity + 1, 16)
+    piece = round_up(capacity + 1 + 3 * (taps - 1), 16)
     gain_rows = width // latent_width
     rows = round_up(slots + gain_rows, 16)
     half = channels // 4
@@ -515,65 +542,64 @@
         (feats,),
         flops=HEAVY // 10,
     )
-    total, placed, edge, named = call(
+    (sent,) = call(
         functools.partial(encode_kernel, piece),
-        [
-            shape((frames, latent_width), F32),
-            shape((count * piece, frames)),
-            shape((8, latent_width), F32),
-            shape((1, latent_width), F32),
-        ],
+        [shape((count * piece, latent_width))],
         (book_lengths, padded, owner[0].T, w_enc),
+        scratch=[pltpu.VMEM((piece, latent_width), F32)],
         smem=1,
     )
-    w_own, edge, turned = lax.optimization_barrier((w_in.T, edge, turned))
-    edge = shifted(edge, "seq", 1)
-    w_far = [w_own] + [swap(w_own, "seq", 2 * far) for far in fars]
-    held = jnp.stack([turned, swap(turned, "seq", 4)])
-    sent = call(
-        functools.partial(place_kernel, piece),
-        [shape((2 * piece, latent_width))] * far_count,
-        (total, edge, placed, named),
-    )
-    held, sent = lax.optimization_barrier((held, sent))
-    landed = [sent[0]] + [swap(sent[far], "seq", 2 * far) for far in fars]
-    w_far = after(w_far, landed[1], landed[2])
-    (w_line,) = call(
-        functools.partial(join_rows_kernel, 0),
-        [shape((far_count * columns, latent_width))],
-        tuple(w_far),
-        flops=HEAVY,
-    )
-    w_near = swap(w_line, "seq", 1)
+    pieces = {0: {far: (sent, 2 * far * piece, 2 * piece) for far in range(far_count)}}
+    w_blocks = {0: (w_in.T, 0, columns)}
+    held, order, mask = turned[None], [0], far_count // 2
+    w_got = None
+    while mask:
+        sources = sorted(pieces)
+        owners = [far for far in range(far_count) if far in pieces[0] and far & mask]
+        message = [w_blocks[far] for far in sources]
+        message += [pieces[source][far] for source in sources for far in owners]
+        w_got = swap(collect(message), "seq", 2 * mask)
+        at = 0
+        for source in sources:
+            w_blocks[source ^ mask] = (w_got, at, columns)
+            at += columns
+        for source in sources:
+            pieces[source ^ mask] = {}
+            for far in owners:
+                pieces[source ^ mask][far ^ mask] = (w_got, at, 2 * piece)
+                at += 2 * piece
+                del pieces[source][far]
+        held = after(held, w_got)
+        got = swap(held, "seq", 2 * mask)
+        held = jnp.concatenate([held, got])
+        order = order + [far ^ mask for far in order]
+        mask //= 2
+    fars_of_w = [w_blocks[far] for far in range(far_count)]
+    near = [pieces[far][0] for far in range(far_count)]
+    x_send = collect(fars_of_w + [(array, at + piece, piece) for array, at, _ in near])
+    w_line = collect(fars_of_w, flops=HEAVY)
+    x_got = swap(x_send, "seq", 1)
     w_side = swap(w_line, "book", 2)
     w_diag = swap(w_line, ("seq", "book"), 4 + 2)
-    got = swap(held, "seq", 2)
-    (near,) = call(
-        functools.partial(join_rows_kernel, piece),
-        [shape((far_count * piece, latent_width))],
-        tuple(landed),
-        flops=HEAVY,
-    )
-    near = swap(near, "seq", 1)
-    w_chips = [w_line, w_near, w_side, w_diag]
-    w_chips, got = lax.optimization_barrier((w_chips, got))
-    held = jnp.concatenate([held, got])
+    w_chips = [w_line, x_got, w_side, w_diag]
     w_pieces = w_chips + [swap(block, "book", 1) for block in w_chips]
-    second = swap(held, "seq", 1)
-    turned_all = [held, second]
-    orders = [[0, 4, 2, 6], [1, 5, 3, 7]]
+    turned_all = [held, swap(held, "seq", 1)]
+    orders = [[2 * far for far in order], [2 * far + 1 for far in order]]
+    gathered = []
+    for far, (array, at, _) in enumerate(near):
+        gathered += [(array, at, piece), (x_got, far_count * columns + far * piece, piece)]
+    gathered = collect(gathered)
 
     back, hidden_grad, arrived, owners = call(
-        functools.partial(middle_kernel, piece, capacity, frames, count, columns),
+        functools.partial(middle_kernel, piece, capacity, frames, count, columns, taps - 1),
         [
             shape((rows, latent_width)),
             shape((rows, width)),
             shape((rows, latent_width)),
             shape((count, frames), F32),
         ],
-        (*landed, near, *w_pieces, gain[None], cot),
+        (gathered, *w_pieces, gain[None], cot),
         scratch=[
-            pltpu.VMEM((count * piece, latent_width), BF16),
             pltpu.VMEM((width, latent_width), BF16),
             pltpu.VMEM((slots, width), F32),
             pltpu.VMEM((rows, latent_width), F32),
@@ -581,13 +607,11 @@
         flops=HEAVY,
     )
     backs = [back] + [swap(back, "seq", 2 * far) for far in fars]
-    (near_backs,) = call(
-        functools.partial(join_rows_kernel, 0),
-        [shape((far_count * rows, latent_width))],
-        tuple(backs),
-        flops=HEAVY,
-    )
-    near_backs = swap(near_backs, "seq", 1)
+    half_far = far_count // 2
+    near_backs = []
+    for at in range(0, far_count, half_far):
+        joined = collect([(block, 0, rows) for block in backs[at : at + half_far]], flops=HEAVY)
+        near_backs.append(swap(joined, "seq", 1))
 
     (facts,) = call(
         functools.partial(prepare_kernel, capacity, rows),
@@ -604,9 +628,9 @@
     w_got, facts = lax.optimization_barrier((swap(w_send, "book", 1), facts))
     w_sum = w_keep.astype(F32) + w_got.astype(F32)
     w_parts = [w_sum[at : at + far_count].astype(BF16) for at in range(0, 2 * count, far_count)]
-    w_sum = w_sum[:far_count] + swap(w_parts[1], "seq", 1).astype(F32)
-    w_sum = w_sum + swap(w_parts[2], "book", 2).astype(F32)
-    w_sum = w_sum + swap(w_parts[3], ("seq", "book"), 4 + 2).astype(F32)
+    w_x = swap(w_parts[1], "seq", 1)
+    w_y = swap(w_parts[2], "book", 2)
+    w_d = swap(w_parts[3], ("seq", "book"), 4 + 2)
     own_lines, sent_lines = call(
         functools.partial(channel_kernel, orders),
         [shape((2 * half, count * frames))] * 2,
@@ -621,7 +645,7 @@
             shape((count * frames, taps * latent_width)),
             shape((gain_rows, latent_width), F32),
         ],
-        (*backs, near_backs, sent_lines, facts),
+        (*backs, *near_backs, sent_lines, facts),
         scratch=[
             pltpu.VMEM((count * rows, latent_width), BF16),
             pltpu.VMEM((count * frames + 8, latent_width), F32),
@@ -645,11 +669,11 @@
         (k_kept, k_got, gain_seq),
     )
     y_got = swap(y_send, "book", 2)
+    w_x, w_y, w_d = after((w_x, w_y, w_d), y_send)
+    w_sum = w_sum[:far_count] + w_x.astype(F32) + w_y.astype(F32) + w_d.astype(F32)
     w_far = [w_sum[far].astype(BF16) for far in fars]
-    w_far = [after(block, k_send) for block in w_far[:0]] + [after(block, y_send) for block in w_far[0:]]
     w_total = w_sum[0]
-    for far in fars:
-        w_total = w_total + swap(w_far[far - 1], "seq", 2 * far).astype(F32)
+    w_got = [swap(block, "seq", 2 * far) for far, block in zip(fars, w_far)]
     (feature_grad,) = call(
         feature_kernel,
         [shape(feats.shape)],
@@ -662,6 +686,8 @@
         [shape((taps * half, latent_width), F32), shape((1, width), F32)],
         (k_mine, y_got, gain_pair),
     )
+    for block in after(w_got, kernel_mine):
+        w_total = w_total + block.astype(F32)
     return (
         feature_grad[None],
         kernel_mine.reshape(taps, half, latent_width),
@@ -672,7 +698,7 @@
 
 def fits(mesh):
     count = mesh.shape["seq"]
-    return mesh.shape["book"] == 4 and count in (2, 4, 8)
+    return mesh.shape["book"] == 4 and count == 8
 
 
 def solution(mesh):

time: 72.8 us -> 68.2 us (0.937)
  starting transfers between devices: 42.6 us -> 29.8 us
  waiting for transfers between devices: 17.5 us -> 25.5 us
    ppermute x30 -> x26, starting transfers between devices: 39.2 us -> 29.8 us  [swap(): lax.ppermute(block, axis, [(i, i ^ mask) for i in range(lax.axis_size(axi...]
    ppermute x30 -> x26, waiting for transfers between devices: 17.5 us -> 25.5 us  [swap(): lax.ppermute(block, axis, [(i, i ^ mask) for i in range(lax.axis_size(axi...]
    ppermute x1 -> x0, starting transfers between devices: 3.38 us -> none  [shifted(): return lax.ppermute(block, axis, route)]
    pallas_call x15 -> x18, Pallas kernels: 8.95 us -> 9.12 us  [call(): pl.pallas_call(kernel, out_shape=outs, in_specs=[SMEM] * smem + [VMEM] *...]
  transfers between devices with their start and end apart: 31 -> 26, of which waited for: 11 -> 12; matrix products, arithmetic and copies ran while one was open for 1% -> 1% of each run, Pallas kernels for 9% -> 11%
where the time goes in v4:
time: 68.2 us; the launch traced here: 68 us
  starting transfers between devices  29.8 us (44%)
  waiting for transfers between devices  25.5 us (37%)
  Pallas kernels  9.12 us (13%)
  local copies, waits for them, and re-layouts  1.85 us (3%)
  other arithmetic  0.92 us (1%)
  between operations  0.9 us (1%)
    ppermute x26, starting transfers between devices, swap(): lax.ppermute(block, axis, [(i, i ^ mask) for i in range(lax.axis_size(axi...  29.8 us
    ppermute x26, waiting for transfers between devices, swap(): lax.ppermute(block, axis, [(i, i ^ mask) for i in range(lax.axis_size(axi...  25.5 us
    pallas_call x18, Pallas kernels, call(): pl.pallas_call(kernel, out_shape=outs, in_specs=[SMEM] * smem + [VMEM] *...  9.12 us
    unnamed x19, local copies, waits for them, and re-layouts  1.78 us
  transfers between devices with their start and end apart: 26, of which 12 were waited for; matrix products, arithmetic and copies ran while one was open for 1% of the time, Pallas kernels for 11%

profile of v4, /device:TPU:0, one launch (start us, length us, event | category | flops | bytes accessed | tf_op | source)
XLA Modules:
  0.0 68.0 jit_solution(17878307511323664336)
XLA Ops:
  0.6 0.0 copy-start.6
  0.6 0.9 %copy-done.6 = bf16[1,128,512]{2,1,0:T(8,128)(2,1)S(1)} copy-done((bf16[1,128,512]{2,1,0:T(8,128)(2,1)S(1)}, bf16[1,128,512]{2,1,0:T(8,128)(2,1)}, u32[]{:S(2)}) %copy-start.6) | copy-done | bytes 131096
  1.6 0.3 shard_map.102
  1.9 0.8 %copy-done = bf16[3,512,256]{2,1,0:T(8,128)(2,1)S(1)} copy-done((bf16[3,512,256]{2,1,0:T(8,128)(2,1)S(1)}, bf16[3,512,256]{2,1,0:T(8,128)(2,1)}, u32[]{:S(2)}) %copy-start) | copy-done | bytes 786456
  2.7 1.1 %shard_map.103.refs_1_.refs_2_.refs_3_.refs_0_ = bf16[256,256]{1,0:T(8,128)(2,1)S(1)} custom-call(s32[8]{0:T(128)S(1)} %bitcast.35, f32[152,512]{1,0:T(8,128)S(1)} %get-tuple-element.36.padded, s32[1,128]{1,0:T(1,128)S(1)} %bitcast.34, bf16[3,512,256]{2,1,0:T(8,128)(2,1)S(1)} %copy-done), custom_call_target="tpu_custom_call" | custom-call | bytes 1024 | tf_op jit(solution)/shard_map/pallas_call | solution.py:490
  3.8 4.1 %collective-permute-start = (bf16[192,256]{1,0:T(8,128)(2,1)S(1)}, bf16[192,256]{1,0:T(8,128)(2,1)S(1)}, u32[]{:S(2)}, u32[]{:S(2)}) collective-permute-start(bf16[192,256]{1,0:T(8,128)(2,1)S(1)} %shard_map.104), channel_id=1, source_target_pairs={{0,16},{4,20},{8,24},{12,28},{16,0},{20,4},{24,8},{28,12},{1,17},{... | collective-permute-start | bytes 294920 | tf_op jit(solution)/shard_map/ppermute | solution.py:144
  7.9 4.9 %collective-permute-done.refs_1_.refs_2_.refs_3_ = bf16[192,256]{1,0:T(8,128)(2,1)S(1)} collective-permute-done((bf16[192,256]{1,0:T(8,128)(2,1)S(1)}, bf16[192,256]{1,0:T(8,128)(2,1)S(1)}, u32[]{:S(2)}, u32[]{:S(2)}) %collective-permute-start) | collective-permute-done | bytes 98336 | tf_op jit(solution)/shard_map/ppermute | solution.py:144
  12.8 0.6 collective-permute-start.14
  13.5 3.5 %collective-permute-start.1 = (bf16[256,256]{1,0:T(8,128)(2,1)S(1)}, bf16[256,256]{1,0:T(8,128)(2,1)S(1)}, u32[]{:S(2)}, u32[]{:S(2)}) collective-permute-start(bf16[256,256]{1,0:T(8,128)(2,1)S(1)} %shard_map.105), channel_id=1, source_target_pairs={{0,8},{4,12},{8,0},{12,4},{16,24},{20,28},{24,16},{28,20},{1,9},{5... | collective-permute-start | bytes 393224 | tf_op jit(solution)/shard_map/ppermute | solution.py:144
  17.0 4.5 %collective-permute-done.14 = bf16[1,512,128]{2,1,0:T(8,128)(2,1)S(1)} collective-permute-done((bf16[1,512,128]{2,1,0:T(8,128)(2,1)S(1)}, bf16[1,512,128]{2,1,0:T(8,128)(2,1)S(1)}, u32[]{:S(2)}, u32[]{:S(2)}) %collective-permute-start.14) | collective-permute-done | bytes 131104 | tf_op jit(solution)/shard_map/ppermute | solution.py:144
  21.6 0.2 collective-permute-done.1.refs_1_.refs_2_
  21.8 1.6 %collective-permute-start.2 = (bf16[384,256]{1,0:T(8,128)(2,1)S(1)}, bf16[384,256]{1,0:T(8,128)(2,1)S(1)}, u32[]{:S(2)}, u32[]{:S(2)}) collective-permute-start(bf16[384,256]{1,0:T(8,128)(2,1)S(1)} %shard_map.106), channel_id=1, source_target_pairs={{0,4},{4,0},{8,12},{12,8},{16,20},{20,16},{24,28},{28,24},{1,5},{5... | collective-permute-start | bytes 589832 | tf_op jit(solution)/shard_map/ppermute | solution.py:144
  23.4 0.4 collective-permute-start.15
  23.8 0.0 copy-start.5
  23.8 0.0 copy-start.8
  23.8 1.6 %collective-permute-start.4 = (bf16[256,256]{1,0:T(8,128)(2,1)S(1)}, bf16[256,256]{1,0:T(8,128)(2,1)S(1)}, u32[]{:S(2)}, u32[]{:S(2)}) collective-permute-start(bf16[256,256]{1,0:T(8,128)(2,1)S(1)} %shard_map.108.refs_1_), channel_id=1, source_target_pairs={{0,6},{1,7},{2,4},{3,5},{4,2},{5,3},{6,0},{7,1},{8,14},{9,15},{10,... | collective-permute-start | bytes 393224 | tf_op jit(solution)/shard_map/ppermute | solution.py:144
  25.3 0.5 collective-permute-start.3
  25.8 4.8 %collective-permute-done.4.refs_4_ = bf16[256,256]{1,0:T(8,128)(2,1)S(1)} collective-permute-done((bf16[256,256]{1,0:T(8,128)(2,1)S(1)}, bf16[256,256]{1,0:T(8,128)(2,1)S(1)}, u32[]{:S(2)}, u32[]{:S(2)}) %collective-permute-start.4) | collective-permute-done | bytes 131104 | tf_op jit(solution)/shard_map/ppermute | solution.py:144
  30.6 0.0 collective-permute-start.8
  30.7 1.1 %collective-permute-done.3.refs_3_ = bf16[256,256]{1,0:T(8,128)(2,1)S(1)} collective-permute-done((bf16[256,256]{1,0:T(8,128)(2,1)S(1)}, bf16[256,256]{1,0:T(8,128)(2,1)S(1)}, u32[]{:S(2)}, u32[]{:S(2)}) %collective-permute-start.3) | collective-permute-done | bytes 131104 | tf_op jit(solution)/shard_map/ppermute | solution.py:144
  31.7 0.0 collective-permute-start.7
  31.7 0.5 collective-permute-start.6
  32.3 0.0 collective-permute-done.15
  32.3 1.6 %collective-permute-start.16 = (bf16[4,512,128]{2,1,0:T(8,128)(2,1)S(1)}, bf16[4,512,128]{2,1,0:T(8,128)(2,1)S(1)}, u32[]{:S(2)}, u32[]{:S(2)}) collective-permute-start(bf16[4,512,128]{2,1,0:T(8,128)(2,1)S(1)} %constant_dynamic-update-slice_fusion.refs_0_), channel_id=1, source_target_pairs={{0,4},{4,0},{8,12},{12,8},{16,20},{20,16},{24,28},{28,24},{1,5},{5... | collective-permute-start | bytes 1572872 | tf_op jit(solution)/shard_map/ppermute | solution.py:144
  33.9 0.0 collective-permute-done.5.refs_5_
  33.9 0.0 collective-permute-done.8.refs_8_
  33.9 0.0 collective-permute-done.7.refs_7_
  33.9 1.4 %shard_map.109 = (bf16[144,256]{1,0:T(8,128)(2,1)S(1)}, bf16[144,2048]{1,0:T(8,128)(2,1)S(1)}, bf16[144,256]{1,0:T(8,128)(2,1)S(1)}, f32[8,128]{1,0:T(8,128)S(1)}) custom-call(bf16[256,256]{1,0:T(8,128)(2,1)S(1)} %shard_map.107.refs_0_, bf16[256,256]{1,0:T(8,128)(2,1)S(1)} %shard_map.108.refs_1_, ...), custom_call_target="tpu_custom_call" | custom-call | flops 20000000000 | bytes 1024 | tf_op jit(solution)/shard_map/pallas_call | solution.py:490
  35.3 3.3 %collective-permute-start.11 = (bf16[144,256]{1,0:T(8,128)(2,1)S(1)}, bf16[144,256]{1,0:T(8,128)(2,1)S(1)}, u32[]{:S(2)}, u32[]{:S(2)}) collective-permute-start(bf16[144,256]{1,0:T(8,128)(2,1)S(1)} %get-tuple-element.37.refs_0_), channel_id=1, source_target_pairs={{0,24},{4,28},{8,16},{12,20},{16,8},{20,12},{24,0},{28,4},{1,25},{... | collective-permute-start | bytes 221192 | tf_op jit(solution)/shard_map/ppermute | solution.py:144
  38.7 0.0 collective-permute-start.10
  38.7 1.1 %collective-permute-start.9 = (bf16[144,256]{1,0:T(8,128)(2,1)S(1)}, bf16[144,256]{1,0:T(8,128)(2,1)S(1)}, u32[]{:S(2)}, u32[]{:S(2)}) collective-permute-start(bf16[144,256]{1,0:T(8,128)(2,1)S(1)} %get-tuple-element.37.refs_0_), channel_id=1, source_target_pairs={{0,8},{4,12},{8,0},{12,4},{16,24},{20,28},{24,16},{28,20},{1,9},{5... | collective-permute-start | bytes 221192 | tf_op jit(solution)/shard_map/ppermute | solution.py:144
  39.8 1.3 %shard_map.113.refs_7_ = s32[1024,3]{1,0:T(8,128)S(1)} custom-call(s32[8]{0:T(128)S(1)} %bitcast.36, f32[8,128]{1,0:T(8,128)S(1)} %get-tuple-element.45.owners_ref), custom_call_target="tpu_custom_call" | custom-call | flops 20000000000 | bytes 1024 | tf_op jit(solution)/shard_map/pallas_call | solution.py:490
  41.1 0.5 shard_map.112
  41.6 0.1 collective-permute-start.17
  41.7 0.0 collective-permute-done.11.refs_1_.refs_3_
  41.7 3.9 %collective-permute-done.10.refs_0_.refs_2_ = bf16[144,256]{1,0:T(8,128)(2,1)S(1)} collective-permute-done((bf16[144,256]{1,0:T(8,128)(2,1)S(1)}, bf16[144,256]{1,0:T(8,128)(2,1)S(1)}, u32[]{:S(2)}, u32[]{:S(2)}) %collective-permute-start.10) | collective-permute-done | bytes 73760 | tf_op jit(solution)/shard_map/ppermute | solution.py:144
  45.6 1.6 %collective-permute-start.13 = (bf16[288,256]{1,0:T(8,128)(2,1)S(1)}, bf16[288,256]{1,0:T(8,128)(2,1)S(1)}, u32[]{:S(2)}, u32[]{:S(2)}) collective-permute-start(bf16[288,256]{1,0:T(8,128)(2,1)S(1)} %shard_map.111), channel_id=1, source_target_pairs={{0,4},{4,0},{8,12},{12,8},{16,20},{20,16},{24,28},{28,24},{1,5},{5... | collective-permute-start | bytes 442376 | tf_op jit(solution)/shard_map/ppermute | solution.py:144
  47.1 0.6 collective-permute-start.12
  47.7 0.2 convert_add_fusion
  48.0 1.5 %collective-permute-start.22 = (bf16[4,64,256]{2,1,0:T(8,128)(2,1)S(1)}, bf16[4,64,256]{2,1,0:T(8,128)(2,1)S(1)}, u32[]{:S(2)}, u32[]{:S(2)}) collective-permute-start(bf16[4,64,256]{2,1,0:T(8,128)(2,1)S(1)} %get-tuple-element.72), channel_id=1, source_target_pairs={{0,6},{1,7},{2,4},{3,5},{4,2},{5,3},{6,0},{7,1},{8,14},{9,15},{10,... | collective-permute-start | bytes 393224 | tf_op jit(solution)/shard_map/ppermute | solution.py:144
  49.5 1.5 %collective-permute-start.21 = (bf16[4,64,256]{2,1,0:T(8,128)(2,1)S(1)}, bf16[4,64,256]{2,1,0:T(8,128)(2,1)S(1)}, u32[]{:S(2)}, u32[]{:S(2)}) collective-permute-start(bf16[4,64,256]{2,1,0:T(8,128)(2,1)S(1)} %get-tuple-element.73), channel_id=1, source_target_pairs={{0,2},{1,3},{2,0},{3,1},{4,6},{5,7},{6,4},{7,5},{8,10},{9,11},{10,... | collective-permute-start | bytes 393224 | tf_op jit(solution)/shard_map/ppermute | solution.py:144
  51.0 0.5 collective-permute-start.20
  51.5 0.3 shard_map.114
  51.8 0.5 collective-permute-done.13.refs_5_
  52.4 3.2 %collective-permute-done.12.refs_4_ = bf16[288,256]{1,0:T(8,128)(2,1)S(1)} collective-permute-done((bf16[288,256]{1,0:T(8,128)(2,1)S(1)}, bf16[288,256]{1,0:T(8,128)(2,1)S(1)}, u32[]{:S(2)}, u32[]{:S(2)}) %collective-permute-start.12) | collective-permute-done | bytes 147488 | tf_op jit(solution)/shard_map/ppermute | solution.py:144
  55.5 1.6 %shard_map.115 = (bf16[784,256]{1,0:T(8,128)(2,1)S(1)}, bf16[1024,768]{1,0:T(8,128)(2,1)S(1)}, f32[8,256]{1,0:T(8,128)S(1)}) custom-call(bf16[144,256]{1,0:T(8,128)(2,1)S(1)} %get-tuple-element.37.refs_0_, bf16[144,256]{1,0:T(8,128)(2,1)S(1)} %collective-permute-done.9.refs_1_, bf16[144,256]{1,0:T(8,128)(2,1)S(1)} %collective-permute-done.10.refs_0_.refs_2_, ...), custom_call_target="tpu_custom_call" | custom-call | flops 20000000000 | bytes 1024 | tf_op jit(solution)/shard_map/pallas_call | solution.py:490
  57.2 0.1 collective-permute-start.18
  57.3 0.6 shard_map.116.kept_ref
  57.8 0.0 copy-start.1
  57.9 0.0 copy-start.7
  57.9 1.1 %collective-permute-done.18.got_ref = bf16[784,256]{1,0:T(8,128)(2,1)S(1)} collective-permute-done((bf16[784,256]{1,0:T(8,128)(2,1)S(1)}, bf16[784,256]{1,0:T(8,128)(2,1)S(1)}, u32[]{:S(2)}, u32[]{:S(2)}) %collective-permute-start.18) | collective-permute-done | bytes 401440 | tf_op jit(solution)/shard_map/ppermute | solution.py:144
  59.0 0.1 shard_map.117
  59.1 0.7 %collective-permute-start.19 = (bf16[400,256]{1,0:T(8,128)(2,1)S(1)}, bf16[400,256]{1,0:T(8,128)(2,1)S(1)}, u32[]{:S(2)}, u32[]{:S(2)}) collective-permute-start(bf16[400,256]{1,0:T(8,128)(2,1)S(1)} %get-tuple-element.55), channel_id=1, source_target_pairs={{0,2},{1,3},{2,0},{3,1},{4,6},{5,7},{6,4},{7,5},{8,10},{9,11},{10,... | collective-permute-start | bytes 614408 | tf_op jit(solution)/shard_map/ppermute | solution.py:144
  59.7 0.0 collective-permute-done.22
  59.8 0.1 collective-permute-done.20
  59.9 0.1 fusion.7
  59.9 2.6 %collective-permute-start.25 = (bf16[64,256]{1,0:T(8,128)(2,1)S(1)}, bf16[64,256]{1,0:T(8,128)(2,1)S(1)}, u32[]{:S(2)}, u32[]{:S(2)}) collective-permute-start(bf16[64,256]{1,0:T(8,128)(2,1)S(1)} %get-tuple-element.75), channel_id=1, source_target_pairs={{0,24},{4,28},{8,16},{12,20},{16,8},{20,12},{24,0},{28,4},{1,25},{... | collective-permute-start | bytes 98312 | tf_op jit(solution)/shard_map/ppermute | solution.py:144
  62.6 1.8 %collective-permute-start.23 = (bf16[64,256]{1,0:T(8,128)(2,1)S(1)}, bf16[64,256]{1,0:T(8,128)(2,1)S(1)}, u32[]{:S(2)}, u32[]{:S(2)}) collective-permute-start(bf16[64,256]{1,0:T(8,128)(2,1)S(1)} %get-tuple-element.77), channel_id=1, source_target_pairs={{0,8},{4,12},{8,0},{12,4},{16,24},{20,28},{24,16},{28,20},{1,9},{5... | collective-permute-start | bytes 98312 | tf_op jit(solution)/shard_map/ppermute | solution.py:144
  64.4 1.0 %shard_map.118 = bf16[128,512]{1,0:T(8,128)(2,1)} custom-call(bf16[128,512]{1,0:T(8,128)(2,1)S(1)} %bitcast.39, bf16[1024,768]{1,0:T(8,128)(2,1)S(1)} %get-tuple-element.56.windows_ref, bf16[3,512,256]{2,1,0:T(8,128)(2,1)S(1)} %copy-done.1), custom_call_target="tpu_custom_call" | custom-call | flops 20000000000 | bytes 1024 | tf_op jit(solution)/shard_map/pallas_call | solution.py:490
  65.5 0.8 %collective-permute-done.19.got_ref = bf16[400,256]{1,0:T(8,128)(2,1)S(1)} collective-permute-done((bf16[400,256]{1,0:T(8,128)(2,1)S(1)}, bf16[400,256]{1,0:T(8,128)(2,1)S(1)}, u32[]{:S(2)}, u32[]{:S(2)}) %collective-permute-start.19) | collective-permute-done | bytes 204832 | tf_op jit(solution)/shard_map/ppermute | solution.py:144
  66.2 0.8 %shard_map.119 = (f32[384,256]{1,0:T(8,128)}, f32[1,2048]{1,0:T(1,128)}) custom-call(f32[384,256]{1,0:T(8,128)S(1)} %get-tuple-element.57.mine_ref, bf16[400,256]{1,0:T(8,128)(2,1)S(1)} %collective-permute-done.19.got_ref, f32[8,256]{1,0:T(8,128)S(1)} %get-tuple-element.59.gain_ref), custom_call_target="tpu_custom_call" | custom-call | bytes 1024 | tf_op jit(solution)/shard_map/pallas_call | solution.py:490
  67.0 0.0 collective-permute-done.25
  67.1 0.3 collective-permute-done.24
  67.4 0.6 fusion.5
  (32 shorter events, 0.2 us)
Async XLA Ops:
  0.6 0.9 %copy-start.6 = (bf16[1,128,512]{2,1,0:T(8,128)(2,1)S(1)}, bf16[1,128,512]{2,1,0:T(8,128)(2,1)}, u32[]{:S(2)}) copy-start(bf16[1,128,512]{2,1,0:T(8,128)(2,1)} %param.7) | copy-start | bytes 393220
  1.5 1.1 %copy-start = (bf16[3,512,256]{2,1,0:T(8,128)(2,1)S(1)}, bf16[3,512,256]{2,1,0:T(8,128)(2,1)}, u32[]{:S(2)}) copy-start(bf16[3,512,256]{2,1,0:T(8,128)(2,1)} %w_ref.3) | copy-start | bytes 2359300
  1.5 1.1 %copy-start.3 = (s32[1,128,1]{1,2,0:T(1,128)S(1)}, s32[1,128,1]{1,2,0:T(1,128)}, u32[]{:S(2)}) copy-start(s32[1,128,1]{1,2,0:T(1,128)} %param.9) | copy-start | bytes 1540
  1.5 1.1 %copy-start.4 = (s32[1,8]{1,0:T(1,128)S(1)}, s32[1,8]{1,0:T(1,128)}, u32[]{:S(2)}) copy-start(s32[1,8]{1,0:T(1,128)} %param.8) | copy-start | bytes 100
  1.5 2.3 %copy-start.2 = (bf16[256,64]{0,1:T(8,128)(2,1)S(1)}, bf16[256,64]{0,1:T(8,128)(2,1)}, u32[]{:S(2)}) copy-start(bf16[256,64]{0,1:T(8,128)(2,1)} %param.11) | copy-start | bytes 98308
  3.8 9.0 %collective-permute-start = (bf16[192,256]{1,0:T(8,128)(2,1)S(1)}, bf16[192,256]{1,0:T(8,128)(2,1)S(1)}, u32[]{:S(2)}, u32[]{:S(2)}) collective-permute-start(bf16[192,256]{1,0:T(8,128)(2,1)S(1)} %shard_map.104), channel_id=1, source_target_pairs={{0,16},{4,20},{8,24},{12,28},{16,0},{20,4},{24,8},{28,12},{1,17},{... | collective-permute-start | bytes 294920 | tf_op jit(solution)/shard_map/ppermute | solution.py:144
  12.8 8.7 %collective-permute-start.14 = (bf16[1,512,128]{2,1,0:T(8,128)(2,1)S(1)}, bf16[1,512,128]{2,1,0:T(8,128)(2,1)S(1)}, u32[]{:S(2)}, u32[]{:S(2)}) collective-permute-start(bf16[1,512,128]{2,1,0:T(8,128)(2,1)S(1)} %bitcast.32), channel_id=1, source_target_pairs={{0,16},{4,20},{8,24},{12,28},{16,0},{20,4},{24,8},{28,12},{1,17},{... | collective-permute-start | bytes 393224 | tf_op jit(solution)/shard_map/ppermute | solution.py:144
  13.5 8.3 %collective-permute-start.1 = (bf16[256,256]{1,0:T(8,128)(2,1)S(1)}, bf16[256,256]{1,0:T(8,128)(2,1)S(1)}, u32[]{:S(2)}, u32[]{:S(2)}) collective-permute-start(bf16[256,256]{1,0:T(8,128)(2,1)S(1)} %shard_map.105), channel_id=1, source_target_pairs={{0,8},{4,12},{8,0},{12,4},{16,24},{20,28},{24,16},{28,20},{1,9},{5... | collective-permute-start | bytes 393224 | tf_op jit(solution)/shard_map/ppermute | solution.py:144
  21.8 9.9 %collective-permute-start.2 = (bf16[384,256]{1,0:T(8,128)(2,1)S(1)}, bf16[384,256]{1,0:T(8,128)(2,1)S(1)}, u32[]{:S(2)}, u32[]{:S(2)}) collective-permute-start(bf16[384,256]{1,0:T(8,128)(2,1)S(1)} %shard_map.106), channel_id=1, source_target_pairs={{0,4},{4,0},{8,12},{12,8},{16,20},{20,16},{24,28},{28,24},{1,5},{5... | collective-permute-start | bytes 589832 | tf_op jit(solution)/shard_map/ppermute | solution.py:144
  23.4 8.9 %collective-permute-start.15 = (bf16[2,512,128]{2,1,0:T(8,128)(2,1)S(1)}, bf16[2,512,128]{2,1,0:T(8,128)(2,1)S(1)}, u32[]{:S(2)}, u32[]{:S(2)}) collective-permute-start(bf16[2,512,128]{2,1,0:T(8,128)(2,1)S(1)} %pad_maximum_fusion), channel_id=1, source_target_pairs={{0,8},{4,12},{8,0},{12,4},{16,24},{20,28},{24,16},{28,20},{1,9},{5... | collective-permute-start | bytes 786440 | tf_op jit(solution)/shard_map/ppermute | solution.py:144
  23.8 10.1 %copy-start.5 = (bf16[1,136,2048]{2,1,0:T(8,128)(2,1)S(1)}, bf16[1,136,2048]{2,1,0:T(8,128)(2,1)}, u32[]{:S(2)}) copy-start(bf16[1,136,2048]{2,1,0:T(8,128)(2,1)} %param.13) | copy-start | bytes 1671172
  23.8 10.1 %copy-start.8 = (f32[2048]{0:T(1024)S(1)}, f32[2048]{0:T(1024)}, u32[]{:S(2)}) copy-start(f32[2048]{0:T(1024)} %param.12) | copy-start | bytes 24580
  23.8 6.9 %collective-permute-start.4 = (bf16[256,256]{1,0:T(8,128)(2,1)S(1)}, bf16[256,256]{1,0:T(8,128)(2,1)S(1)}, u32[]{:S(2)}, u32[]{:S(2)}) collective-permute-start(bf16[256,256]{1,0:T(8,128)(2,1)S(1)} %shard_map.108.refs_1_), channel_id=1, source_target_pairs={{0,6},{1,7},{2,4},{3,5},{4,2},{5,3},{6,0},{7,1},{8,14},{9,15},{10,... | collective-permute-start | bytes 393224 | tf_op jit(solution)/shard_map/ppermute | solution.py:144
  25.3 6.4 %collective-permute-start.3 = (bf16[256,256]{1,0:T(8,128)(2,1)S(1)}, bf16[256,256]{1,0:T(8,128)(2,1)S(1)}, u32[]{:S(2)}, u32[]{:S(2)}) collective-permute-start(bf16[256,256]{1,0:T(8,128)(2,1)S(1)} %shard_map.108.refs_1_), channel_id=1, source_target_pairs={{0,2},{1,3},{2,0},{3,1},{4,6},{5,7},{6,4},{7,5},{8,10},{9,11},{10,... | collective-permute-start | bytes 393224 | tf_op jit(solution)/shard_map/ppermute | solution.py:144
  25.8 8.0 %collective-permute-start.5 = (bf16[256,256]{1,0:T(8,128)(2,1)S(1)}, bf16[256,256]{1,0:T(8,128)(2,1)S(1)}, u32[]{:S(2)}, u32[]{:S(2)}) collective-permute-start(bf16[256,256]{1,0:T(8,128)(2,1)S(1)} %shard_map.108.refs_1_), channel_id=1, source_target_pairs={{0,1},{1,0},{2,3},{3,2},{4,5},{5,4},{6,7},{7,6},{8,9},{9,8},{10,11... | collective-permute-start | bytes 393224 | tf_op jit(solution)/shard_map/ppermute | solution.py:144
  30.6 3.2 %collective-permute-start.8 = (bf16[256,256]{1,0:T(8,128)(2,1)S(1)}, bf16[256,256]{1,0:T(8,128)(2,1)S(1)}, u32[]{:S(2)}, u32[]{:S(2)}) collective-permute-start(bf16[256,256]{1,0:T(8,128)(2,1)S(1)} %collective-permute-done.4.refs_4_), channel_id=1, source_target_pairs={{0,1},{1,0},{2,3},{3,2},{4,5},{5,4},{6,7},{7,6},{8,9},{9,8},{10,11... | collective-permute-start | bytes 393224 | tf_op jit(solution)/shard_map/ppermute | solution.py:144
  31.7 2.2 %collective-permute-start.7 = (bf16[256,256]{1,0:T(8,128)(2,1)S(1)}, bf16[256,256]{1,0:T(8,128)(2,1)S(1)}, u32[]{:S(2)}, u32[]{:S(2)}) collective-permute-start(bf16[256,256]{1,0:T(8,128)(2,1)S(1)} %collective-permute-done.3.refs_3_), channel_id=1, source_target_pairs={{0,1},{1,0},{2,3},{3,2},{4,5},{5,4},{6,7},{7,6},{8,9},{9,8},{10,11... | collective-permute-start | bytes 393224 | tf_op jit(solution)/shard_map/ppermute | solution.py:144
  31.7 2.2 %collective-permute-start.6 = (bf16[384,256]{1,0:T(8,128)(2,1)S(1)}, bf16[384,256]{1,0:T(8,128)(2,1)S(1)}, u32[]{:S(2)}, u32[]{:S(2)}) collective-permute-start(bf16[384,256]{1,0:T(8,128)(2,1)S(1)} %collective-permute-done.2.refs_1_.refs_2_), channel_id=1, source_target_pairs={{0,1},{1,0},{2,3},{3,2},{4,5},{5,4},{6,7},{7,6},{8,9},{9,8},{10,11... | collective-permute-start | bytes 589832 | tf_op jit(solution)/shard_map/ppermute | solution.py:144
  32.3 18.7 %collective-permute-start.16 = (bf16[4,512,128]{2,1,0:T(8,128)(2,1)S(1)}, bf16[4,512,128]{2,1,0:T(8,128)(2,1)S(1)}, u32[]{:S(2)}, u32[]{:S(2)}) collective-permute-start(bf16[4,512,128]{2,1,0:T(8,128)(2,1)S(1)} %constant_dynamic-update-slice_fusion.refs_0_), channel_id=1, source_target_pairs={{0,4},{4,0},{8,12},{12,8},{16,20},{20,16},{24,28},{28,24},{1,5},{5... | collective-permute-start | bytes 1572872 | tf_op jit(solution)/shard_map/ppermute | solution.py:144
  35.3 6.3 %collective-permute-start.11 = (bf16[144,256]{1,0:T(8,128)(2,1)S(1)}, bf16[144,256]{1,0:T(8,128)(2,1)S(1)}, u32[]{:S(2)}, u32[]{:S(2)}) collective-permute-start(bf16[144,256]{1,0:T(8,128)(2,1)S(1)} %get-tuple-element.37.refs_0_), channel_id=1, source_target_pairs={{0,24},{4,28},{8,16},{12,20},{16,8},{20,12},{24,0},{28,4},{1,25},{... | collective-permute-start | bytes 221192 | tf_op jit(solution)/shard_map/ppermute | solution.py:144
  38.7 6.9 %collective-permute-start.10 = (bf16[144,256]{1,0:T(8,128)(2,1)S(1)}, bf16[144,256]{1,0:T(8,128)(2,1)S(1)}, u32[]{:S(2)}, u32[]{:S(2)}) collective-permute-start(bf16[144,256]{1,0:T(8,128)(2,1)S(1)} %get-tuple-element.37.refs_0_), channel_id=1, source_target_pairs={{0,16},{4,20},{8,24},{12,28},{16,0},{20,4},{24,8},{28,12},{1,17},{... | collective-permute-start | bytes 221192 | tf_op jit(solution)/shard_map/ppermute | solution.py:144
  38.7 8.4 %collective-permute-start.9 = (bf16[144,256]{1,0:T(8,128)(2,1)S(1)}, bf16[144,256]{1,0:T(8,128)(2,1)S(1)}, u32[]{:S(2)}, u32[]{:S(2)}) collective-permute-start(bf16[144,256]{1,0:T(8,128)(2,1)S(1)} %get-tuple-element.37.refs_0_), channel_id=1, source_target_pairs={{0,8},{4,12},{8,0},{12,4},{16,24},{20,28},{24,16},{28,20},{1,9},{5... | collective-permute-start | bytes 221192 | tf_op jit(solution)/shard_map/ppermute | solution.py:144
  41.6 6.2 %collective-permute-start.17 = (bf16[16,64,256]{2,1,0:T(8,128)(2,1)S(1)}, bf16[16,64,256]{2,1,0:T(8,128)(2,1)S(1)}, u32[]{:S(2)}, u32[]{:S(2)}) collective-permute-start(bf16[16,64,256]{2,1,0:T(8,128)(2,1)S(1)} %get-tuple-element.44), channel_id=1, source_target_pairs={{0,1},{1,0},{2,3},{3,2},{4,5},{5,4},{6,7},{7,6},{8,9},{9,8},{10,11... | collective-permute-start | bytes 1572872 | tf_op jit(solution)/shard_map/ppermute | solution.py:144
  45.6 6.8 %collective-permute-start.13 = (bf16[288,256]{1,0:T(8,128)(2,1)S(1)}, bf16[288,256]{1,0:T(8,128)(2,1)S(1)}, u32[]{:S(2)}, u32[]{:S(2)}) collective-permute-start(bf16[288,256]{1,0:T(8,128)(2,1)S(1)} %shard_map.111), channel_id=1, source_target_pairs={{0,4},{4,0},{8,12},{12,8},{16,20},{20,16},{24,28},{28,24},{1,5},{5... | collective-permute-start | bytes 442376 | tf_op jit(solution)/shard_map/ppermute | solution.py:144
  47.1 8.4 %collective-permute-start.12 = (bf16[288,256]{1,0:T(8,128)(2,1)S(1)}, bf16[288,256]{1,0:T(8,128)(2,1)S(1)}, u32[]{:S(2)}, u32[]{:S(2)}) collective-permute-start(bf16[288,256]{1,0:T(8,128)(2,1)S(1)} %shard_map.110), channel_id=1, source_target_pairs={{0,4},{4,0},{8,12},{12,8},{16,20},{20,16},{24,28},{28,24},{1,5},{5... | collective-permute-start | bytes 442376 | tf_op jit(solution)/shard_map/ppermute | solution.py:144
  48.0 11.8 %collective-permute-start.22 = (bf16[4,64,256]{2,1,0:T(8,128)(2,1)S(1)}, bf16[4,64,256]{2,1,0:T(8,128)(2,1)S(1)}, u32[]{:S(2)}, u32[]{:S(2)}) collective-permute-start(bf16[4,64,256]{2,1,0:T(8,128)(2,1)S(1)} %get-tuple-element.72), channel_id=1, source_target_pairs={{0,6},{1,7},{2,4},{3,5},{4,2},{5,3},{6,0},{7,1},{8,14},{9,15},{10,... | collective-permute-start | bytes 393224 | tf_op jit(solution)/shard_map/ppermute | solution.py:144
  49.5 10.3 %collective-permute-start.21 = (bf16[4,64,256]{2,1,0:T(8,128)(2,1)S(1)}, bf16[4,64,256]{2,1,0:T(8,128)(2,1)S(1)}, u32[]{:S(2)}, u32[]{:S(2)}) collective-permute-start(bf16[4,64,256]{2,1,0:T(8,128)(2,1)S(1)} %get-tuple-element.73), channel_id=1, source_target_pairs={{0,2},{1,3},{2,0},{3,1},{4,6},{5,7},{6,4},{7,5},{8,10},{9,11},{10,... | collective-permute-start | bytes 393224 | tf_op jit(solution)/shard_map/ppermute | solution.py:144
  51.0 8.9 %collective-permute-start.20 = (bf16[4,64,256]{2,1,0:T(8,128)(2,1)S(1)}, bf16[4,64,256]{2,1,0:T(8,128)(2,1)S(1)}, u32[]{:S(2)}, u32[]{:S(2)}) collective-permute-start(bf16[4,64,256]{2,1,0:T(8,128)(2,1)S(1)} %get-tuple-element.74), channel_id=1, source_target_pairs={{0,4},{4,0},{8,12},{12,8},{16,20},{20,16},{24,28},{28,24},{1,5},{5... | collective-permute-start | bytes 393224 | tf_op jit(solution)/shard_map/ppermute | solution.py:144
  57.2 1.8 %collective-permute-start.18 = (bf16[784,256]{1,0:T(8,128)(2,1)S(1)}, bf16[784,256]{1,0:T(8,128)(2,1)S(1)}, u32[]{:S(2)}, u32[]{:S(2)}) collective-permute-start(bf16[784,256]{1,0:T(8,128)(2,1)S(1)} %get-tuple-element.53), channel_id=1, source_target_pairs={{0,1},{1,0},{2,3},{3,2},{4,5},{5,4},{6,7},{7,6},{8,9},{9,8},{10,11... | collective-permute-start | bytes 1204232 | tf_op jit(solution)/shard_map/ppermute | solution.py:144
  57.8 6.6 %copy-start.1 = (bf16[3,512,256]{2,1,0:T(8,128)(2,1)S(1)}, bf16[3,512,256]{2,1,0:T(8,128)(2,1)}, u32[]{:S(2)}) copy-start(bf16[3,512,256]{2,1,0:T(8,128)(2,1)} %w_ref.3) | copy-start | bytes 2359300
  57.9 6.6 %copy-start.7 = (bf16[1,128,512]{2,1,0:T(8,128)(2,1)S(1)}, bf16[1,128,512]{2,1,0:T(8,128)(2,1)}, u32[]{:S(2)}) copy-start(bf16[1,128,512]{2,1,0:T(8,128)(2,1)} %param.7) | copy-start | bytes 393220
  59.1 7.2 %collective-permute-start.19 = (bf16[400,256]{1,0:T(8,128)(2,1)S(1)}, bf16[400,256]{1,0:T(8,128)(2,1)S(1)}, u32[]{:S(2)}, u32[]{:S(2)}) collective-permute-start(bf16[400,256]{1,0:T(8,128)(2,1)S(1)} %get-tuple-element.55), channel_id=1, source_target_pairs={{0,2},{1,3},{2,0},{3,1},{4,6},{5,7},{6,4},{7,5},{8,10},{9,11},{10,... | collective-permute-start | bytes 614408 | tf_op jit(solution)/shard_map/ppermute | solution.py:144
  59.9 7.1 %collective-permute-start.25 = (bf16[64,256]{1,0:T(8,128)(2,1)S(1)}, bf16[64,256]{1,0:T(8,128)(2,1)S(1)}, u32[]{:S(2)}, u32[]{:S(2)}) collective-permute-start(bf16[64,256]{1,0:T(8,128)(2,1)S(1)} %get-tuple-element.75), channel_id=1, source_target_pairs={{0,24},{4,28},{8,16},{12,20},{16,8},{20,12},{24,0},{28,4},{1,25},{... | collective-permute-start | bytes 98312 | tf_op jit(solution)/shard_map/ppermute | solution.py:144
  62.6 4.8 %collective-permute-start.24 = (bf16[64,256]{1,0:T(8,128)(2,1)S(1)}, bf16[64,256]{1,0:T(8,128)(2,1)S(1)}, u32[]{:S(2)}, u32[]{:S(2)}) collective-permute-start(bf16[64,256]{1,0:T(8,128)(2,1)S(1)} %get-tuple-element.76), channel_id=1, source_target_pairs={{0,16},{4,20},{8,24},{12,28},{16,0},{20,4},{24,8},{28,12},{1,17},{... | collective-permute-start | bytes 98312 | tf_op jit(solution)/shard_map/ppermute | solution.py:144
  62.6 4.8 %collective-permute-start.23 = (bf16[64,256]{1,0:T(8,128)(2,1)S(1)}, bf16[64,256]{1,0:T(8,128)(2,1)S(1)}, u32[]{:S(2)}, u32[]{:S(2)}) collective-permute-start(bf16[64,256]{1,0:T(8,128)(2,1)S(1)} %get-tuple-element.77), channel_id=1, source_target_pairs={{0,8},{4,12},{8,0},{12,4},{16,24},{20,28},{24,16},{28,20},{1,9},{5... | collective-permute-start | bytes 98312 | tf_op jit(solution)/shard_map/ppermute | solution.py:144

commit v5 on v4

--- a/solution.py
+++ b/solution.py
@@ -353,7 +353,7 @@
     ranks = ranks_of(owners, count)
     position = iota((count, frames), 0) * frames + iota((count, frames), 1)
     relative = jnp.bitwise_xor(owners.astype(jnp.int32), me)
-    relative = (relative >> 1) + (relative & 1) * (count // 2)
+    relative = jnp.where(relative & 1 == 1, -count, relative >> 1)
     rows_of = [relative.astype(F32), ranks]
     for tap in range(1, taps):
         later = position + tap
@@ -376,26 +376,28 @@
 
 
 def spread_kernel(count, frames, taps, *refs):
-    backs = refs[: count // 2 + 2]
-    lines_ref, facts_ref, send_ref, windows_ref, gain_ref, gathered, wide = refs[len(backs) :]
+    backs = refs[: count // 2]
+    lines_ref, facts_ref, send_ref, windows_ref, gain_ref, own_ref, peer_ref = refs[count // 2 : -2]
+    gathered, wide = refs[-2:]
     rows, latent_width = backs[0].shape
     share = lines_ref.shape[0] // 2
     gain_rows = gain_ref.shape[0]
     gain = jnp.zeros((gain_rows, latent_width), F32)
-    at = 0
-    for back_ref in backs:
-        gathered[at : at + back_ref.shape[0], :] = back_ref[...]
-        at += back_ref.shape[0]
-    for rel in range(count):
-        gain = gain + gathered[rel * rows : (rel + 1) * rows, :].astype(F32)[rows - gain_rows :]
+    for far, back_ref in enumerate(backs):
+        gathered[far * rows : (far + 1) * rows, :] = back_ref[...]
+        gain = gain + back_ref[...].astype(F32)[rows - gain_rows :]
     gain_ref[...] = gain
     for block in range(count):
         here = slice(block * frames, (block + 1) * frames)
-        placed = iota((frames, count * rows), 1) == facts_ref[here, 0:1]
+        placed = iota((frames, gathered.shape[0]), 1) == facts_ref[here, 0:1]
         wide[here, :] = jnp.dot(
             placed.astype(F32).astype(BF16), gathered[...], preferred_element_type=F32
         )
-    wide[count * frames :, :] = jnp.zeros((8, latent_width), F32)
+    wide[count * frames :, :] = jnp.zeros((16, latent_width), F32)
+    me = lax.axis_index("seq")
+    for out_ref, block in ((own_ref, me), (peer_ref, jnp.bitwise_xor(me, 1))):
+        at = pl.multiple_of(block * frames, frames)
+        out_ref[...] = wide[pl.ds(at, frames + 16), :].astype(BF16)
     for block in range(count):
         here = slice(block * frames, (block + 1) * frames)
         windows_ref[here, 0:latent_width] = wide[here, :].astype(BF16)
@@ -459,27 +461,42 @@
     ).astype(BF16)
 
 
-def finish_kernel(mine_ref, got_ref, gain_ref, out_ref, gain_out_ref):
+def sum_kernel(mine_ref, got_ref, gain_ref, send_ref):
     half, gain_rows = mine_ref.shape[0], gain_ref.shape[0]
-    out_ref[...] = mine_ref[...] + got_ref[0:half, :].astype(F32)
+    send_ref[0:half, :] = (mine_ref[...] + got_ref[0:half, :].astype(F32)).astype(BF16)
     pair = got_ref[half : half + 2 * gain_rows, :].astype(F32)
     gain = gain_ref[...] + (pair[:gain_rows] + pair[gain_rows:])
+    high = gain.astype(BF16).astype(F32)
+    send_ref[half : half + 2 * gain_rows, :] = jnp.concatenate(
+        [high, gain - high], axis=0
+    ).astype(BF16)
+
+
+def finish_kernel(mine_ref, got_ref, out_ref, gain_out_ref):
+    half = out_ref.shape[0]
+    gain_rows = (mine_ref.shape[0] - half) // 2
+    out_ref[...] = mine_ref[0:half, :].astype(F32) + got_ref[0:half, :].astype(F32)
+    gain = jnp.zeros((gain_rows, mine_ref.shape[1]), F32)
+    for ref in (mine_ref, got_ref):
+        pair = ref[half : half + 2 * gain_rows, :].astype(F32)
+        gain = gain + (pair[:gain_rows] + pair[gain_rows:])
     step = gain.shape[1]
     for line in range(gain_rows):
         gain_out_ref[:, line * step : (line + 1) * step] = gain[line : line + 1]
 
 
-def feature_kernel(feat_ref, windows_ref, w_ref, out_ref):
+def feature_kernel(feat_ref, own_ref, got_ref, facts_ref, w_ref, out_ref, wide):
     frames = feat_ref.shape[0]
-    taps, _, latent_width = w_ref.shape
     at = pl.multiple_of(lax.axis_index("seq") * frames, frames)
+    wide[...] = own_ref[...].astype(F32) + got_ref[...].astype(F32)
+    facts = facts_ref[pl.ds(at, frames), :]
     total = jnp.zeros(feat_ref.shape, F32)
-    for tap in range(taps):
-        window = windows_ref[
-            pl.ds(at, frames), tap * latent_width : (tap + 1) * latent_width
-        ]
+    for tap in range(w_ref.shape[0]):
+        window = wide[tap : tap + frames, :]
+        if tap:
+            window = jnp.where(facts[:, tap : tap + 1] > 0, window, 0.0)
         total = total + lax.dot_general(
-            window, w_ref[tap], (((1,), (1,)), ((), ())), preferred_element_type=F32
+            window.astype(BF16), w_ref[tap], (((1,), (1,)), ((), ())), preferred_element_type=F32
         )
     feats = feat_ref[...].astype(F32)
     slope = jnp.where(feats > 0, 1.0, jnp.exp(jnp.minimum(feats, 0.0)))
@@ -551,7 +568,7 @@
     )
     pieces = {0: {far: (sent, 2 * far * piece, 2 * piece) for far in range(far_count)}}
     w_blocks = {0: (w_in.T, 0, columns)}
-    held, order, mask = turned[None], [0], far_count // 2
+    held, mask = turned[None], far_count // 2
     w_got = None
     while mask:
         sources = sorted(pieces)
@@ -569,26 +586,33 @@
                 pieces[source ^ mask][far ^ mask] = (w_got, at, 2 * piece)
                 at += 2 * piece
                 del pieces[source][far]
-        held = after(held, w_got)
+        if mask == far_count // 2:
+            joined = collect([w_blocks[far] for far in sorted(w_blocks)], flops=HEAVY)
+            w_blocks = {far: (joined, i * columns, columns) for i, far in enumerate(sorted(w_blocks))}
+        if mask < far_count // 2:
+            held = after(held, w_got)
         got = swap(held, "seq", 2 * mask)
-        held = jnp.concatenate([held, got])
-        order = order + [far ^ mask for far in order]
+        if mask == far_count // 2:
+            held = jnp.concatenate([held, got])
         mask //= 2
+    x_first, x_last = swap(held, "seq", 1), swap(got, "seq", 1)
     fars_of_w = [w_blocks[far] for far in range(far_count)]
     near = [pieces[far][0] for far in range(far_count)]
     x_send = collect(fars_of_w + [(array, at + piece, piece) for array, at, _ in near])
-    w_line = collect(fars_of_w, flops=HEAVY)
+    w_line = collect(fars_of_w)
     x_got = swap(x_send, "seq", 1)
     w_side = swap(w_line, "book", 2)
     w_diag = swap(w_line, ("seq", "book"), 4 + 2)
     w_chips = [w_line, x_got, w_side, w_diag]
-    w_pieces = w_chips + [swap(block, "book", 1) for block in w_chips]
-    turned_all = [held, swap(held, "seq", 1)]
-    orders = [[2 * far for far in order], [2 * far + 1 for far in order]]
+    turned_all = [held, got, x_first, x_last]
+    orders = [[0, 4], [2, 6], [1, 5], [3, 7]]
     gathered = []
     for far, (array, at, _) in enumerate(near):
         gathered += [(array, at, piece), (x_got, far_count * columns + far * piece, piece)]
-    gathered = collect(gathered)
+    gathered = collect(gathered, flops=HEAVY)
+    w_pieces = w_chips + [
+        swap(after(block, gathered) if block is x_got else block, "book", 1) for block in w_chips
+    ]
 
     back, hidden_grad, arrived, owners = call(
         functools.partial(middle_kernel, piece, capacity, frames, count, columns, taps - 1),
@@ -607,12 +631,6 @@
         flops=HEAVY,
     )
     backs = [back] + [swap(back, "seq", 2 * far) for far in fars]
-    half_far = far_count // 2
-    near_backs = []
-    for at in range(0, far_count, half_far):
-        joined = collect([(block, 0, rows) for block in backs[at : at + half_far]], flops=HEAVY)
-        near_backs.append(swap(joined, "seq", 1))
-
     (facts,) = call(
         functools.partial(prepare_kernel, capacity, rows),
         [shape((count * frames, taps), jnp.int32)],
@@ -638,17 +656,19 @@
         flops=HEAVY,
     )
     message = 2 * taps * half + 2 * gain_rows
-    k_send, windows, gain_seq = call(
+    k_send, windows, gain_seq, lines_own, lines_peer = call(
         functools.partial(spread_kernel, count, frames, taps),
         [
             shape((message, latent_width)),
             shape((count * frames, taps * latent_width)),
             shape((gain_rows, latent_width), F32),
+            shape((frames + 16, latent_width)),
+            shape((frames + 16, latent_width)),
         ],
-        (*backs, *near_backs, sent_lines, facts),
+        (*backs, sent_lines, facts),
         scratch=[
-            pltpu.VMEM((count * rows, latent_width), BF16),
-            pltpu.VMEM((count * frames + 8, latent_width), F32),
+            pltpu.VMEM((far_count * rows, latent_width), BF16),
+            pltpu.VMEM((count * frames + 16, latent_width), F32),
         ],
         flops=HEAVY,
     )
@@ -669,22 +689,30 @@
         (k_kept, k_got, gain_seq),
     )
     y_got = swap(y_send, "book", 2)
+    lines_got = swap(after(lines_peer, y_send), "seq", 1)
     w_x, w_y, w_d = after((w_x, w_y, w_d), y_send)
     w_sum = w_sum[:far_count] + w_x.astype(F32) + w_y.astype(F32) + w_d.astype(F32)
     w_far = [w_sum[far].astype(BF16) for far in fars]
     w_total = w_sum[0]
     w_got = [swap(block, "seq", 2 * far) for far, block in zip(fars, w_far)]
+    (x_send,) = call(
+        sum_kernel,
+        [shape((taps * half + 2 * gain_rows, latent_width))],
+        (k_mine, y_got, gain_pair),
+    )
+    x_got = swap(x_send, "seq", 1)
     (feature_grad,) = call(
         feature_kernel,
         [shape(feats.shape)],
-        (feats, after(windows, y_send), w_enc),
+        (feats, lines_own, lines_got, facts, w_enc),
+        scratch=[pltpu.VMEM((frames + 16, latent_width), F32)],
         flops=HEAVY,
     )
-    y_got = after(y_got, feature_grad)
+    x_got = after(x_got, feature_grad)
     kernel_mine, gain_total = call(
         finish_kernel,
         [shape((taps * half, latent_width), F32), shape((1, width), F32)],
-        (k_mine, y_got, gain_pair),
+        (x_send, x_got),
     )
     for block in after(w_got, kernel_mine):
         w_total = w_total + block.astype(F32)

time: 68.2 us -> 66.7 us (0.978)
  waiting for transfers between devices: 25.5 us -> 20.7 us
  starting transfers between devices: 29.8 us -> 33.3 us
    ppermute x26 -> x27, waiting for transfers between devices: 25.5 us -> 20.7 us  [swap(): lax.ppermute(block, axis, [(i, i ^ mask) for i in range(lax.axis_size(axi...]
    ppermute x26 -> x27, starting transfers between devices: 29.8 us -> 33.3 us  [swap(): lax.ppermute(block, axis, [(i, i ^ mask) for i in range(lax.axis_size(axi...]
    unnamed x19 -> x16, local copies, waits for them, and re-layouts: 1.78 us -> 1.75 us
  transfers between devices with their start and end apart: 26 -> 27, of which waited for: 12 -> 12; matrix products, arithmetic and copies ran while one was open for 1% -> 0% of each run, Pallas kernels for 11% -> 11%
where the time goes in v5:
time: 66.7 us; the launch traced here: 66.5 us
  starting transfers between devices  33.3 us (50%)
  waiting for transfers between devices  20.7 us (31%)
  Pallas kernels  8.91 us (13%)
  local copies, waits for them, and re-layouts  1.79 us (3%)
  other arithmetic  0.93 us (1%)
  between operations  0.87 us (1%)
    ppermute x27, starting transfers between devices, swap(): lax.ppermute(block, axis, [(i, i ^ mask) for i in range(lax.axis_size(axi...  33.3 us
    ppermute x27, waiting for transfers between devices, swap(): lax.ppermute(block, axis, [(i, i ^ mask) for i in range(lax.axis_size(axi...  20.7 us
    pallas_call x18, Pallas kernels, call(): pl.pallas_call(kernel, out_shape=outs, in_specs=[SMEM] * smem + [VMEM] *...  8.91 us
    unnamed x16, local copies, waits for them, and re-layouts  1.75 us
  transfers between devices with their start and end apart: 27, of which 12 were waited for; matrix products, arithmetic and copies ran while one was open for 0% of the time, Pallas kernels for 11%

profile of v5, /device:TPU:0, one launch (start us, length us, event | category | flops | bytes accessed | tf_op | source)
XLA Modules:
  0.0 66.5 jit_solution(1094987062457269495)
XLA Ops:
  0.6 0.0 copy-start.5
  0.6 0.9 %copy-done.5 = bf16[1,128,512]{2,1,0:T(8,128)(2,1)S(1)} copy-done((bf16[1,128,512]{2,1,0:T(8,128)(2,1)S(1)}, bf16[1,128,512]{2,1,0:T(8,128)(2,1)}, u32[]{:S(2)}) %copy-start.5) | copy-done | bytes 131096
  1.6 0.3 shard_map.102
  1.9 0.8 %copy-done = bf16[3,512,256]{2,1,0:T(8,128)(2,1)S(1)} copy-done((bf16[3,512,256]{2,1,0:T(8,128)(2,1)S(1)}, bf16[3,512,256]{2,1,0:T(8,128)(2,1)}, u32[]{:S(2)}) %copy-start) | copy-done | bytes 786456
  2.7 1.1 %shard_map.103.refs_1_.refs_2_.refs_0_ = bf16[256,256]{1,0:T(8,128)(2,1)S(1)} custom-call(s32[8]{0:T(128)S(1)} %bitcast.33, f32[152,512]{1,0:T(8,128)S(1)} %get-tuple-element.40.padded, s32[1,128]{1,0:T(1,128)S(1)} %bitcast.32, bf16[3,512,256]{2,1,0:T(8,128)(2,1)S(1)} %copy-done), custom_call_target="tpu_custom_call" | custom-call | bytes 1024 | tf_op jit(solution)/shard_map/pallas_call | solution.py:507
  3.8 4.1 %collective-permute-start = (bf16[192,256]{1,0:T(8,128)(2,1)S(1)}, bf16[192,256]{1,0:T(8,128)(2,1)S(1)}, u32[]{:S(2)}, u32[]{:S(2)}) collective-permute-start(bf16[192,256]{1,0:T(8,128)(2,1)S(1)} %shard_map.104), channel_id=1, source_target_pairs={{0,16},{4,20},{8,24},{12,28},{16,0},{20,4},{24,8},{28,12},{1,17},{... | collective-permute-start | bytes 294920 | tf_op jit(solution)/shard_map/ppermute | solution.py:144
  7.9 4.9 %collective-permute-done.refs_1_.refs_2_.refs_3_ = bf16[192,256]{1,0:T(8,128)(2,1)S(1)} collective-permute-done((bf16[192,256]{1,0:T(8,128)(2,1)S(1)}, bf16[192,256]{1,0:T(8,128)(2,1)S(1)}, u32[]{:S(2)}, u32[]{:S(2)}) %collective-permute-start) | collective-permute-done | bytes 98336 | tf_op jit(solution)/shard_map/ppermute | solution.py:144
  12.8 0.8 %collective-permute-start.1 = (bf16[256,256]{1,0:T(8,128)(2,1)S(1)}, bf16[256,256]{1,0:T(8,128)(2,1)S(1)}, u32[]{:S(2)}, u32[]{:S(2)}) collective-permute-start(bf16[256,256]{1,0:T(8,128)(2,1)S(1)} %shard_map.106), channel_id=1, source_target_pairs={{0,8},{4,12},{8,0},{12,4},{16,24},{20,28},{24,16},{28,20},{1,9},{5... | collective-permute-start | bytes 393224 | tf_op jit(solution)/shard_map/ppermute | solution.py:144
  13.6 3.4 %collective-permute-start.12 = (bf16[1,512,128]{2,1,0:T(8,128)(2,1)S(1)}, bf16[1,512,128]{2,1,0:T(8,128)(2,1)S(1)}, u32[]{:S(2)}, u32[]{:S(2)}) collective-permute-start(bf16[1,512,128]{2,1,0:T(8,128)(2,1)S(1)} %bitcast.28), channel_id=1, source_target_pairs={{0,16},{4,20},{8,24},{12,28},{16,0},{20,4},{24,8},{28,12},{1,17},{... | collective-permute-start | bytes 393224 | tf_op jit(solution)/shard_map/ppermute | solution.py:144
  17.0 3.0 %collective-permute-done.1.refs_1_.refs_2_ = bf16[256,256]{1,0:T(8,128)(2,1)S(1)} collective-permute-done((bf16[256,256]{1,0:T(8,128)(2,1)S(1)}, bf16[256,256]{1,0:T(8,128)(2,1)S(1)}, u32[]{:S(2)}, u32[]{:S(2)}) %collective-permute-start.1) | collective-permute-done | bytes 131104 | tf_op jit(solution)/shard_map/ppermute | solution.py:144
  20.0 1.7 %collective-permute-start.2 = (bf16[384,256]{1,0:T(8,128)(2,1)S(1)}, bf16[384,256]{1,0:T(8,128)(2,1)S(1)}, u32[]{:S(2)}, u32[]{:S(2)}) collective-permute-start(bf16[384,256]{1,0:T(8,128)(2,1)S(1)} %shard_map.107), channel_id=1, source_target_pairs={{0,4},{4,0},{8,12},{12,8},{16,20},{20,16},{24,28},{28,24},{1,5},{5... | collective-permute-start | bytes 589832 | tf_op jit(solution)/shard_map/ppermute | solution.py:144
  21.6 1.6 %collective-permute-done.12 = bf16[1,512,128]{2,1,0:T(8,128)(2,1)S(1)} collective-permute-done((bf16[1,512,128]{2,1,0:T(8,128)(2,1)S(1)}, bf16[1,512,128]{2,1,0:T(8,128)(2,1)S(1)}, u32[]{:S(2)}, u32[]{:S(2)}) %collective-permute-start.12) | collective-permute-done | bytes 131104 | tf_op jit(solution)/shard_map/ppermute | solution.py:144
  23.3 0.0 copy-start.4
  23.3 0.0 copy-start.7
  23.3 2.5 %collective-permute-start.4 = (bf16[256,256]{1,0:T(8,128)(2,1)S(1)}, bf16[256,256]{1,0:T(8,128)(2,1)S(1)}, u32[]{:S(2)}, u32[]{:S(2)}) collective-permute-start(bf16[256,256]{1,0:T(8,128)(2,1)S(1)} %shard_map.109.refs_1_), channel_id=1, source_target_pairs={{0,6},{1,7},{2,4},{3,5},{4,2},{5,3},{6,0},{7,1},{8,14},{9,15},{10,... | collective-permute-start | bytes 393224 | tf_op jit(solution)/shard_map/ppermute | solution.py:144
  25.8 0.5 collective-permute-start.3
  26.3 0.3 collective-permute-start.13
  26.7 0.1 collective-permute-done.2.refs_1_.refs_2_
  26.8 0.1 collective-permute-start.6
  26.9 0.5 collective-permute-start.5
  27.4 1.8 %collective-permute-done.4.refs_4_ = bf16[256,256]{1,0:T(8,128)(2,1)S(1)} collective-permute-done((bf16[256,256]{1,0:T(8,128)(2,1)S(1)}, bf16[256,256]{1,0:T(8,128)(2,1)S(1)}, u32[]{:S(2)}, u32[]{:S(2)}) %collective-permute-start.4) | collective-permute-done | bytes 131104 | tf_op jit(solution)/shard_map/ppermute | solution.py:144
  29.3 1.5 %collective-permute-done.3.refs_3_ = bf16[256,256]{1,0:T(8,128)(2,1)S(1)} collective-permute-done((bf16[256,256]{1,0:T(8,128)(2,1)S(1)}, bf16[256,256]{1,0:T(8,128)(2,1)S(1)}, u32[]{:S(2)}, u32[]{:S(2)}) %collective-permute-start.3) | collective-permute-done | bytes 131104 | tf_op jit(solution)/shard_map/ppermute | solution.py:144
  30.8 1.3 %collective-permute-start.14 = (bf16[2,512,128]{2,1,0:T(8,128)(2,1)S(1)}, bf16[2,512,128]{2,1,0:T(8,128)(2,1)S(1)}, u32[]{:S(2)}, u32[]{:S(2)}) collective-permute-start(bf16[2,512,128]{2,1,0:T(8,128)(2,1)S(1)} %pad_maximum_fusion.refs_0_), channel_id=1, source_target_pairs={{0,4},{4,0},{8,12},{12,8},{16,20},{20,16},{24,28},{28,24},{1,5},{5... | collective-permute-start | bytes 786440 | tf_op jit(solution)/shard_map/ppermute | solution.py:144
  32.2 0.6 collective-permute-done.13.refs_1_
  32.7 0.5 collective-permute-start.15
  33.3 1.4 %shard_map.110 = (bf16[144,256]{1,0:T(8,128)(2,1)S(1)}, bf16[144,2048]{1,0:T(8,128)(2,1)S(1)}, bf16[144,256]{1,0:T(8,128)(2,1)S(1)}, f32[8,128]{1,0:T(8,128)S(1)}) custom-call(bf16[256,256]{1,0:T(8,128)(2,1)S(1)} %shard_map.108.refs_0_, bf16[256,256]{1,0:T(8,128)(2,1)S(1)} %shard_map.109.refs_1_, ...), custom_call_target="tpu_custom_call" | custom-call | flops 20000000000 | bytes 1024 | tf_op jit(solution)/shard_map/pallas_call | solution.py:507
  34.7 3.6 %collective-permute-start.11 = (bf16[144,256]{1,0:T(8,128)(2,1)S(1)}, bf16[144,256]{1,0:T(8,128)(2,1)S(1)}, u32[]{:S(2)}, u32[]{:S(2)}) collective-permute-start(bf16[144,256]{1,0:T(8,128)(2,1)S(1)} %get-tuple-element.42.refs_0_), channel_id=1, source_target_pairs={{0,24},{4,28},{8,16},{12,20},{16,8},{20,12},{24,0},{28,4},{1,25},{... | collective-permute-start | bytes 221192 | tf_op jit(solution)/shard_map/ppermute | solution.py:144
  38.3 0.5 shard_map.111
  38.8 0.1 collective-permute-start.16
  38.9 1.3 %shard_map.112.refs_5_.facts_ref = s32[1024,3]{1,0:T(8,128)S(1)} custom-call(s32[8]{0:T(128)S(1)} %bitcast.34, f32[8,128]{1,0:T(8,128)S(1)} %get-tuple-element.49.owners_ref), custom_call_target="tpu_custom_call" | custom-call | flops 20000000000 | bytes 1024 | tf_op jit(solution)/shard_map/pallas_call | solution.py:507
  40.2 0.6 collective-permute-done.16
  40.8 0.9 %collective-permute-start.9 = (bf16[144,256]{1,0:T(8,128)(2,1)S(1)}, bf16[144,256]{1,0:T(8,128)(2,1)S(1)}, u32[]{:S(2)}, u32[]{:S(2)}) collective-permute-start(bf16[144,256]{1,0:T(8,128)(2,1)S(1)} %get-tuple-element.42.refs_0_), channel_id=1, source_target_pairs={{0,8},{4,12},{8,0},{12,4},{16,24},{20,28},{24,16},{28,20},{1,9},{5... | collective-permute-start | bytes 221192 | tf_op jit(solution)/shard_map/ppermute | solution.py:144
  41.6 0.2 convert_add_fusion
  41.9 0.0 collective-permute-done.14.refs_2_
  41.9 2.5 %collective-permute-start.23 = (bf16[4,64,256]{2,1,0:T(8,128)(2,1)S(1)}, bf16[4,64,256]{2,1,0:T(8,128)(2,1)S(1)}, u32[]{:S(2)}, u32[]{:S(2)}) collective-permute-start(bf16[4,64,256]{2,1,0:T(8,128)(2,1)S(1)} %get-tuple-element.80), channel_id=1, source_target_pairs={{0,6},{1,7},{2,4},{3,5},{4,2},{5,3},{6,0},{7,1},{8,14},{9,15},{10,... | collective-permute-start | bytes 393224 | tf_op jit(solution)/shard_map/ppermute | solution.py:144
  44.4 0.8 %collective-permute-done.15.refs_3_ = bf16[2,512,128]{2,1,0:T(8,128)(2,1)S(1)} collective-permute-done((bf16[2,512,128]{2,1,0:T(8,128)(2,1)S(1)}, bf16[2,512,128]{2,1,0:T(8,128)(2,1)S(1)}, u32[]{:S(2)}, u32[]{:S(2)}) %collective-permute-start.15) | collective-permute-done | bytes 262176 | tf_op jit(solution)/shard_map/ppermute | solution.py:144
  45.2 1.8 %collective-permute-start.22 = (bf16[4,64,256]{2,1,0:T(8,128)(2,1)S(1)}, bf16[4,64,256]{2,1,0:T(8,128)(2,1)S(1)}, u32[]{:S(2)}, u32[]{:S(2)}) collective-permute-start(bf16[4,64,256]{2,1,0:T(8,128)(2,1)S(1)} %get-tuple-element.81), channel_id=1, source_target_pairs={{0,2},{1,3},{2,0},{3,1},{4,6},{5,7},{6,4},{7,5},{8,10},{9,11},{10,... | collective-permute-start | bytes 393224 | tf_op jit(solution)/shard_map/ppermute | solution.py:144
  46.9 0.3 shard_map.113
  47.2 0.0 collective-permute-done.11.refs_3_
  47.2 0.9 %collective-permute-start.21 = (bf16[4,64,256]{2,1,0:T(8,128)(2,1)S(1)}, bf16[4,64,256]{2,1,0:T(8,128)(2,1)S(1)}, u32[]{:S(2)}, u32[]{:S(2)}) collective-permute-start(bf16[4,64,256]{2,1,0:T(8,128)(2,1)S(1)} %get-tuple-element.82), channel_id=1, source_target_pairs={{0,4},{4,0},{8,12},{12,8},{16,20},{20,16},{24,28},{28,24},{1,5},{5... | collective-permute-start | bytes 393224 | tf_op jit(solution)/shard_map/ppermute | solution.py:144
  48.1 0.0 collective-permute-done.10.refs_2_
  48.1 0.0 collective-permute-done.9.refs_1_
  48.1 1.4 %shard_map.114 = (bf16[784,256]{1,0:T(8,128)(2,1)S(1)}, bf16[1024,768]{1,0:T(8,128)(2,1)S(1)}, f32[8,256]{1,0:T(8,128)S(1)}, bf16[144,256]{1,0:T(8,128)(2,1)S(1)}, bf16[144,256]{1,0:T(8,128)(2,1)S(1)}) custom-call(bf16[144,256]{1,0:T(8,128)(2,1)S(1)} %get-tuple-element.42.refs_0_, bf16[144,256]{1,0:T(8,128)(2,1)S(1)} %collective-permute-done.9.refs_1_, ...), custom_call_target="tpu_custom_call" | custom-call | flops 20000000000 | bytes 1024 | tf_op jit(solution)/shard_map/pallas_call | solution.py:507
  49.6 0.1 collective-permute-start.17
  49.7 0.6 shard_map.115.kept_ref
  50.3 1.1 %collective-permute-done.17.got_ref = bf16[784,256]{1,0:T(8,128)(2,1)S(1)} collective-permute-done((bf16[784,256]{1,0:T(8,128)(2,1)S(1)}, bf16[784,256]{1,0:T(8,128)(2,1)S(1)}, u32[]{:S(2)}, u32[]{:S(2)}) %collective-permute-start.17) | collective-permute-done | bytes 401440 | tf_op jit(solution)/shard_map/ppermute | solution.py:144
  51.4 0.1 shard_map.116
  51.5 0.8 %collective-permute-start.19 = (bf16[400,256]{1,0:T(8,128)(2,1)S(1)}, bf16[400,256]{1,0:T(8,128)(2,1)S(1)}, u32[]{:S(2)}, u32[]{:S(2)}) collective-permute-start(bf16[400,256]{1,0:T(8,128)(2,1)S(1)} %get-tuple-element.63), channel_id=1, source_target_pairs={{0,2},{1,3},{2,0},{3,1},{4,6},{5,7},{6,4},{7,5},{8,10},{9,11},{10,... | collective-permute-start | bytes 614408 | tf_op jit(solution)/shard_map/ppermute | solution.py:144
  52.3 0.0 collective-permute-done.22
  52.3 0.0 collective-permute-done.21
  52.3 0.8 %collective-permute-start.18 = (bf16[144,256]{1,0:T(8,128)(2,1)S(1)}, bf16[144,256]{1,0:T(8,128)(2,1)S(1)}, u32[]{:S(2)}, u32[]{:S(2)}) collective-permute-start(bf16[144,256]{1,0:T(8,128)(2,1)S(1)} %get-tuple-element.64), channel_id=1, source_target_pairs={{0,4},{4,0},{8,12},{12,8},{16,20},{20,16},{24,28},{28,24},{1,5},{5... | collective-permute-start | bytes 221192 | tf_op jit(solution)/shard_map/ppermute | solution.py:144
  53.1 0.1 fusion.7
  53.2 4.3 %collective-permute-start.26 = (bf16[64,256]{1,0:T(8,128)(2,1)S(1)}, bf16[64,256]{1,0:T(8,128)(2,1)S(1)}, u32[]{:S(2)}, u32[]{:S(2)}) collective-permute-start(bf16[64,256]{1,0:T(8,128)(2,1)S(1)} %get-tuple-element.83), channel_id=1, source_target_pairs={{0,24},{4,28},{8,16},{12,20},{16,8},{20,12},{24,0},{28,4},{1,25},{... | collective-permute-start | bytes 98312 | tf_op jit(solution)/shard_map/ppermute | solution.py:144
  57.5 0.0 collective-permute-start.25
  57.5 0.6 collective-permute-start.24
  58.2 0.5 collective-permute-done.19.got_ref
  58.7 1.2 %collective-permute-start.20 = (bf16[400,256]{1,0:T(8,128)(2,1)S(1)}, bf16[400,256]{1,0:T(8,128)(2,1)S(1)}, u32[]{:S(2)}, u32[]{:S(2)}) collective-permute-start(bf16[400,256]{1,0:T(8,128)(2,1)S(1)} %shard_map.118.mine_ref), channel_id=1, source_target_pairs={{0,4},{4,0},{8,12},{12,8},{16,20},{20,16},{24,28},{28,24},{1,5},{5... | collective-permute-start | bytes 614408 | tf_op jit(solution)/shard_map/ppermute | solution.py:144
  59.9 0.0 collective-permute-done.18.got_ref
  59.9 1.1 %shard_map.117 = bf16[128,512]{1,0:T(8,128)(2,1)} custom-call(bf16[128,512]{1,0:T(8,128)(2,1)S(1)} %bitcast.37, bf16[144,256]{1,0:T(8,128)(2,1)S(1)} %get-tuple-element.57.own_ref, bf16[144,256]{1,0:T(8,128)(2,1)S(1)} %collective-permute-done.18.got_ref, s32[1024,3]{1,0:T(8,128)S(1)} %shard_map.112.refs_5_.facts_ref, bf16[3,512,256]{2,1,0:T(8,128)(2,1)S(1)} %copy-done), custom_call_target="tpu_custom_call" | custom-call | flops 20000000000 | bytes 1024 | tf_op jit(solution)/shard_map/pallas_call | solution.py:507
  61.0 4.0 %collective-permute-done.20.got_ref = bf16[400,256]{1,0:T(8,128)(2,1)S(1)} collective-permute-done((bf16[400,256]{1,0:T(8,128)(2,1)S(1)}, bf16[400,256]{1,0:T(8,128)(2,1)S(1)}, u32[]{:S(2)}, u32[]{:S(2)}) %collective-permute-start.20) | collective-permute-done | bytes 204832 | tf_op jit(solution)/shard_map/ppermute | solution.py:144
  65.1 0.8 %shard_map.119 = (f32[384,256]{1,0:T(8,128)}, f32[1,2048]{1,0:T(1,128)}) custom-call(bf16[400,256]{1,0:T(8,128)(2,1)S(1)} %shard_map.118.mine_ref, bf16[400,256]{1,0:T(8,128)(2,1)S(1)} %collective-permute-done.20.got_ref), custom_call_target="tpu_custom_call" | custom-call | bytes 1024 | tf_op jit(solution)/shard_map/pallas_call | solution.py:507
  65.8 0.0 collective-permute-done.26
  65.9 0.0 collective-permute-done.25
  65.9 0.6 fusion.5
  (30 shorter events, 0.2 us)
Async XLA Ops:
  0.6 0.9 %copy-start.5 = (bf16[1,128,512]{2,1,0:T(8,128)(2,1)S(1)}, bf16[1,128,512]{2,1,0:T(8,128)(2,1)}, u32[]{:S(2)}) copy-start(bf16[1,128,512]{2,1,0:T(8,128)(2,1)} %param.7) | copy-start | bytes 393220
  1.5 1.1 %copy-start = (bf16[3,512,256]{2,1,0:T(8,128)(2,1)S(1)}, bf16[3,512,256]{2,1,0:T(8,128)(2,1)}, u32[]{:S(2)}) copy-start(bf16[3,512,256]{2,1,0:T(8,128)(2,1)} %w_ref.3) | copy-start | bytes 2359300
  1.5 1.1 %copy-start.2 = (s32[1,128,1]{1,2,0:T(1,128)S(1)}, s32[1,128,1]{1,2,0:T(1,128)}, u32[]{:S(2)}) copy-start(s32[1,128,1]{1,2,0:T(1,128)} %param.9) | copy-start | bytes 1540
  1.5 1.1 %copy-start.3 = (s32[1,8]{1,0:T(1,128)S(1)}, s32[1,8]{1,0:T(1,128)}, u32[]{:S(2)}) copy-start(s32[1,8]{1,0:T(1,128)} %param.8) | copy-start | bytes 100
  1.5 2.2 %copy-start.1 = (bf16[256,64]{0,1:T(8,128)(2,1)S(1)}, bf16[256,64]{0,1:T(8,128)(2,1)}, u32[]{:S(2)}) copy-start(bf16[256,64]{0,1:T(8,128)(2,1)} %param.11) | copy-start | bytes 98308
  3.8 9.0 %collective-permute-start = (bf16[192,256]{1,0:T(8,128)(2,1)S(1)}, bf16[192,256]{1,0:T(8,128)(2,1)S(1)}, u32[]{:S(2)}, u32[]{:S(2)}) collective-permute-start(bf16[192,256]{1,0:T(8,128)(2,1)S(1)} %shard_map.104), channel_id=1, source_target_pairs={{0,16},{4,20},{8,24},{12,28},{16,0},{20,4},{24,8},{28,12},{1,17},{... | collective-permute-start | bytes 294920 | tf_op jit(solution)/shard_map/ppermute | solution.py:144
  12.8 7.1 %collective-permute-start.1 = (bf16[256,256]{1,0:T(8,128)(2,1)S(1)}, bf16[256,256]{1,0:T(8,128)(2,1)S(1)}, u32[]{:S(2)}, u32[]{:S(2)}) collective-permute-start(bf16[256,256]{1,0:T(8,128)(2,1)S(1)} %shard_map.106), channel_id=1, source_target_pairs={{0,8},{4,12},{8,0},{12,4},{16,24},{20,28},{24,16},{28,20},{1,9},{5... | collective-permute-start | bytes 393224 | tf_op jit(solution)/shard_map/ppermute | solution.py:144
  13.6 9.6 %collective-permute-start.12 = (bf16[1,512,128]{2,1,0:T(8,128)(2,1)S(1)}, bf16[1,512,128]{2,1,0:T(8,128)(2,1)S(1)}, u32[]{:S(2)}, u32[]{:S(2)}) collective-permute-start(bf16[1,512,128]{2,1,0:T(8,128)(2,1)S(1)} %bitcast.28), channel_id=1, source_target_pairs={{0,16},{4,20},{8,24},{12,28},{16,0},{20,4},{24,8},{28,12},{1,17},{... | collective-permute-start | bytes 393224 | tf_op jit(solution)/shard_map/ppermute | solution.py:144
  20.0 6.8 %collective-permute-start.2 = (bf16[384,256]{1,0:T(8,128)(2,1)S(1)}, bf16[384,256]{1,0:T(8,128)(2,1)S(1)}, u32[]{:S(2)}, u32[]{:S(2)}) collective-permute-start(bf16[384,256]{1,0:T(8,128)(2,1)S(1)} %shard_map.107), channel_id=1, source_target_pairs={{0,4},{4,0},{8,12},{12,8},{16,20},{20,16},{24,28},{28,24},{1,5},{5... | collective-permute-start | bytes 589832 | tf_op jit(solution)/shard_map/ppermute | solution.py:144
  23.3 10.0 %copy-start.4 = (bf16[1,136,2048]{2,1,0:T(8,128)(2,1)S(1)}, bf16[1,136,2048]{2,1,0:T(8,128)(2,1)}, u32[]{:S(2)}) copy-start(bf16[1,136,2048]{2,1,0:T(8,128)(2,1)} %param.13) | copy-start | bytes 1671172
  23.3 10.0 %copy-start.7 = (f32[2048]{0:T(1024)S(1)}, f32[2048]{0:T(1024)}, u32[]{:S(2)}) copy-start(f32[2048]{0:T(1024)} %param.12) | copy-start | bytes 24580
  23.3 5.9 %collective-permute-start.4 = (bf16[256,256]{1,0:T(8,128)(2,1)S(1)}, bf16[256,256]{1,0:T(8,128)(2,1)S(1)}, u32[]{:S(2)}, u32[]{:S(2)}) collective-permute-start(bf16[256,256]{1,0:T(8,128)(2,1)S(1)} %shard_map.109.refs_1_), channel_id=1, source_target_pairs={{0,6},{1,7},{2,4},{3,5},{4,2},{5,3},{6,0},{7,1},{8,14},{9,15},{10,... | collective-permute-start | bytes 393224 | tf_op jit(solution)/shard_map/ppermute | solution.py:144
  25.8 5.0 %collective-permute-start.3 = (bf16[256,256]{1,0:T(8,128)(2,1)S(1)}, bf16[256,256]{1,0:T(8,128)(2,1)S(1)}, u32[]{:S(2)}, u32[]{:S(2)}) collective-permute-start(bf16[256,256]{1,0:T(8,128)(2,1)S(1)} %shard_map.109.refs_1_), channel_id=1, source_target_pairs={{0,2},{1,3},{2,0},{3,1},{4,6},{5,7},{6,4},{7,5},{8,10},{9,11},{10,... | collective-permute-start | bytes 393224 | tf_op jit(solution)/shard_map/ppermute | solution.py:144
  26.3 6.4 %collective-permute-start.13 = (bf16[2,512,128]{2,1,0:T(8,128)(2,1)S(1)}, bf16[2,512,128]{2,1,0:T(8,128)(2,1)S(1)}, u32[]{:S(2)}, u32[]{:S(2)}) collective-permute-start(bf16[2,512,128]{2,1,0:T(8,128)(2,1)S(1)} %pad_maximum_fusion.refs_0_), channel_id=1, source_target_pairs={{0,8},{4,12},{8,0},{12,4},{16,24},{20,28},{24,16},{28,20},{1,9},{5... | collective-permute-start | bytes 786440 | tf_op jit(solution)/shard_map/ppermute | solution.py:144
  26.8 6.4 %collective-permute-start.6 = (bf16[384,256]{1,0:T(8,128)(2,1)S(1)}, bf16[384,256]{1,0:T(8,128)(2,1)S(1)}, u32[]{:S(2)}, u32[]{:S(2)}) collective-permute-start(bf16[384,256]{1,0:T(8,128)(2,1)S(1)} %collective-permute-done.2.refs_1_.refs_2_), channel_id=1, source_target_pairs={{0,1},{1,0},{2,3},{3,2},{4,5},{5,4},{6,7},{7,6},{8,9},{9,8},{10,11... | collective-permute-start | bytes 589832 | tf_op jit(solution)/shard_map/ppermute | solution.py:144
  26.9 3.9 %collective-permute-start.5 = (bf16[256,256]{1,0:T(8,128)(2,1)S(1)}, bf16[256,256]{1,0:T(8,128)(2,1)S(1)}, u32[]{:S(2)}, u32[]{:S(2)}) collective-permute-start(bf16[256,256]{1,0:T(8,128)(2,1)S(1)} %shard_map.109.refs_1_), channel_id=1, source_target_pairs={{0,1},{1,0},{2,3},{3,2},{4,5},{5,4},{6,7},{7,6},{8,9},{9,8},{10,11... | collective-permute-start | bytes 393224 | tf_op jit(solution)/shard_map/ppermute | solution.py:144
  29.3 4.0 %collective-permute-start.8 = (bf16[256,256]{1,0:T(8,128)(2,1)S(1)}, bf16[256,256]{1,0:T(8,128)(2,1)S(1)}, u32[]{:S(2)}, u32[]{:S(2)}) collective-permute-start(bf16[256,256]{1,0:T(8,128)(2,1)S(1)} %collective-permute-done.4.refs_4_), channel_id=1, source_target_pairs={{0,1},{1,0},{2,3},{3,2},{4,5},{5,4},{6,7},{7,6},{8,9},{9,8},{10,11... | collective-permute-start | bytes 393224 | tf_op jit(solution)/shard_map/ppermute | solution.py:144
  30.8 2.5 %collective-permute-start.7 = (bf16[256,256]{1,0:T(8,128)(2,1)S(1)}, bf16[256,256]{1,0:T(8,128)(2,1)S(1)}, u32[]{:S(2)}, u32[]{:S(2)}) collective-permute-start(bf16[256,256]{1,0:T(8,128)(2,1)S(1)} %collective-permute-done.3.refs_3_), channel_id=1, source_target_pairs={{0,1},{1,0},{2,3},{3,2},{4,5},{5,4},{6,7},{7,6},{8,9},{9,8},{10,11... | collective-permute-start | bytes 393224 | tf_op jit(solution)/shard_map/ppermute | solution.py:144
  30.8 11.1 %collective-permute-start.14 = (bf16[2,512,128]{2,1,0:T(8,128)(2,1)S(1)}, bf16[2,512,128]{2,1,0:T(8,128)(2,1)S(1)}, u32[]{:S(2)}, u32[]{:S(2)}) collective-permute-start(bf16[2,512,128]{2,1,0:T(8,128)(2,1)S(1)} %pad_maximum_fusion.refs_0_), channel_id=1, source_target_pairs={{0,4},{4,0},{8,12},{12,8},{16,20},{20,16},{24,28},{28,24},{1,5},{5... | collective-permute-start | bytes 786440 | tf_op jit(solution)/shard_map/ppermute | solution.py:144
  32.7 12.4 %collective-permute-start.15 = (bf16[2,512,128]{2,1,0:T(8,128)(2,1)S(1)}, bf16[2,512,128]{2,1,0:T(8,128)(2,1)S(1)}, u32[]{:S(2)}, u32[]{:S(2)}) collective-permute-start(bf16[2,512,128]{2,1,0:T(8,128)(2,1)S(1)} %collective-permute-done.13.refs_1_), channel_id=1, source_target_pairs={{0,4},{4,0},{8,12},{12,8},{16,20},{20,16},{24,28},{28,24},{1,5},{5... | collective-permute-start | bytes 786440 | tf_op jit(solution)/shard_map/ppermute | solution.py:144
  34.7 12.5 %collective-permute-start.11 = (bf16[144,256]{1,0:T(8,128)(2,1)S(1)}, bf16[144,256]{1,0:T(8,128)(2,1)S(1)}, u32[]{:S(2)}, u32[]{:S(2)}) collective-permute-start(bf16[144,256]{1,0:T(8,128)(2,1)S(1)} %get-tuple-element.42.refs_0_), channel_id=1, source_target_pairs={{0,24},{4,28},{8,16},{12,20},{16,8},{20,12},{24,0},{28,4},{1,25},{... | collective-permute-start | bytes 221192 | tf_op jit(solution)/shard_map/ppermute | solution.py:144
  38.3 9.9 %collective-permute-start.10 = (bf16[144,256]{1,0:T(8,128)(2,1)S(1)}, bf16[144,256]{1,0:T(8,128)(2,1)S(1)}, u32[]{:S(2)}, u32[]{:S(2)}) collective-permute-start(bf16[144,256]{1,0:T(8,128)(2,1)S(1)} %get-tuple-element.42.refs_0_), channel_id=1, source_target_pairs={{0,16},{4,20},{8,24},{12,28},{16,0},{20,4},{24,8},{28,12},{1,17},{... | collective-permute-start | bytes 221192 | tf_op jit(solution)/shard_map/ppermute | solution.py:144
  38.8 2.0 %collective-permute-start.16 = (bf16[16,64,256]{2,1,0:T(8,128)(2,1)S(1)}, bf16[16,64,256]{2,1,0:T(8,128)(2,1)S(1)}, u32[]{:S(2)}, u32[]{:S(2)}) collective-permute-start(bf16[16,64,256]{2,1,0:T(8,128)(2,1)S(1)} %get-tuple-element.48), channel_id=1, source_target_pairs={{0,1},{1,0},{2,3},{3,2},{4,5},{5,4},{6,7},{7,6},{8,9},{9,8},{10,11... | collective-permute-start | bytes 1572872 | tf_op jit(solution)/shard_map/ppermute | solution.py:144
  40.8 7.4 %collective-permute-start.9 = (bf16[144,256]{1,0:T(8,128)(2,1)S(1)}, bf16[144,256]{1,0:T(8,128)(2,1)S(1)}, u32[]{:S(2)}, u32[]{:S(2)}) collective-permute-start(bf16[144,256]{1,0:T(8,128)(2,1)S(1)} %get-tuple-element.42.refs_0_), channel_id=1, source_target_pairs={{0,8},{4,12},{8,0},{12,4},{16,24},{20,28},{24,16},{28,20},{1,9},{5... | collective-permute-start | bytes 221192 | tf_op jit(solution)/shard_map/ppermute | solution.py:144
  41.9 10.4 %collective-permute-start.23 = (bf16[4,64,256]{2,1,0:T(8,128)(2,1)S(1)}, bf16[4,64,256]{2,1,0:T(8,128)(2,1)S(1)}, u32[]{:S(2)}, u32[]{:S(2)}) collective-permute-start(bf16[4,64,256]{2,1,0:T(8,128)(2,1)S(1)} %get-tuple-element.80), channel_id=1, source_target_pairs={{0,6},{1,7},{2,4},{3,5},{4,2},{5,3},{6,0},{7,1},{8,14},{9,15},{10,... | collective-permute-start | bytes 393224 | tf_op jit(solution)/shard_map/ppermute | solution.py:144
  45.2 7.1 %collective-permute-start.22 = (bf16[4,64,256]{2,1,0:T(8,128)(2,1)S(1)}, bf16[4,64,256]{2,1,0:T(8,128)(2,1)S(1)}, u32[]{:S(2)}, u32[]{:S(2)}) collective-permute-start(bf16[4,64,256]{2,1,0:T(8,128)(2,1)S(1)} %get-tuple-element.81), channel_id=1, source_target_pairs={{0,2},{1,3},{2,0},{3,1},{4,6},{5,7},{6,4},{7,5},{8,10},{9,11},{10,... | collective-permute-start | bytes 393224 | tf_op jit(solution)/shard_map/ppermute | solution.py:144
  47.2 5.1 %collective-permute-start.21 = (bf16[4,64,256]{2,1,0:T(8,128)(2,1)S(1)}, bf16[4,64,256]{2,1,0:T(8,128)(2,1)S(1)}, u32[]{:S(2)}, u32[]{:S(2)}) collective-permute-start(bf16[4,64,256]{2,1,0:T(8,128)(2,1)S(1)} %get-tuple-element.82), channel_id=1, source_target_pairs={{0,4},{4,0},{8,12},{12,8},{16,20},{20,16},{24,28},{28,24},{1,5},{5... | collective-permute-start | bytes 393224 | tf_op jit(solution)/shard_map/ppermute | solution.py:144
  49.6 1.8 %collective-permute-start.17 = (bf16[784,256]{1,0:T(8,128)(2,1)S(1)}, bf16[784,256]{1,0:T(8,128)(2,1)S(1)}, u32[]{:S(2)}, u32[]{:S(2)}) collective-permute-start(bf16[784,256]{1,0:T(8,128)(2,1)S(1)} %get-tuple-element.61), channel_id=1, source_target_pairs={{0,1},{1,0},{2,3},{3,2},{4,5},{5,4},{6,7},{7,6},{8,9},{9,8},{10,11... | collective-permute-start | bytes 1204232 | tf_op jit(solution)/shard_map/ppermute | solution.py:144
  51.4 8.5 %copy-start.6 = (bf16[1,128,512]{2,1,0:T(8,128)(2,1)S(1)}, bf16[1,128,512]{2,1,0:T(8,128)(2,1)}, u32[]{:S(2)}) copy-start(bf16[1,128,512]{2,1,0:T(8,128)(2,1)} %param.7) | copy-start | bytes 393220
  51.5 7.2 %collective-permute-start.19 = (bf16[400,256]{1,0:T(8,128)(2,1)S(1)}, bf16[400,256]{1,0:T(8,128)(2,1)S(1)}, u32[]{:S(2)}, u32[]{:S(2)}) collective-permute-start(bf16[400,256]{1,0:T(8,128)(2,1)S(1)} %get-tuple-element.63), channel_id=1, source_target_pairs={{0,2},{1,3},{2,0},{3,1},{4,6},{5,7},{6,4},{7,5},{8,10},{9,11},{10,... | collective-permute-start | bytes 614408 | tf_op jit(solution)/shard_map/ppermute | solution.py:144
  52.3 7.6 %collective-permute-start.18 = (bf16[144,256]{1,0:T(8,128)(2,1)S(1)}, bf16[144,256]{1,0:T(8,128)(2,1)S(1)}, u32[]{:S(2)}, u32[]{:S(2)}) collective-permute-start(bf16[144,256]{1,0:T(8,128)(2,1)S(1)} %get-tuple-element.64), channel_id=1, source_target_pairs={{0,4},{4,0},{8,12},{12,8},{16,20},{20,16},{24,28},{28,24},{1,5},{5... | collective-permute-start | bytes 221192 | tf_op jit(solution)/shard_map/ppermute | solution.py:144
  53.2 12.6 %collective-permute-start.26 = (bf16[64,256]{1,0:T(8,128)(2,1)S(1)}, bf16[64,256]{1,0:T(8,128)(2,1)S(1)}, u32[]{:S(2)}, u32[]{:S(2)}) collective-permute-start(bf16[64,256]{1,0:T(8,128)(2,1)S(1)} %get-tuple-element.83), channel_id=1, source_target_pairs={{0,24},{4,28},{8,16},{12,20},{16,8},{20,12},{24,0},{28,4},{1,25},{... | collective-permute-start | bytes 98312 | tf_op jit(solution)/shard_map/ppermute | solution.py:144
  57.5 8.3 %collective-permute-start.25 = (bf16[64,256]{1,0:T(8,128)(2,1)S(1)}, bf16[64,256]{1,0:T(8,128)(2,1)S(1)}, u32[]{:S(2)}, u32[]{:S(2)}) collective-permute-start(bf16[64,256]{1,0:T(8,128)(2,1)S(1)} %get-tuple-element.84), channel_id=1, source_target_pairs={{0,16},{4,20},{8,24},{12,28},{16,0},{20,4},{24,8},{28,12},{1,17},{... | collective-permute-start | bytes 98312 | tf_op jit(solution)/shard_map/ppermute | solution.py:144
  57.5 8.3 %collective-permute-start.24 = (bf16[64,256]{1,0:T(8,128)(2,1)S(1)}, bf16[64,256]{1,0:T(8,128)(2,1)S(1)}, u32[]{:S(2)}, u32[]{:S(2)}) collective-permute-start(bf16[64,256]{1,0:T(8,128)(2,1)S(1)} %get-tuple-element.85), channel_id=1, source_target_pairs={{0,8},{4,12},{8,0},{12,4},{16,24},{20,28},{24,16},{28,20},{1,9},{5... | collective-permute-start | bytes 98312 | tf_op jit(solution)/shard_map/ppermute | solution.py:144
  58.7 6.4 %collective-permute-start.20 = (bf16[400,256]{1,0:T(8,128)(2,1)S(1)}, bf16[400,256]{1,0:T(8,128)(2,1)S(1)}, u32[]{:S(2)}, u32[]{:S(2)}) collective-permute-start(bf16[400,256]{1,0:T(8,128)(2,1)S(1)} %shard_map.118.mine_ref), channel_id=1, source_target_pairs={{0,4},{4,0},{8,12},{12,8},{16,20},{20,16},{24,28},{28,24},{1,5},{5... | collective-permute-start | bytes 614408 | tf_op jit(solution)/shard_map/ppermute | solution.py:144

commit v6 on v5

--- a/solution.py
+++ b/solution.py
@@ -9,7 +9,7 @@
 
 F32 = jnp.float32
 BF16 = jnp.bfloat16
-HEAVY = 20000000000
+HEAVY = 8000000000
 VMEM = pl.BlockSpec(memory_space=pltpu.VMEM)
 SMEM = pl.BlockSpec(memory_space=pltpu.SMEM)
 
@@ -714,7 +714,7 @@
         [shape((taps * half, latent_width), F32), shape((1, width), F32)],
         (x_send, x_got),
     )
-    for block in after(w_got, kernel_mine):
+    for block in after(w_got, x_send):
         w_total = w_total + block.astype(F32)
     return (
         feature_grad[None],

time: 66.7 us -> 65.6 us (0.984)
  local copies, waits for them, and re-layouts: 1.79 us -> 1.04 us
    unnamed x16, local copies, waits for them, and re-layouts: 1.75 us -> 1 us
  transfers between devices with their start and end apart: 27 -> 27, of which waited for: 12 -> 12; matrix products, arithmetic and copies ran while one was open for 0% -> 1% of each run, Pallas kernels for 11% -> 10%
where the time goes in v6:
time: 65.6 us; the launch traced here: 65.4 us
  starting transfers between devices  33.1 us (50%)
  waiting for transfers between devices  20.5 us (31%)
  Pallas kernels  8.95 us (14%)
  local copies, waits for them, and re-layouts  1.04 us (2%)
  between operations  0.92 us (1%)
  other arithmetic  0.89 us (1%)
    ppermute x27, starting transfers between devices, swap(): lax.ppermute(block, axis, [(i, i ^ mask) for i in range(lax.axis_size(axi...  33.1 us
    ppermute x27, waiting for transfers between devices, swap(): lax.ppermute(block, axis, [(i, i ^ mask) for i in range(lax.axis_size(axi...  20.5 us
    pallas_call x18, Pallas kernels, call(): pl.pallas_call(kernel, out_shape=outs, in_specs=[SMEM] * smem + [VMEM] *...  8.95 us
  transfers between devices with their start and end apart: 27, of which 12 were waited for; matrix products, arithmetic and copies ran while one was open for 1% of the time, Pallas kernels for 10%

profile of v6, /device:TPU:0, one launch (start us, length us, event | category | flops | bytes accessed | tf_op | source)
XLA Modules:
  0.0 65.4 jit_solution(9174707766231311408)
XLA Ops:
  0.7 0.0 copy-start.5
  0.7 1.0 %copy-done.5 = bf16[1,128,512]{2,1,0:T(8,128)(2,1)S(1)} copy-done((bf16[1,128,512]{2,1,0:T(8,128)(2,1)S(1)}, bf16[1,128,512]{2,1,0:T(8,128)(2,1)}, u32[]{:S(2)}) %copy-start.5) | copy-done | bytes 131096
  1.6 0.3 shard_map.102
  2.0 1.1 %shard_map.103.refs_1_.refs_2_.refs_0_ = bf16[256,256]{1,0:T(8,128)(2,1)S(1)} custom-call(s32[8]{0:T(128)S(1)} %bitcast.33, f32[152,512]{1,0:T(8,128)S(1)} %get-tuple-element.40.padded, s32[1,128]{1,0:T(1,128)S(1)} %bitcast.32, bf16[3,512,256]{2,1,0:T(8,128)(2,1)S(1)} %copy-done), custom_call_target="tpu_custom_call" | custom-call | bytes 1024 | tf_op jit(solution)/shard_map/pallas_call | solution.py:507
  3.1 4.1 %collective-permute-start = (bf16[192,256]{1,0:T(8,128)(2,1)S(1)}, bf16[192,256]{1,0:T(8,128)(2,1)S(1)}, u32[]{:S(2)}, u32[]{:S(2)}) collective-permute-start(bf16[192,256]{1,0:T(8,128)(2,1)S(1)} %shard_map.104), channel_id=1, source_target_pairs={{0,16},{4,20},{8,24},{12,28},{16,0},{20,4},{24,8},{28,12},{1,17},{... | collective-permute-start | bytes 294920 | tf_op jit(solution)/shard_map/ppermute | solution.py:144
  7.2 4.9 %collective-permute-done.refs_1_.refs_2_.refs_3_ = bf16[192,256]{1,0:T(8,128)(2,1)S(1)} collective-permute-done((bf16[192,256]{1,0:T(8,128)(2,1)S(1)}, bf16[192,256]{1,0:T(8,128)(2,1)S(1)}, u32[]{:S(2)}, u32[]{:S(2)}) %collective-permute-start) | collective-permute-done | bytes 98336 | tf_op jit(solution)/shard_map/ppermute | solution.py:144
  12.1 0.8 %collective-permute-start.1 = (bf16[256,256]{1,0:T(8,128)(2,1)S(1)}, bf16[256,256]{1,0:T(8,128)(2,1)S(1)}, u32[]{:S(2)}, u32[]{:S(2)}) collective-permute-start(bf16[256,256]{1,0:T(8,128)(2,1)S(1)} %shard_map.106), channel_id=1, source_target_pairs={{0,8},{4,12},{8,0},{12,4},{16,24},{20,28},{24,16},{28,20},{1,9},{5... | collective-permute-start | bytes 393224 | tf_op jit(solution)/shard_map/ppermute | solution.py:144
  12.9 3.4 %collective-permute-start.12 = (bf16[1,512,128]{2,1,0:T(8,128)(2,1)S(1)}, bf16[1,512,128]{2,1,0:T(8,128)(2,1)S(1)}, u32[]{:S(2)}, u32[]{:S(2)}) collective-permute-start(bf16[1,512,128]{2,1,0:T(8,128)(2,1)S(1)} %bitcast.28), channel_id=1, source_target_pairs={{0,16},{4,20},{8,24},{12,28},{16,0},{20,4},{24,8},{28,12},{1,17},{... | collective-permute-start | bytes 393224 | tf_op jit(solution)/shard_map/ppermute | solution.py:144
  16.3 3.0 %collective-permute-done.1.refs_1_.refs_2_ = bf16[256,256]{1,0:T(8,128)(2,1)S(1)} collective-permute-done((bf16[256,256]{1,0:T(8,128)(2,1)S(1)}, bf16[256,256]{1,0:T(8,128)(2,1)S(1)}, u32[]{:S(2)}, u32[]{:S(2)}) %collective-permute-start.1) | collective-permute-done | bytes 131104 | tf_op jit(solution)/shard_map/ppermute | solution.py:144
  19.3 1.6 %collective-permute-start.2 = (bf16[384,256]{1,0:T(8,128)(2,1)S(1)}, bf16[384,256]{1,0:T(8,128)(2,1)S(1)}, u32[]{:S(2)}, u32[]{:S(2)}) collective-permute-start(bf16[384,256]{1,0:T(8,128)(2,1)S(1)} %shard_map.107), channel_id=1, source_target_pairs={{0,4},{4,0},{8,12},{12,8},{16,20},{20,16},{24,28},{28,24},{1,5},{5... | collective-permute-start | bytes 589832 | tf_op jit(solution)/shard_map/ppermute | solution.py:144
  20.9 1.6 %collective-permute-done.12 = bf16[1,512,128]{2,1,0:T(8,128)(2,1)S(1)} collective-permute-done((bf16[1,512,128]{2,1,0:T(8,128)(2,1)S(1)}, bf16[1,512,128]{2,1,0:T(8,128)(2,1)S(1)}, u32[]{:S(2)}, u32[]{:S(2)}) %collective-permute-start.12) | collective-permute-done | bytes 131104 | tf_op jit(solution)/shard_map/ppermute | solution.py:144
  22.6 0.0 copy-start.4
  22.6 0.0 copy-start.7
  22.6 2.5 %collective-permute-start.4 = (bf16[256,256]{1,0:T(8,128)(2,1)S(1)}, bf16[256,256]{1,0:T(8,128)(2,1)S(1)}, u32[]{:S(2)}, u32[]{:S(2)}) collective-permute-start(bf16[256,256]{1,0:T(8,128)(2,1)S(1)} %shard_map.109.refs_1_), channel_id=1, source_target_pairs={{0,6},{1,7},{2,4},{3,5},{4,2},{5,3},{6,0},{7,1},{8,14},{9,15},{10,... | collective-permute-start | bytes 393224 | tf_op jit(solution)/shard_map/ppermute | solution.py:144
  25.1 0.5 collective-permute-start.3
  25.6 0.3 collective-permute-start.13
  26.0 0.1 collective-permute-done.2.refs_1_.refs_2_
  26.1 0.1 collective-permute-start.6
  26.2 0.5 collective-permute-start.5
  26.7 1.8 %collective-permute-done.4.refs_4_ = bf16[256,256]{1,0:T(8,128)(2,1)S(1)} collective-permute-done((bf16[256,256]{1,0:T(8,128)(2,1)S(1)}, bf16[256,256]{1,0:T(8,128)(2,1)S(1)}, u32[]{:S(2)}, u32[]{:S(2)}) %collective-permute-start.4) | collective-permute-done | bytes 131104 | tf_op jit(solution)/shard_map/ppermute | solution.py:144
  28.6 0.0 collective-permute-start.8
  28.6 1.5 %collective-permute-done.3.refs_3_ = bf16[256,256]{1,0:T(8,128)(2,1)S(1)} collective-permute-done((bf16[256,256]{1,0:T(8,128)(2,1)S(1)}, bf16[256,256]{1,0:T(8,128)(2,1)S(1)}, u32[]{:S(2)}, u32[]{:S(2)}) %collective-permute-start.3) | collective-permute-done | bytes 131104 | tf_op jit(solution)/shard_map/ppermute | solution.py:144
  30.1 0.0 collective-permute-start.7
  30.1 0.0 collective-permute-done.5.refs_5_
  30.1 1.3 %collective-permute-start.14 = (bf16[2,512,128]{2,1,0:T(8,128)(2,1)S(1)}, bf16[2,512,128]{2,1,0:T(8,128)(2,1)S(1)}, u32[]{:S(2)}, u32[]{:S(2)}) collective-permute-start(bf16[2,512,128]{2,1,0:T(8,128)(2,1)S(1)} %pad_maximum_fusion.refs_0_), channel_id=1, source_target_pairs={{0,4},{4,0},{8,12},{12,8},{16,20},{20,16},{24,28},{28,24},{1,5},{5... | collective-permute-start | bytes 786440 | tf_op jit(solution)/shard_map/ppermute | solution.py:144
  31.5 0.6 collective-permute-done.13.refs_1_
  32.0 0.5 collective-permute-start.15
  32.6 1.4 %shard_map.110 = (bf16[144,256]{1,0:T(8,128)(2,1)S(1)}, bf16[144,2048]{1,0:T(8,128)(2,1)S(1)}, bf16[144,256]{1,0:T(8,128)(2,1)S(1)}, f32[8,128]{1,0:T(8,128)S(1)}) custom-call(bf16[256,256]{1,0:T(8,128)(2,1)S(1)} %shard_map.108.refs_0_, bf16[256,256]{1,0:T(8,128)(2,1)S(1)} %shard_map.109.refs_1_, ...), custom_call_target="tpu_custom_call" | custom-call | flops 8000000000 | bytes 1024 | tf_op jit(solution)/shard_map/pallas_call | solution.py:507
  34.0 3.6 %collective-permute-start.11 = (bf16[144,256]{1,0:T(8,128)(2,1)S(1)}, bf16[144,256]{1,0:T(8,128)(2,1)S(1)}, u32[]{:S(2)}, u32[]{:S(2)}) collective-permute-start(bf16[144,256]{1,0:T(8,128)(2,1)S(1)} %get-tuple-element.42.refs_0_), channel_id=1, source_target_pairs={{0,24},{4,28},{8,16},{12,20},{16,8},{20,12},{24,0},{28,4},{1,25},{... | collective-permute-start | bytes 221192 | tf_op jit(solution)/shard_map/ppermute | solution.py:144
  37.6 0.0 collective-permute-start.10
  37.6 0.5 shard_map.111
  38.1 0.1 collective-permute-start.16
  38.2 1.3 %shard_map.112.refs_5_.facts_ref = s32[1024,3]{1,0:T(8,128)S(1)} custom-call(s32[8]{0:T(128)S(1)} %bitcast.34, f32[8,128]{1,0:T(8,128)S(1)} %get-tuple-element.49.owners_ref), custom_call_target="tpu_custom_call" | custom-call | flops 8000000000 | bytes 1024 | tf_op jit(solution)/shard_map/pallas_call | solution.py:507
  39.4 0.6 collective-permute-done.16
  40.1 0.9 %collective-permute-start.9 = (bf16[144,256]{1,0:T(8,128)(2,1)S(1)}, bf16[144,256]{1,0:T(8,128)(2,1)S(1)}, u32[]{:S(2)}, u32[]{:S(2)}) collective-permute-start(bf16[144,256]{1,0:T(8,128)(2,1)S(1)} %get-tuple-element.42.refs_0_), channel_id=1, source_target_pairs={{0,8},{4,12},{8,0},{12,4},{16,24},{20,28},{24,16},{28,20},{1,9},{5... | collective-permute-start | bytes 221192 | tf_op jit(solution)/shard_map/ppermute | solution.py:144
  40.9 0.2 convert_add_fusion
  41.2 2.5 %collective-permute-start.23 = (bf16[4,64,256]{2,1,0:T(8,128)(2,1)S(1)}, bf16[4,64,256]{2,1,0:T(8,128)(2,1)S(1)}, u32[]{:S(2)}, u32[]{:S(2)}) collective-permute-start(bf16[4,64,256]{2,1,0:T(8,128)(2,1)S(1)} %get-tuple-element.80), channel_id=1, source_target_pairs={{0,6},{1,7},{2,4},{3,5},{4,2},{5,3},{6,0},{7,1},{8,14},{9,15},{10,... | collective-permute-start | bytes 393224 | tf_op jit(solution)/shard_map/ppermute | solution.py:144
  43.7 0.8 %collective-permute-done.15.refs_3_ = bf16[2,512,128]{2,1,0:T(8,128)(2,1)S(1)} collective-permute-done((bf16[2,512,128]{2,1,0:T(8,128)(2,1)S(1)}, bf16[2,512,128]{2,1,0:T(8,128)(2,1)S(1)}, u32[]{:S(2)}, u32[]{:S(2)}) %collective-permute-start.15) | collective-permute-done | bytes 262176 | tf_op jit(solution)/shard_map/ppermute | solution.py:144
  44.4 1.8 %collective-permute-start.22 = (bf16[4,64,256]{2,1,0:T(8,128)(2,1)S(1)}, bf16[4,64,256]{2,1,0:T(8,128)(2,1)S(1)}, u32[]{:S(2)}, u32[]{:S(2)}) collective-permute-start(bf16[4,64,256]{2,1,0:T(8,128)(2,1)S(1)} %get-tuple-element.81), channel_id=1, source_target_pairs={{0,2},{1,3},{2,0},{3,1},{4,6},{5,7},{6,4},{7,5},{8,10},{9,11},{10,... | collective-permute-start | bytes 393224 | tf_op jit(solution)/shard_map/ppermute | solution.py:144
  46.2 0.3 shard_map.113
  46.5 0.9 %collective-permute-start.21 = (bf16[4,64,256]{2,1,0:T(8,128)(2,1)S(1)}, bf16[4,64,256]{2,1,0:T(8,128)(2,1)S(1)}, u32[]{:S(2)}, u32[]{:S(2)}) collective-permute-start(bf16[4,64,256]{2,1,0:T(8,128)(2,1)S(1)} %get-tuple-element.82), channel_id=1, source_target_pairs={{0,4},{4,0},{8,12},{12,8},{16,20},{20,16},{24,28},{28,24},{1,5},{5... | collective-permute-start | bytes 393224 | tf_op jit(solution)/shard_map/ppermute | solution.py:144
  47.4 0.0 collective-permute-done.10.refs_2_
  47.5 0.0 collective-permute-done.9.refs_1_
  47.5 1.5 %shard_map.114 = (bf16[784,256]{1,0:T(8,128)(2,1)S(1)}, bf16[1024,768]{1,0:T(8,128)(2,1)S(1)}, f32[8,256]{1,0:T(8,128)S(1)}, bf16[144,256]{1,0:T(8,128)(2,1)S(1)}, bf16[144,256]{1,0:T(8,128)(2,1)S(1)}) custom-call(bf16[144,256]{1,0:T(8,128)(2,1)S(1)} %get-tuple-element.42.refs_0_, bf16[144,256]{1,0:T(8,128)(2,1)S(1)} %collective-permute-done.9.refs_1_, ...), custom_call_target="tpu_custom_call" | custom-call | flops 8000000000 | bytes 1024 | tf_op jit(solution)/shard_map/pallas_call | solution.py:507
  48.9 0.1 collective-permute-start.17
  49.0 0.6 shard_map.115.kept_ref
  49.6 0.0 copy-start.6
  49.6 1.1 %collective-permute-done.17.got_ref = bf16[784,256]{1,0:T(8,128)(2,1)S(1)} collective-permute-done((bf16[784,256]{1,0:T(8,128)(2,1)S(1)}, bf16[784,256]{1,0:T(8,128)(2,1)S(1)}, u32[]{:S(2)}, u32[]{:S(2)}) %collective-permute-start.17) | collective-permute-done | bytes 401440 | tf_op jit(solution)/shard_map/ppermute | solution.py:144
  50.7 0.1 shard_map.116
  50.8 0.8 %collective-permute-start.19 = (bf16[400,256]{1,0:T(8,128)(2,1)S(1)}, bf16[400,256]{1,0:T(8,128)(2,1)S(1)}, u32[]{:S(2)}, u32[]{:S(2)}) collective-permute-start(bf16[400,256]{1,0:T(8,128)(2,1)S(1)} %get-tuple-element.63), channel_id=1, source_target_pairs={{0,2},{1,3},{2,0},{3,1},{4,6},{5,7},{6,4},{7,5},{8,10},{9,11},{10,... | collective-permute-start | bytes 614408 | tf_op jit(solution)/shard_map/ppermute | solution.py:144
  51.6 0.0 collective-permute-done.23
  51.6 0.8 %collective-permute-start.18 = (bf16[144,256]{1,0:T(8,128)(2,1)S(1)}, bf16[144,256]{1,0:T(8,128)(2,1)S(1)}, u32[]{:S(2)}, u32[]{:S(2)}) collective-permute-start(bf16[144,256]{1,0:T(8,128)(2,1)S(1)} %get-tuple-element.64), channel_id=1, source_target_pairs={{0,4},{4,0},{8,12},{12,8},{16,20},{20,16},{24,28},{28,24},{1,5},{5... | collective-permute-start | bytes 221192 | tf_op jit(solution)/shard_map/ppermute | solution.py:144
  52.4 0.1 fusion.7
  52.5 4.3 %collective-permute-start.26 = (bf16[64,256]{1,0:T(8,128)(2,1)S(1)}, bf16[64,256]{1,0:T(8,128)(2,1)S(1)}, u32[]{:S(2)}, u32[]{:S(2)}) collective-permute-start(bf16[64,256]{1,0:T(8,128)(2,1)S(1)} %get-tuple-element.83), channel_id=1, source_target_pairs={{0,24},{4,28},{8,16},{12,20},{16,8},{20,12},{24,0},{28,4},{1,25},{... | collective-permute-start | bytes 98312 | tf_op jit(solution)/shard_map/ppermute | solution.py:144
  56.8 0.0 collective-permute-start.25
  56.8 0.6 collective-permute-start.24
  57.5 0.0 collective-permute-done.18.got_ref
  57.5 1.1 %shard_map.117 = bf16[128,512]{1,0:T(8,128)(2,1)} custom-call(bf16[128,512]{1,0:T(8,128)(2,1)S(1)} %bitcast.37, bf16[144,256]{1,0:T(8,128)(2,1)S(1)} %get-tuple-element.57.own_ref, bf16[144,256]{1,0:T(8,128)(2,1)S(1)} %collective-permute-done.18.got_ref, s32[1024,3]{1,0:T(8,128)S(1)} %shard_map.112.refs_5_.facts_ref, bf16[3,512,256]{2,1,0:T(8,128)(2,1)S(1)} %copy-done), custom_call_target="tpu_custom_call" | custom-call | flops 8000000000 | bytes 1024 | tf_op jit(solution)/shard_map/pallas_call | solution.py:507
  58.6 1.0 %collective-permute-start.20 = (bf16[400,256]{1,0:T(8,128)(2,1)S(1)}, bf16[400,256]{1,0:T(8,128)(2,1)S(1)}, u32[]{:S(2)}, u32[]{:S(2)}) collective-permute-start(bf16[400,256]{1,0:T(8,128)(2,1)S(1)} %shard_map.118.mine_ref), channel_id=1, source_target_pairs={{0,4},{4,0},{8,12},{12,8},{16,20},{20,16},{24,28},{28,24},{1,5},{5... | collective-permute-start | bytes 614408 | tf_op jit(solution)/shard_map/ppermute | solution.py:144
  59.6 2.0 %collective-permute-done.25 = bf16[64,256]{1,0:T(8,128)(2,1)S(1)} collective-permute-done((bf16[64,256]{1,0:T(8,128)(2,1)S(1)}, bf16[64,256]{1,0:T(8,128)(2,1)S(1)}, u32[]{:S(2)}, u32[]{:S(2)}) %collective-permute-start.25) | collective-permute-done | bytes 32800 | tf_op jit(solution)/shard_map/ppermute | solution.py:144
  61.6 0.0 collective-permute-done.24
  61.6 0.6 fusion.5
  62.3 2.4 %collective-permute-done.20.got_ref = bf16[400,256]{1,0:T(8,128)(2,1)S(1)} collective-permute-done((bf16[400,256]{1,0:T(8,128)(2,1)S(1)}, bf16[400,256]{1,0:T(8,128)(2,1)S(1)}, u32[]{:S(2)}, u32[]{:S(2)}) %collective-permute-start.20) | collective-permute-done | bytes 204832 | tf_op jit(solution)/shard_map/ppermute | solution.py:144
  64.7 0.8 %shard_map.119 = (f32[384,256]{1,0:T(8,128)}, f32[1,2048]{1,0:T(1,128)}) custom-call(bf16[400,256]{1,0:T(8,128)(2,1)S(1)} %shard_map.118.mine_ref, bf16[400,256]{1,0:T(8,128)(2,1)S(1)} %collective-permute-done.20.got_ref), custom_call_target="tpu_custom_call" | custom-call | bytes 1024 | tf_op jit(solution)/shard_map/pallas_call | solution.py:507
  (30 shorter events, 0.2 us)
Async XLA Ops:
  0.6 1.3 %copy-start = (bf16[3,512,256]{2,1,0:T(8,128)(2,1)S(1)}, bf16[3,512,256]{2,1,0:T(8,128)(2,1)}, u32[]{:S(2)}) copy-start(bf16[3,512,256]{2,1,0:T(8,128)(2,1)} %w_ref.3) | copy-start | bytes 2359300
  0.6 1.3 %copy-start.2 = (s32[1,128,1]{1,2,0:T(1,128)S(1)}, s32[1,128,1]{1,2,0:T(1,128)}, u32[]{:S(2)}) copy-start(s32[1,128,1]{1,2,0:T(1,128)} %param.9) | copy-start | bytes 1540
  0.7 1.3 %copy-start.3 = (s32[1,8]{1,0:T(1,128)S(1)}, s32[1,8]{1,0:T(1,128)}, u32[]{:S(2)}) copy-start(s32[1,8]{1,0:T(1,128)} %param.8) | copy-start | bytes 100
  0.7 1.0 %copy-start.5 = (bf16[1,128,512]{2,1,0:T(8,128)(2,1)S(1)}, bf16[1,128,512]{2,1,0:T(8,128)(2,1)}, u32[]{:S(2)}) copy-start(bf16[1,128,512]{2,1,0:T(8,128)(2,1)} %param.7) | copy-start | bytes 393220
  1.6 1.4 %copy-start.1 = (bf16[256,64]{0,1:T(8,128)(2,1)S(1)}, bf16[256,64]{0,1:T(8,128)(2,1)}, u32[]{:S(2)}) copy-start(bf16[256,64]{0,1:T(8,128)(2,1)} %param.11) | copy-start | bytes 98308
  3.1 9.0 %collective-permute-start = (bf16[192,256]{1,0:T(8,128)(2,1)S(1)}, bf16[192,256]{1,0:T(8,128)(2,1)S(1)}, u32[]{:S(2)}, u32[]{:S(2)}) collective-permute-start(bf16[192,256]{1,0:T(8,128)(2,1)S(1)} %shard_map.104), channel_id=1, source_target_pairs={{0,16},{4,20},{8,24},{12,28},{16,0},{20,4},{24,8},{28,12},{1,17},{... | collective-permute-start | bytes 294920 | tf_op jit(solution)/shard_map/ppermute | solution.py:144
  12.1 7.1 %collective-permute-start.1 = (bf16[256,256]{1,0:T(8,128)(2,1)S(1)}, bf16[256,256]{1,0:T(8,128)(2,1)S(1)}, u32[]{:S(2)}, u32[]{:S(2)}) collective-permute-start(bf16[256,256]{1,0:T(8,128)(2,1)S(1)} %shard_map.106), channel_id=1, source_target_pairs={{0,8},{4,12},{8,0},{12,4},{16,24},{20,28},{24,16},{28,20},{1,9},{5... | collective-permute-start | bytes 393224 | tf_op jit(solution)/shard_map/ppermute | solution.py:144
  12.9 9.6 %collective-permute-start.12 = (bf16[1,512,128]{2,1,0:T(8,128)(2,1)S(1)}, bf16[1,512,128]{2,1,0:T(8,128)(2,1)S(1)}, u32[]{:S(2)}, u32[]{:S(2)}) collective-permute-start(bf16[1,512,128]{2,1,0:T(8,128)(2,1)S(1)} %bitcast.28), channel_id=1, source_target_pairs={{0,16},{4,20},{8,24},{12,28},{16,0},{20,4},{24,8},{28,12},{1,17},{... | collective-permute-start | bytes 393224 | tf_op jit(solution)/shard_map/ppermute | solution.py:144
  19.3 6.8 %collective-permute-start.2 = (bf16[384,256]{1,0:T(8,128)(2,1)S(1)}, bf16[384,256]{1,0:T(8,128)(2,1)S(1)}, u32[]{:S(2)}, u32[]{:S(2)}) collective-permute-start(bf16[384,256]{1,0:T(8,128)(2,1)S(1)} %shard_map.107), channel_id=1, source_target_pairs={{0,4},{4,0},{8,12},{12,8},{16,20},{20,16},{24,28},{28,24},{1,5},{5... | collective-permute-start | bytes 589832 | tf_op jit(solution)/shard_map/ppermute | solution.py:144
  22.6 10.0 %copy-start.4 = (bf16[1,136,2048]{2,1,0:T(8,128)(2,1)S(1)}, bf16[1,136,2048]{2,1,0:T(8,128)(2,1)}, u32[]{:S(2)}) copy-start(bf16[1,136,2048]{2,1,0:T(8,128)(2,1)} %param.13) | copy-start | bytes 1671172
  22.6 10.0 %copy-start.7 = (f32[2048]{0:T(1024)S(1)}, f32[2048]{0:T(1024)}, u32[]{:S(2)}) copy-start(f32[2048]{0:T(1024)} %param.12) | copy-start | bytes 24580
  22.6 5.9 %collective-permute-start.4 = (bf16[256,256]{1,0:T(8,128)(2,1)S(1)}, bf16[256,256]{1,0:T(8,128)(2,1)S(1)}, u32[]{:S(2)}, u32[]{:S(2)}) collective-permute-start(bf16[256,256]{1,0:T(8,128)(2,1)S(1)} %shard_map.109.refs_1_), channel_id=1, source_target_pairs={{0,6},{1,7},{2,4},{3,5},{4,2},{5,3},{6,0},{7,1},{8,14},{9,15},{10,... | collective-permute-start | bytes 393224 | tf_op jit(solution)/shard_map/ppermute | solution.py:144
  25.1 5.0 %collective-permute-start.3 = (bf16[256,256]{1,0:T(8,128)(2,1)S(1)}, bf16[256,256]{1,0:T(8,128)(2,1)S(1)}, u32[]{:S(2)}, u32[]{:S(2)}) collective-permute-start(bf16[256,256]{1,0:T(8,128)(2,1)S(1)} %shard_map.109.refs_1_), channel_id=1, source_target_pairs={{0,2},{1,3},{2,0},{3,1},{4,6},{5,7},{6,4},{7,5},{8,10},{9,11},{10,... | collective-permute-start | bytes 393224 | tf_op jit(solution)/shard_map/ppermute | solution.py:144
  25.6 6.4 %collective-permute-start.13 = (bf16[2,512,128]{2,1,0:T(8,128)(2,1)S(1)}, bf16[2,512,128]{2,1,0:T(8,128)(2,1)S(1)}, u32[]{:S(2)}, u32[]{:S(2)}) collective-permute-start(bf16[2,512,128]{2,1,0:T(8,128)(2,1)S(1)} %pad_maximum_fusion.refs_0_), channel_id=1, source_target_pairs={{0,8},{4,12},{8,0},{12,4},{16,24},{20,28},{24,16},{28,20},{1,9},{5... | collective-permute-start | bytes 786440 | tf_op jit(solution)/shard_map/ppermute | solution.py:144
  26.1 6.4 %collective-permute-start.6 = (bf16[384,256]{1,0:T(8,128)(2,1)S(1)}, bf16[384,256]{1,0:T(8,128)(2,1)S(1)}, u32[]{:S(2)}, u32[]{:S(2)}) collective-permute-start(bf16[384,256]{1,0:T(8,128)(2,1)S(1)} %collective-permute-done.2.refs_1_.refs_2_), channel_id=1, source_target_pairs={{0,1},{1,0},{2,3},{3,2},{4,5},{5,4},{6,7},{7,6},{8,9},{9,8},{10,11... | collective-permute-start | bytes 589832 | tf_op jit(solution)/shard_map/ppermute | solution.py:144
  26.2 3.9 %collective-permute-start.5 = (bf16[256,256]{1,0:T(8,128)(2,1)S(1)}, bf16[256,256]{1,0:T(8,128)(2,1)S(1)}, u32[]{:S(2)}, u32[]{:S(2)}) collective-permute-start(bf16[256,256]{1,0:T(8,128)(2,1)S(1)} %shard_map.109.refs_1_), channel_id=1, source_target_pairs={{0,1},{1,0},{2,3},{3,2},{4,5},{5,4},{6,7},{7,6},{8,9},{9,8},{10,11... | collective-permute-start | bytes 393224 | tf_op jit(solution)/shard_map/ppermute | solution.py:144
  28.6 4.0 %collective-permute-start.8 = (bf16[256,256]{1,0:T(8,128)(2,1)S(1)}, bf16[256,256]{1,0:T(8,128)(2,1)S(1)}, u32[]{:S(2)}, u32[]{:S(2)}) collective-permute-start(bf16[256,256]{1,0:T(8,128)(2,1)S(1)} %collective-permute-done.4.refs_4_), channel_id=1, source_target_pairs={{0,1},{1,0},{2,3},{3,2},{4,5},{5,4},{6,7},{7,6},{8,9},{9,8},{10,11... | collective-permute-start | bytes 393224 | tf_op jit(solution)/shard_map/ppermute | solution.py:144
  30.1 2.5 %collective-permute-start.7 = (bf16[256,256]{1,0:T(8,128)(2,1)S(1)}, bf16[256,256]{1,0:T(8,128)(2,1)S(1)}, u32[]{:S(2)}, u32[]{:S(2)}) collective-permute-start(bf16[256,256]{1,0:T(8,128)(2,1)S(1)} %collective-permute-done.3.refs_3_), channel_id=1, source_target_pairs={{0,1},{1,0},{2,3},{3,2},{4,5},{5,4},{6,7},{7,6},{8,9},{9,8},{10,11... | collective-permute-start | bytes 393224 | tf_op jit(solution)/shard_map/ppermute | solution.py:144
  30.1 11.0 %collective-permute-start.14 = (bf16[2,512,128]{2,1,0:T(8,128)(2,1)S(1)}, bf16[2,512,128]{2,1,0:T(8,128)(2,1)S(1)}, u32[]{:S(2)}, u32[]{:S(2)}) collective-permute-start(bf16[2,512,128]{2,1,0:T(8,128)(2,1)S(1)} %pad_maximum_fusion.refs_0_), channel_id=1, source_target_pairs={{0,4},{4,0},{8,12},{12,8},{16,20},{20,16},{24,28},{28,24},{1,5},{5... | collective-permute-start | bytes 786440 | tf_op jit(solution)/shard_map/ppermute | solution.py:144
  32.0 12.4 %collective-permute-start.15 = (bf16[2,512,128]{2,1,0:T(8,128)(2,1)S(1)}, bf16[2,512,128]{2,1,0:T(8,128)(2,1)S(1)}, u32[]{:S(2)}, u32[]{:S(2)}) collective-permute-start(bf16[2,512,128]{2,1,0:T(8,128)(2,1)S(1)} %collective-permute-done.13.refs_1_), channel_id=1, source_target_pairs={{0,4},{4,0},{8,12},{12,8},{16,20},{20,16},{24,28},{28,24},{1,5},{5... | collective-permute-start | bytes 786440 | tf_op jit(solution)/shard_map/ppermute | solution.py:144
  34.0 12.5 %collective-permute-start.11 = (bf16[144,256]{1,0:T(8,128)(2,1)S(1)}, bf16[144,256]{1,0:T(8,128)(2,1)S(1)}, u32[]{:S(2)}, u32[]{:S(2)}) collective-permute-start(bf16[144,256]{1,0:T(8,128)(2,1)S(1)} %get-tuple-element.42.refs_0_), channel_id=1, source_target_pairs={{0,24},{4,28},{8,16},{12,20},{16,8},{20,12},{24,0},{28,4},{1,25},{... | collective-permute-start | bytes 221192 | tf_op jit(solution)/shard_map/ppermute | solution.py:144
  37.6 9.9 %collective-permute-start.10 = (bf16[144,256]{1,0:T(8,128)(2,1)S(1)}, bf16[144,256]{1,0:T(8,128)(2,1)S(1)}, u32[]{:S(2)}, u32[]{:S(2)}) collective-permute-start(bf16[144,256]{1,0:T(8,128)(2,1)S(1)} %get-tuple-element.42.refs_0_), channel_id=1, source_target_pairs={{0,16},{4,20},{8,24},{12,28},{16,0},{20,4},{24,8},{28,12},{1,17},{... | collective-permute-start | bytes 221192 | tf_op jit(solution)/shard_map/ppermute | solution.py:144
  38.1 2.0 %collective-permute-start.16 = (bf16[16,64,256]{2,1,0:T(8,128)(2,1)S(1)}, bf16[16,64,256]{2,1,0:T(8,128)(2,1)S(1)}, u32[]{:S(2)}, u32[]{:S(2)}) collective-permute-start(bf16[16,64,256]{2,1,0:T(8,128)(2,1)S(1)} %get-tuple-element.48), channel_id=1, source_target_pairs={{0,1},{1,0},{2,3},{3,2},{4,5},{5,4},{6,7},{7,6},{8,9},{9,8},{10,11... | collective-permute-start | bytes 1572872 | tf_op jit(solution)/shard_map/ppermute | solution.py:144
  40.1 7.4 %collective-permute-start.9 = (bf16[144,256]{1,0:T(8,128)(2,1)S(1)}, bf16[144,256]{1,0:T(8,128)(2,1)S(1)}, u32[]{:S(2)}, u32[]{:S(2)}) collective-permute-start(bf16[144,256]{1,0:T(8,128)(2,1)S(1)} %get-tuple-element.42.refs_0_), channel_id=1, source_target_pairs={{0,8},{4,12},{8,0},{12,4},{16,24},{20,28},{24,16},{28,20},{1,9},{5... | collective-permute-start | bytes 221192 | tf_op jit(solution)/shard_map/ppermute | solution.py:144
  41.2 10.5 %collective-permute-start.23 = (bf16[4,64,256]{2,1,0:T(8,128)(2,1)S(1)}, bf16[4,64,256]{2,1,0:T(8,128)(2,1)S(1)}, u32[]{:S(2)}, u32[]{:S(2)}) collective-permute-start(bf16[4,64,256]{2,1,0:T(8,128)(2,1)S(1)} %get-tuple-element.80), channel_id=1, source_target_pairs={{0,6},{1,7},{2,4},{3,5},{4,2},{5,3},{6,0},{7,1},{8,14},{9,15},{10,... | collective-permute-start | bytes 393224 | tf_op jit(solution)/shard_map/ppermute | solution.py:144
  44.4 7.2 %collective-permute-start.22 = (bf16[4,64,256]{2,1,0:T(8,128)(2,1)S(1)}, bf16[4,64,256]{2,1,0:T(8,128)(2,1)S(1)}, u32[]{:S(2)}, u32[]{:S(2)}) collective-permute-start(bf16[4,64,256]{2,1,0:T(8,128)(2,1)S(1)} %get-tuple-element.81), channel_id=1, source_target_pairs={{0,2},{1,3},{2,0},{3,1},{4,6},{5,7},{6,4},{7,5},{8,10},{9,11},{10,... | collective-permute-start | bytes 393224 | tf_op jit(solution)/shard_map/ppermute | solution.py:144
  46.5 5.1 %collective-permute-start.21 = (bf16[4,64,256]{2,1,0:T(8,128)(2,1)S(1)}, bf16[4,64,256]{2,1,0:T(8,128)(2,1)S(1)}, u32[]{:S(2)}, u32[]{:S(2)}) collective-permute-start(bf16[4,64,256]{2,1,0:T(8,128)(2,1)S(1)} %get-tuple-element.82), channel_id=1, source_target_pairs={{0,4},{4,0},{8,12},{12,8},{16,20},{20,16},{24,28},{28,24},{1,5},{5... | collective-permute-start | bytes 393224 | tf_op jit(solution)/shard_map/ppermute | solution.py:144
  48.9 1.8 %collective-permute-start.17 = (bf16[784,256]{1,0:T(8,128)(2,1)S(1)}, bf16[784,256]{1,0:T(8,128)(2,1)S(1)}, u32[]{:S(2)}, u32[]{:S(2)}) collective-permute-start(bf16[784,256]{1,0:T(8,128)(2,1)S(1)} %get-tuple-element.61), channel_id=1, source_target_pairs={{0,1},{1,0},{2,3},{3,2},{4,5},{5,4},{6,7},{7,6},{8,9},{9,8},{10,11... | collective-permute-start | bytes 1204232 | tf_op jit(solution)/shard_map/ppermute | solution.py:144
  49.6 7.9 %copy-start.6 = (bf16[1,128,512]{2,1,0:T(8,128)(2,1)S(1)}, bf16[1,128,512]{2,1,0:T(8,128)(2,1)}, u32[]{:S(2)}) copy-start(bf16[1,128,512]{2,1,0:T(8,128)(2,1)} %param.7) | copy-start | bytes 393220
  50.8 7.7 %collective-permute-start.19 = (bf16[400,256]{1,0:T(8,128)(2,1)S(1)}, bf16[400,256]{1,0:T(8,128)(2,1)S(1)}, u32[]{:S(2)}, u32[]{:S(2)}) collective-permute-start(bf16[400,256]{1,0:T(8,128)(2,1)S(1)} %get-tuple-element.63), channel_id=1, source_target_pairs={{0,2},{1,3},{2,0},{3,1},{4,6},{5,7},{6,4},{7,5},{8,10},{9,11},{10,... | collective-permute-start | bytes 614408 | tf_op jit(solution)/shard_map/ppermute | solution.py:144
  51.6 5.8 %collective-permute-start.18 = (bf16[144,256]{1,0:T(8,128)(2,1)S(1)}, bf16[144,256]{1,0:T(8,128)(2,1)S(1)}, u32[]{:S(2)}, u32[]{:S(2)}) collective-permute-start(bf16[144,256]{1,0:T(8,128)(2,1)S(1)} %get-tuple-element.64), channel_id=1, source_target_pairs={{0,4},{4,0},{8,12},{12,8},{16,20},{20,16},{24,28},{28,24},{1,5},{5... | collective-permute-start | bytes 221192 | tf_op jit(solution)/shard_map/ppermute | solution.py:144
  52.5 7.1 %collective-permute-start.26 = (bf16[64,256]{1,0:T(8,128)(2,1)S(1)}, bf16[64,256]{1,0:T(8,128)(2,1)S(1)}, u32[]{:S(2)}, u32[]{:S(2)}) collective-permute-start(bf16[64,256]{1,0:T(8,128)(2,1)S(1)} %get-tuple-element.83), channel_id=1, source_target_pairs={{0,24},{4,28},{8,16},{12,20},{16,8},{20,12},{24,0},{28,4},{1,25},{... | collective-permute-start | bytes 98312 | tf_op jit(solution)/shard_map/ppermute | solution.py:144
  56.8 4.8 %collective-permute-start.25 = (bf16[64,256]{1,0:T(8,128)(2,1)S(1)}, bf16[64,256]{1,0:T(8,128)(2,1)S(1)}, u32[]{:S(2)}, u32[]{:S(2)}) collective-permute-start(bf16[64,256]{1,0:T(8,128)(2,1)S(1)} %get-tuple-element.84), channel_id=1, source_target_pairs={{0,16},{4,20},{8,24},{12,28},{16,0},{20,4},{24,8},{28,12},{1,17},{... | collective-permute-start | bytes 98312 | tf_op jit(solution)/shard_map/ppermute | solution.py:144
  56.8 4.8 %collective-permute-start.24 = (bf16[64,256]{1,0:T(8,128)(2,1)S(1)}, bf16[64,256]{1,0:T(8,128)(2,1)S(1)}, u32[]{:S(2)}, u32[]{:S(2)}) collective-permute-start(bf16[64,256]{1,0:T(8,128)(2,1)S(1)} %get-tuple-element.85), channel_id=1, source_target_pairs={{0,8},{4,12},{8,0},{12,4},{16,24},{20,28},{24,16},{28,20},{1,9},{5... | collective-permute-start | bytes 98312 | tf_op jit(solution)/shard_map/ppermute | solution.py:144
  58.6 6.1 %collective-permute-start.20 = (bf16[400,256]{1,0:T(8,128)(2,1)S(1)}, bf16[400,256]{1,0:T(8,128)(2,1)S(1)}, u32[]{:S(2)}, u32[]{:S(2)}) collective-permute-start(bf16[400,256]{1,0:T(8,128)(2,1)S(1)} %shard_map.118.mine_ref), channel_id=1, source_target_pairs={{0,4},{4,0},{8,12},{12,8},{16,20},{20,16},{24,28},{28,24},{1,5},{5... | collective-permute-start | bytes 614408 | tf_op jit(solution)/shard_map/ppermute | solution.py:144
